TPU v7x, 256 devices: a whole 4x4x8 slice. The times are simulated.
256 devices in a mesh: row: 16 (over z_hi, y, core), col: 16 (over z_lo, x).
Axes of the slice: x: 4, y: 4, z: 8 (z_hi: 2, z_lo: 4; z = z_hi * 4 + z_lo), core: 2. Of those that a mesh axis runs over, the one named last changes fastest.
Arguments:
- vectors: float32 [4, 16, 16, 16, 128], P(None, 'col', 'row'), may hold values from -6 to 6
- tiles: float32 [16, 16, 96, 128, 128], P('row', 'col')
- tile_rows: int32 [16, 16, 96], P('row', 'col'), may hold values from 0 to 63, as said below
- tile_cols: int32 [16, 16, 96], P('row', 'col'), may hold values from 0 to 63
- counts: int32 [16, 16], P('row', 'col'), may hold values from 1 to 96
Outputs:
- product: float32 [4, 16, 16, 16, 128], P(None, 'col', 'row')
Inputs may be any that keep to these rules, and one draw needn't show every extreme that they name: `tile_rows`: live slots have i_s <= j_s, and no pair (i_s, j_s) is named by two live slots of the whole array.
All inputs are finite; a program needn't handle non-finite values.
Results may differ from a plain program's by a relative error of at most 0.0003.
Values sent between devices are 32-bit elements; how exact they have to be, the bound alone decides.
No kernel may reach another device: no remote copies, remote signals or barrier semaphores. Data moves between devices by JAX's collectives and lax.ppermute only.
A program may use at most 64 MiB of HBM per device.

v0:
```python
import jax
import jax.numpy as jnp
from jax import lax
from jax.sharding import PartitionSpec as P


def shards(vectors, tiles, tile_rows, tile_cols, counts):
    row_count = lax.axis_size("row")
    col_count = lax.axis_size("col")
    row_index = lax.axis_index("row")
    col_index = lax.axis_index("col")
    blocks = vectors.shape[0]
    vec_count = vectors.shape[3]
    tile_edge = vectors.shape[4]
    slot_count = tiles.shape[2]
    local_rows = blocks * col_count
    local_cols = blocks * row_count
    column_side = lax.all_gather(vectors, "row", axis=2, tiled=True).reshape(
        local_cols, vec_count, tile_edge
    )
    row_side = lax.all_gather(vectors, "col", axis=1, tiled=True).reshape(
        local_rows, vec_count, tile_edge
    )
    block_tiles = tiles.reshape(slot_count, tile_edge, tile_edge)
    rows_local = tile_rows.reshape(slot_count)
    cols_local = tile_cols.reshape(slot_count)
    live_count = counts.reshape(())
    slot_ids = jnp.arange(slot_count, dtype=jnp.int32)
    live_mask = slot_ids < live_count
    global_row = rows_local * row_count + row_index
    global_col = (
        cols_local // row_count * col_count + col_index
    ) * row_count + cols_local % row_count
    mirror = live_mask & (global_row < global_col)
    picked_cols = jnp.take(column_side, cols_local, axis=0)
    picked_rows = jnp.take(row_side, rows_local, axis=0)
    forward = jnp.einsum(
        "skm,svm->svk",
        block_tiles,
        picked_cols,
        precision=lax.Precision.HIGHEST,
        preferred_element_type=jnp.float32,
    )
    backward = jnp.einsum(
        "skm,svk->svm",
        block_tiles,
        picked_rows,
        precision=lax.Precision.HIGHEST,
        preferred_element_type=jnp.float32,
    )
    forward = jnp.where(live_mask[:, None, None], forward, 0.0).reshape(
        slot_count, vec_count * tile_edge
    )
    backward = jnp.where(mirror[:, None, None], backward, 0.0).reshape(
        slot_count, vec_count * tile_edge
    )
    row_key = rows_local % col_count * blocks + rows_local // col_count
    col_key = cols_local % row_count * blocks + cols_local // row_count
    targets = jnp.arange(lax.axis_size("col") * blocks, dtype=jnp.int32)
    onehot = (targets[:, None] == row_key[None, :]).astype(jnp.float32)
    row_part = lax.psum_scatter(
        jnp.dot(
            onehot, forward, precision=lax.Precision.HIGHEST, preferred_element_type=jnp.float32
        ),
        "col",
        scatter_dimension=0,
        tiled=True,
    )
    targets = jnp.arange(lax.axis_size("row") * blocks, dtype=jnp.int32)
    onehot = (targets[:, None] == col_key[None, :]).astype(jnp.float32)
    col_part = lax.psum_scatter(
        jnp.dot(
            onehot, backward, precision=lax.Precision.HIGHEST, preferred_element_type=jnp.float32
        ),
        "row",
        scatter_dimension=0,
        tiled=True,
    )
    return (row_part + col_part).reshape(blocks, 1, 1, vec_count, tile_edge)


def solution(mesh):
    in_specs = (
        P(None, "col", "row", None, None),
        P("row", "col", None, None, None),
        P("row", "col", None),
        P("row", "col", None),
        P("row", "col"),
    )
    out_specs = P(None, "col", "row", None, None)
    return jax.shard_map(shards, mesh=mesh, in_specs=in_specs, out_specs=out_specs, check_vma=False)
```

profile of v0, /device:TPU:8, one launch (start us, length us, event | category | flops | bytes accessed | tf_op | source)
XLA Modules:
  0.0 414.9 jit_solution(13500323537019869990)
XLA Ops:
  6.5 0.0 copy-start
  6.5 0.0 all-reduce.7.cloned.1.call-start
  6.5 0.7 multiply_add_fusion
  7.9 0.7 fusion.26
  8.5 46.7 %all_gather.7 = f32[4,16,1,16,128]{4,3,2,1,0:T(8,128)S(1)} all-gather(f32[4,1,1,16,128]{4,3,2,1,0:T(8,128)} %param.7), channel_id=1, replica_groups=mesh['row'=16,'col'=16] {'col'}, dimensions={1}, use_global_device_ids=true | all-gather | bytes 557056 | tf_op jit(solution)/shard_map/all_gather | solution.py:21
  55.3 0.7 gather_fusion.1
  56.0 0.7 compare_and_fusion.1
  56.7 7.5 %fusion.7 = f32[96,16,128]{2,1,0:T(8,128)S(1)} fusion(f32[1,1,96,128,128]{4,3,2,1,0:T(8,128)} %param.8, f32[96,16,128]{2,1,0:T(8,128)S(1)} %gather_fusion.1, pred[96]{0:T(512)(128)(4,1)S(1)} %get-tuple-element.12, pred[96]{0:T(512)(128)(4,1)S(1)} %get-tuple-element.11), kind=kOutput, calls=%fused_computation.7 | convolution fusion | flops 302383104 | bytes 7864512 | tf_op jit(solution)/shard_map/skm,svk->svm/dot_general | solution.py:44
  64.2 1.5 fusion.10
  65.7 0.0 copy-start.2
  65.7 0.0 copy-start.1
  65.7 0.0 all-reduce.7.cloned.1.call-update
  65.7 0.0 all-reduce.5.cloned.1.call-start
  65.8 0.0 copy-done
  65.8 26.1 %all_gather.6 = f32[4,1,16,16,128]{4,3,2,1,0:T(8,128)S(1)} all-gather(f32[4,1,1,16,128]{4,3,2,1,0:T(8,128)S(1)} %copy-done), channel_id=1, replica_groups=mesh['row'=16,'col'=16] {'row'}, dimensions={2}, use_global_device_ids=true | all-gather | bytes 557056 | tf_op jit(solution)/shard_map/all_gather | solution.py:18
  91.8 0.7 gather_fusion
  92.5 12.0 %fusion.4 = f32[96,16,128]{2,1,0:T(8,128)S(1)} fusion(f32[1,1,96,128,128]{4,3,2,1,0:T(8,128)} %param.8, f32[96,16,128]{2,1,0:T(8,128)S(1)} %gather_fusion, pred[96]{0:T(512)(128)(4,1)S(1)} %get-tuple-element.10, pred[96]{0:T(512)(128)(4,1)S(1)} %iota_compare_fusion.4), kind=kOutput, calls=%fused_computation.6 | convolution fusion | flops 302383104 | bytes 7864512 | tf_op jit(solution)/shard_map/skm,svm->svk/dot_general | solution.py:37
  104.5 1.5 fusion.13
  106.0 0.0 all-reduce.5.cloned.1.call-update
  106.0 0.0 copy-done.2
  106.0 0.7 dynamic-slice
  106.7 0.0 copy-done.1
  106.7 0.6 dynamic-slice.2
  108.6 125.5 %all-reduce.7.cloned.1.call-done = f32[64,2048]{1,0:T(8,128)} async-done(((f32[64,2048]{1,0:T(8,128)}), f32[64,2048]{1,0:T(8,128)}) %all-reduce.7.cloned.1.call-update) | async-done | bytes 524304
  234.1 172.5 %all-reduce.5.cloned.1.call-done = f32[64,2048]{1,0:T(8,128)} async-done(((f32[64,2048]{1,0:T(8,128)}), f32[64,2048]{1,0:T(8,128)}) %all-reduce.5.cloned.1.call-update) | async-done | bytes 524304
  406.5 0.9 fusion.22
  407.4 0.6 copy.20
  (3 shorter events, 0.0 us)
Async XLA Ops:
  6.5 59.2 %copy-start = (f32[4,1,1,16,128]{4,3,2,1,0:T(8,128)S(1)}, f32[4,1,1,16,128]{4,3,2,1,0:T(8,128)}, u32[]{:S(2)}) copy-start(f32[4,1,1,16,128]{4,3,2,1,0:T(8,128)} %param.7) | copy-start | bytes 98308
  6.5 227.5 %all-reduce.7.cloned.1.call-start = ((), (), s32[]{:S(2)}) async-start(), calls=%async_computation.1 | async-start | bytes 1048576
  65.7 40.3 %copy-start.2 = (u32[256]{0:T(256)S(1)}, u32[256]{0:T(256)}, u32[]{:S(2)}) copy-start(u32[256]{0:T(256)} %constant.75) | copy-start | bytes 3076
  65.7 41.0 %copy-start.1 = (u32[256]{0:T(256)S(1)}, u32[256]{0:T(256)}, u32[]{:S(2)}) copy-start(u32[256]{0:T(256)} %constant.79) | copy-start | bytes 3076
  65.7 340.8 %all-reduce.5.cloned.1.call-start = ((), (), s32[]{:S(2)}) async-start(), calls=%async_computation | async-start | bytes 1048576
Sparse Core Ops, SparseCore 0:
  65.8 168.1 all-reduce.6
  236.8 169.6 all-reduce.4
where the time goes:
time: 415 us
  waiting for transfers between devices  298 us (72%)
  blocking collectives  72.8 us (18%)
  matrix products  22.5 us (5%)
  between operations  15.5 us (4%)
    unnamed x4, waiting for transfers between devices  298 us
    all_gather x1, blocking collectives, shards(): lax.all_gather(vectors, 'col', axis=1, tiled=True)  46.7 us
    all_gather x1, blocking collectives, shards(): lax.all_gather(vectors, 'row', axis=2, tiled=True)  26.1 us
    dot_general x1, matrix products, shards(): jnp.einsum('skm,svm->svk', block_tiles, picked_cols, precision=lax.Precis...  12 us
  transfers between devices with their start and end apart: 2, of which 2 were waited for; matrix products, arithmetic and copies ran while one was open for 4% of the time, Pallas kernels for 0%

commit v1 on v0

--- a/solution.py
+++ b/solution.py
@@ -2,6 +2,10 @@
 import jax.numpy as jnp
 from jax import lax
 from jax.sharding import PartitionSpec as P
+
+
+def exchange(parts, axis):
+    return lax.all_to_all(parts, axis, 0, 0, tiled=True)
 
 
 def shards(vectors, tiles, tile_rows, tile_cols, counts):
@@ -15,10 +19,11 @@
     slot_count = tiles.shape[2]
     local_rows = blocks * col_count
     local_cols = blocks * row_count
-    column_side = lax.all_gather(vectors, "row", axis=2, tiled=True).reshape(
+    own = vectors.reshape(1, blocks, vec_count, tile_edge)
+    column_side = exchange(jnp.tile(own, (row_count, 1, 1, 1)), "row").reshape(
         local_cols, vec_count, tile_edge
     )
-    row_side = lax.all_gather(vectors, "col", axis=1, tiled=True).reshape(
+    row_side = exchange(jnp.tile(own, (col_count, 1, 1, 1)), "col").reshape(
         local_rows, vec_count, tile_edge
     )
     block_tiles = tiles.reshape(slot_count, tile_edge, tile_edge)
@@ -32,8 +37,10 @@
         cols_local // row_count * col_count + col_index
     ) * row_count + cols_local % row_count
     mirror = live_mask & (global_row < global_col)
-    picked_cols = jnp.take(column_side, cols_local, axis=0)
-    picked_rows = jnp.take(row_side, rows_local, axis=0)
+    row_key = rows_local % col_count * blocks + rows_local // col_count
+    col_key = cols_local % row_count * blocks + cols_local // row_count
+    picked_cols = jnp.take(column_side, col_key, axis=0)
+    picked_rows = jnp.take(row_side, row_key, axis=0)
     forward = jnp.einsum(
         "skm,svm->svk",
         block_tiles,
@@ -54,28 +61,22 @@
     backward = jnp.where(mirror[:, None, None], backward, 0.0).reshape(
         slot_count, vec_count * tile_edge
     )
-    row_key = rows_local % col_count * blocks + rows_local // col_count
-    col_key = cols_local % row_count * blocks + cols_local // row_count
     targets = jnp.arange(lax.axis_size("col") * blocks, dtype=jnp.int32)
     onehot = (targets[:, None] == row_key[None, :]).astype(jnp.float32)
-    row_part = lax.psum_scatter(
+    row_part = exchange(
         jnp.dot(
             onehot, forward, precision=lax.Precision.HIGHEST, preferred_element_type=jnp.float32
-        ),
+        ).reshape(col_count, blocks, vec_count, tile_edge),
         "col",
-        scatter_dimension=0,
-        tiled=True,
-    )
+    ).sum(0)
     targets = jnp.arange(lax.axis_size("row") * blocks, dtype=jnp.int32)
     onehot = (targets[:, None] == col_key[None, :]).astype(jnp.float32)
-    col_part = lax.psum_scatter(
+    col_part = exchange(
         jnp.dot(
             onehot, backward, precision=lax.Precision.HIGHEST, preferred_element_type=jnp.float32
-        ),
+        ).reshape(row_count, blocks, vec_count, tile_edge),
         "row",
-        scatter_dimension=0,
-        tiled=True,
-    )
+    ).sum(0)
     return (row_part + col_part).reshape(blocks, 1, 1, vec_count, tile_edge)
 
 

time: 415 us -> 99.3 us (0.24)
  the two profiles are of different devices: /device:TPU:8 before, /device:TPU:32 now
where the time goes in v1:
time: 99.3 us; the launch traced here: 98.7 us
  waiting for transfers between devices  42.5 us (43%)
  starting transfers between devices  27.6 us (28%)
  matrix products  20.8 us (21%)
  local copies, waits for them, and re-layouts  4.91 us (5%)
  other arithmetic  2.09 us (2%)
    all_to_all x4, waiting for transfers between devices, exchange(): return lax.all_to_all(parts, axis, 0, 0, tiled=True)  42.5 us
    all_to_all x4, starting transfers between devices, exchange(): return lax.all_to_all(parts, axis, 0, 0, tiled=True)  27.6 us
    dot_general x1, matrix products, shards(): jnp.einsum('skm,svm->svk', block_tiles, picked_cols, precision=lax.Precis...  11.9 us
    dot_general x1, matrix products, shards(): jnp.einsum('skm,svk->svm', block_tiles, picked_rows, precision=lax.Precis...  7.53 us
  transfers between devices with their start and end apart: 4, of which 3 were waited for; matrix products, arithmetic and copies ran while one was open for 26% of the time, Pallas kernels for 0%

profile of v1, /device:TPU:32, one launch (start us, length us, event | category | flops | bytes accessed | tf_op | source)
XLA Modules:
  0.0 98.7 jit_solution(4091517338827267479)
XLA Ops:
  0.0 1.6 %tile.5 = f32[16,4,16,128]{3,2,1,0:T(8,128)} broadcast(f32[4,16,128]{2,1,0:T(8,128)} %bitcast.101), dimensions={1,2,3} | broadcast | bytes 557056 | tf_op jit(solution)/shard_map/tile | solution.py:23
  1.6 10.3 %all-to-all-start = ((f32[16,4,16,128]{3,2,1,0:T(8,128)}), f32[16,4,16,128]{3,2,1,0:T(8,128)S(1)}, u32[]{:S(2)}, u32[]{:S(2)}) async-start(f32[16,4,16,128]{3,2,1,0:T(8,128)} %tile.5), calls=%async_computation | async-start | bytes 1048576 | tf_op jit(solution)/shard_map/all_to_all | solution.py:8
  12.6 0.7 compare_and_fusion
  13.3 0.7 compare_and_fusion.1
  14.0 18.3 %all-to-all-done = f32[16,4,16,128]{3,2,1,0:T(8,128)S(1)} async-done(((f32[16,4,16,128]{3,2,1,0:T(8,128)}), f32[16,4,16,128]{3,2,1,0:T(8,128)S(1)}, u32[]{:S(2)}, u32[]{:S(2)}) %all-to-all-start) | async-done | bytes 524320 | tf_op jit(solution)/shard_map/all_to_all | solution.py:8
  32.3 6.2 %all-to-all-start.2 = ((f32[16,4,16,128]{3,2,1,0:T(8,128)}), f32[16,4,16,128]{3,2,1,0:T(8,128)S(1)}, u32[]{:S(2)}, u32[]{:S(2)}) async-start(f32[16,4,16,128]{3,2,1,0:T(8,128)} %tile.5), calls=%async_computation.2 | async-start | bytes 1048576 | tf_op jit(solution)/shard_map/all_to_all | solution.py:8
  38.5 0.7 gather_fusion
  39.2 11.9 %fusion.4 = f32[96,16,128]{2,1,0:T(8,128)S(1)} fusion(f32[1,1,96,128,128]{4,3,2,1,0:T(8,128)} %param.8, f32[96,16,128]{2,1,0:T(8,128)S(1)} %gather_fusion, pred[96]{0:T(512)(128)(4,1)S(1)} %get-tuple-element.10, pred[96]{0:T(512)(128)(4,1)S(1)} %get-tuple-element.14), kind=kOutput, calls=%fused_computation.6 | convolution fusion | flops 302383104 | bytes 7864512 | tf_op jit(solution)/shard_map/skm,svm->svk/dot_general | solution.py:44
  51.2 0.7 fusion.12
  51.9 1.0 copy.9
  52.9 0.0 all-to-all-done.2
  52.9 7.5 %all-to-all-start.1 = ((f32[16,4,16,128]{3,2,1,0:T(8,128)}), f32[16,4,16,128]{3,2,1,0:T(8,128)S(1)}, u32[]{:S(2)}, u32[]{:S(2)}) async-start(f32[16,4,16,128]{3,2,1,0:T(8,128)} %copy.9), calls=%async_computation.1 | async-start | bytes 1048576 | tf_op jit(solution)/shard_map/all_to_all | solution.py:8
  60.4 0.7 gather_fusion.1
  61.1 7.5 %fusion.7 = f32[96,16,128]{2,1,0:T(8,128)S(1)} fusion(f32[1,1,96,128,128]{4,3,2,1,0:T(8,128)} %param.8, f32[96,16,128]{2,1,0:T(8,128)S(1)} %gather_fusion.1, pred[96]{0:T(512)(128)(4,1)S(1)} %get-tuple-element.8, pred[96]{0:T(512)(128)(4,1)S(1)} %get-tuple-element.12), kind=kOutput, calls=%fused_computation.7 | convolution fusion | flops 302383104 | bytes 7864512 | tf_op jit(solution)/shard_map/skm,svk->svm/dot_general | solution.py:51
  68.6 0.7 fusion.10
  69.3 1.0 copy.11
  70.3 3.9 %all-to-all-done.1 = f32[16,4,16,128]{3,2,1,0:T(8,128)S(1)} async-done(((f32[16,4,16,128]{3,2,1,0:T(8,128)}), f32[16,4,16,128]{3,2,1,0:T(8,128)S(1)}, u32[]{:S(2)}, u32[]{:S(2)}) %all-to-all-start.1) | async-done | bytes 524320 | tf_op jit(solution)/shard_map/all_to_all | solution.py:8
  74.2 3.6 %all-to-all-start.3 = ((f32[16,4,16,128]{3,2,1,0:T(8,128)}), f32[16,4,16,128]{3,2,1,0:T(8,128)S(1)}, u32[]{:S(2)}, u32[]{:S(2)}) async-start(f32[16,4,16,128]{3,2,1,0:T(8,128)} %copy.11), calls=%async_computation.3 | async-start | bytes 1048576 | tf_op jit(solution)/shard_map/all_to_all | solution.py:8
  77.8 20.3 %all-to-all-done.3 = f32[16,4,16,128]{3,2,1,0:T(8,128)S(1)} async-done(((f32[16,4,16,128]{3,2,1,0:T(8,128)}), f32[16,4,16,128]{3,2,1,0:T(8,128)S(1)}, u32[]{:S(2)}, u32[]{:S(2)}) %all-to-all-start.3) | async-done | bytes 524320 | tf_op jit(solution)/shard_map/all_to_all | solution.py:8
  98.1 0.6 add_bitcast_fusion
  (7 shorter events, 0.1 us)
Async XLA Ops:
  1.6 30.7 %all-to-all-start = ((f32[16,4,16,128]{3,2,1,0:T(8,128)}), f32[16,4,16,128]{3,2,1,0:T(8,128)S(1)}, u32[]{:S(2)}, u32[]{:S(2)}) async-start(f32[16,4,16,128]{3,2,1,0:T(8,128)} %tile.5), calls=%async_computation | async-start | bytes 1048576 | tf_op jit(solution)/shard_map/all_to_all | solution.py:8
  32.3 20.6 %all-to-all-start.2 = ((f32[16,4,16,128]{3,2,1,0:T(8,128)}), f32[16,4,16,128]{3,2,1,0:T(8,128)S(1)}, u32[]{:S(2)}, u32[]{:S(2)}) async-start(f32[16,4,16,128]{3,2,1,0:T(8,128)} %tile.5), calls=%async_computation.2 | async-start | bytes 1048576 | tf_op jit(solution)/shard_map/all_to_all | solution.py:8
  52.9 21.3 %all-to-all-start.1 = ((f32[16,4,16,128]{3,2,1,0:T(8,128)}), f32[16,4,16,128]{3,2,1,0:T(8,128)S(1)}, u32[]{:S(2)}, u32[]{:S(2)}) async-start(f32[16,4,16,128]{3,2,1,0:T(8,128)} %copy.9), calls=%async_computation.1 | async-start | bytes 1048576 | tf_op jit(solution)/shard_map/all_to_all | solution.py:8
  74.2 23.9 %all-to-all-start.3 = ((f32[16,4,16,128]{3,2,1,0:T(8,128)}), f32[16,4,16,128]{3,2,1,0:T(8,128)S(1)}, u32[]{:S(2)}, u32[]{:S(2)}) async-start(f32[16,4,16,128]{3,2,1,0:T(8,128)} %copy.11), calls=%async_computation.3 | async-start | bytes 1048576 | tf_op jit(solution)/shard_map/all_to_all | solution.py:8

commit v2 on v1

v2 whole, which is shorter than its diff:
```python
import functools
import jax
import jax.numpy as jnp
from jax import lax
from jax.experimental import pallas as pl
from jax.experimental.pallas import tpu as pltpu
from jax.sharding import PartitionSpec as P

AXIS = 16
GROUP = 4
CHUNK = 8
BF16 = jnp.bfloat16
F32 = jnp.float32


def send(value, axis, target):
    return lax.ppermute(value, axis, [(i, target(i)) for i in range(AXIS)])


def turn_y(step):
    return lambda i: i // 8 * 8 + (i // 2 + step) % 4 * 2 + i % 2


def turn_x(step):
    return lambda i: i // 4 * 4 + (i + step) % 4


def turn_z(step):
    return lambda i: (i + 4 * step) % AXIS


def other_z(i):
    return i ^ 8


def other_core(i):
    return i ^ 1


def multiply_kernel(transposed, part_count, out_count, *refs):
    source, target, live = refs[:3]
    parts = refs[3 : 3 + part_count]
    tiles = refs[3 + part_count]
    outs = refs[4 + part_count : 4 + part_count + out_count]
    split, total, held, arrived = refs[4 + part_count + out_count :]
    chunks = held.shape[0] // CHUNK
    vecs = split.shape[1] // 2
    edge = split.shape[2] // 2

    def fetch(chunk):
        span = pl.ds(chunk * CHUNK, CHUNK)
        return pltpu.make_async_copy(tiles.at[span], held.at[span], arrived.at[chunk])

    for chunk in range(chunks):
        fetch(chunk).start()
    place = 0
    for part in parts:
        values = part[...]
        high = values.astype(BF16)
        low = (values - high.astype(F32)).astype(BF16)
        span = slice(place, place + part.shape[0])
        split[span, :vecs, :edge] = high
        split[span, :vecs, edge:] = high
        split[span, vecs:, :edge] = low
        split[span, vecs:, edge:] = low
        place += part.shape[0]
    total[...] = jnp.zeros_like(total)

    def one_slot(slot):
        tile = held[slot]
        high = tile.astype(BF16)
        low = (tile - high.astype(F32)).astype(BF16)
        both = jnp.concatenate([high, low], axis=0 if transposed else 1)
        product = lax.dot_general(
            split[source[slot]],
            both,
            (((1,), (0 if transposed else 1,)), ((), ())),
            preferred_element_type=F32,
        )
        total[target[slot]] += product[:vecs] + product[vecs:]

    def one_chunk(chunk, carry):
        fetch(chunk).wait()

        @pl.when(chunk * CHUNK < live[0])
        def _():
            for step in range(CHUNK):
                one_slot(chunk * CHUNK + step)

        return carry

    lax.fori_loop(0, chunks, one_chunk, 0)
    place = 0
    for out in outs:
        out[...] = total[place : place + out.shape[0]]
        place += out.shape[0]


def multiply(transposed, source, target, live, parts, tiles, out_count):
    slots, edge = tiles.shape[0], tiles.shape[1]
    vecs = parts[0].shape[1]
    places = sum(part.shape[0] for part in parts)
    scalars = [pl.BlockSpec(memory_space=pltpu.SMEM)] * 3
    vector = pl.BlockSpec(memory_space=pltpu.VMEM)
    return pl.pallas_call(
        functools.partial(multiply_kernel, transposed, len(parts), out_count),
        out_shape=[jax.ShapeDtypeStruct((places // out_count, vecs, edge), F32)] * out_count,
        in_specs=scalars + [vector] * len(parts) + [pl.BlockSpec(memory_space=pl.ANY)],
        out_specs=[vector] * out_count,
        scratch_shapes=[
            pltpu.VMEM((places, 2 * vecs, 2 * edge), BF16),
            pltpu.VMEM((places + 8, vecs, edge), F32),
            pltpu.VMEM((slots, edge, edge), F32),
            pltpu.SemaphoreType.DMA((slots // CHUNK,)),
        ],
        compiler_params=pltpu.CompilerParams(vmem_limit_bytes=20 * 1024 * 1024),
        cost_estimate=pl.CostEstimate(
            flops=8 * slots * vecs * edge * edge, bytes_accessed=4 * slots * edge * edge, transcendentals=0
        ),
        name="backward" if transposed else "forward",
    )(source, target, live, *parts, tiles)


def shards(vectors, tiles, tile_rows, tile_cols, counts):
    blocks = vectors.shape[0]
    vecs, edge = vectors.shape[3], vectors.shape[4]
    slots = tiles.shape[2]
    row, col = lax.axis_index("row"), lax.axis_index("col")
    tiles = tiles.reshape(slots, edge, edge)
    rows, cols = tile_rows.reshape(slots), tile_cols.reshape(slots)
    live = counts.reshape(1)
    row_block, row_col = rows // AXIS, rows % AXIS
    col_block, col_row = cols // AXIS, cols % AXIS
    is_live = jnp.arange(slots, dtype=jnp.int32) < live
    mirror = is_live & (rows * AXIS + row < (col_block * AXIS + col) * AXIS + col_row)

    def row_place(step_y):
        core, z = (col_row ^ row) & 1, (col_row ^ row) >> 3
        return ((core * GROUP + (step_y & 3)) * 2 + z) * blocks + col_block

    def col_place(step_x, step_z):
        return ((step_x & 3) * GROUP + (step_z & 3)) * blocks + row_block

    nowhere = blocks * AXIS
    step_y = (col_row >> 1) - (row >> 1)
    step_x, step_z = row_col - col, (row_col >> 2) - (col >> 2)
    forward_source = row_place(-step_y)
    forward_target = jnp.where(is_live, col_place(step_x, step_z), nowhere)
    backward_source = col_place(-step_x, -step_z)
    backward_target = jnp.where(mirror, row_place(step_y), nowhere)

    own = vectors.reshape(blocks, vecs, edge)
    with jax.named_scope("gather_z"):
        across = send(own, "row", other_z)
        along = [send(own, "col", turn_z(step)) for step in (1, 2, 3)]
    with jax.named_scope("gather_y"):
        pair = jnp.concatenate([own, across])
        sides = [pair] + [send(pair, "row", turn_y(step)) for step in (1, 2, 3)]
    with jax.named_scope("gather_core"):
        sides = sides + [send(side, "row", other_core) for side in sides]
    with jax.named_scope("gather_x"):
        line = jnp.concatenate([own] + along)
        lines = [line] + [send(line, "col", turn_x(step)) for step in (1, 2, 3)]
    row_parts = multiply(False, forward_source, forward_target, live, sides, tiles, 4)
    col_parts = multiply(True, backward_source, backward_target, live, lines, tiles, 2)
    with jax.named_scope("sum_x"):
        line = row_parts[0]
        for step in (1, 2, 3):
            line = line + send(row_parts[step], "col", turn_x(step))
    with jax.named_scope("sum_core"):
        side = col_parts[0] + send(col_parts[1], "row", other_core)
    with jax.named_scope("sum_y"):
        side = side.reshape(GROUP, 2 * blocks, vecs, edge)
        pair = side[0]
        for step in (1, 2, 3):
            pair = pair + send(side[step], "row", turn_y(step))
    with jax.named_scope("sum_z"):
        line = line.reshape(GROUP, blocks, vecs, edge)
        result = line[0] + pair[:blocks] + send(pair[blocks:], "row", other_z)
        for step in (1, 2, 3):
            result = result + send(line[step], "col", turn_z(step))
    return result.reshape(blocks, 1, 1, vecs, edge)


def solution(mesh):
    in_specs = (
        P(None, "col", "row", None, None),
        P("row", "col", None, None, None),
        P("row", "col", None),
        P("row", "col", None),
        P("row", "col"),
    )
    out_specs = P(None, "col", "row", None, None)
    return jax.shard_map(shards, mesh=mesh, in_specs=in_specs, out_specs=out_specs, check_vma=False)
```

time: 99.3 us -> 64 us (0.64)
  the two profiles are of different devices: /device:TPU:32 before, /device:TPU:8 now
where the time goes in v2:
time: 64 us; the launch traced here: 63.8 us
  starting transfers between devices  42.7 us (67%)
  waiting for transfers between devices  7.41 us (12%)
  Pallas kernels  5.82 us (9%)
  other arithmetic  4.29 us (7%)
  local copies, waits for them, and re-layouts  2.81 us (4%)
  between operations  0.75 us (1%)
    ppermute x25, starting transfers between devices, send(): return lax.ppermute(value, axis, [(i, target(i)) for i in range(AXIS)])  42.7 us
    ppermute x25, waiting for transfers between devices, send(): return lax.ppermute(value, axis, [(i, target(i)) for i in range(AXIS)])  7.41 us
    pallas_call x2, Pallas kernels, multiply(): pl.pallas_call(functools.partial(multiply_kernel, transposed, len(parts),...  5.82 us
    unnamed x4, local copies, waits for them, and re-layouts  2.79 us
  transfers between devices with their start and end apart: 25, of which 6 were waited for; matrix products, arithmetic and copies ran while one was open for 6% of the time, Pallas kernels for 9%

profile of v2, /device:TPU:8, one launch (start us, length us, event | category | flops | bytes accessed | tf_op | source)
XLA Modules:
  0.0 63.8 jit_solution(8859901128185996585)
XLA Ops:
  0.0 1.9 %collective-permute-start.11 = (f32[4,16,128]{2,1,0:T(8,128)}, f32[4,16,128]{2,1,0:T(8,128)S(1)}, u32[]{:S(2)}, u32[]{:S(2)}) collective-permute-start(f32[4,16,128]{2,1,0:T(8,128)} %bitcast.54), channel_id=1, source_target_pairs={{0,4},{1,5},{2,6},{3,7},{4,8},{5,9},{6,10},{7,11},{8,12},{9,13},{1... | collective-permute-start | bytes 98312 | tf_op jit(solution)/shard_map/gather_z/ppermute | solution.py:17
  1.9 3.3 %collective-permute-start.12 = (f32[4,16,128]{2,1,0:T(8,128)}, f32[4,16,128]{2,1,0:T(8,128)S(1)}, u32[]{:S(2)}, u32[]{:S(2)}) collective-permute-start(f32[4,16,128]{2,1,0:T(8,128)} %bitcast.55), channel_id=1, source_target_pairs={{0,8},{1,9},{2,10},{3,11},{4,12},{5,13},{6,14},{7,15},{8,0},{9,1},... | collective-permute-start | bytes 98312 | tf_op jit(solution)/shard_map/gather_z/ppermute | solution.py:17
  5.2 1.0 %collective-permute-start.13 = (f32[4,16,128]{2,1,0:T(8,128)}, f32[4,16,128]{2,1,0:T(8,128)S(1)}, u32[]{:S(2)}, u32[]{:S(2)}) collective-permute-start(f32[4,16,128]{2,1,0:T(8,128)} %bitcast.56), channel_id=1, source_target_pairs={{0,12},{1,13},{2,14},{3,15},{4,0},{5,1},{6,2},{7,3},{8,4},{9,5},{1... | collective-permute-start | bytes 98312 | tf_op jit(solution)/shard_map/gather_z/ppermute | solution.py:17
  6.2 5.4 %collective-permute-start = (f32[4,16,128]{2,1,0:T(8,128)}, f32[4,16,128]{2,1,0:T(8,128)S(1)}, u32[]{:S(2)}, u32[]{:S(2)}) collective-permute-start(f32[4,16,128]{2,1,0:T(8,128)} %bitcast.57), channel_id=1, source_target_pairs={{0,128},{16,144},{32,160},{48,176},{64,192},{80,208},{96,224},{112... | collective-permute-start | bytes 98312 | tf_op jit(solution)/shard_map/gather_z/ppermute | solution.py:17
  11.6 0.7 %multiply_add_fusion = (s32[96]{0:T(128)S(1)}, s32[96]{0:T(128)S(1)}) fusion(s32[]{:T(128)S(6)} %shift_right_arithmetic.20, s32[]{:T(128)S(6)} %axis_index.25, s32[1,1,96]{2,1,0:T(1,128)} %param.7), kind=kLoop, calls=%fused_computation.28 | loop fusion | flops 2880 | bytes 1160 | tf_op jit(solution)/shard_map/add | solution.py:142
  12.9 1.3 %collective-permute-done = f32[4,16,128]{2,1,0:T(8,128)S(1)} collective-permute-done((f32[4,16,128]{2,1,0:T(8,128)}, f32[4,16,128]{2,1,0:T(8,128)S(1)}, u32[]{:S(2)}, u32[]{:S(2)}) %collective-permute-start) | collective-permute-done | bytes 32800 | tf_op jit(solution)/shard_map/gather_z/ppermute | solution.py:17
  14.2 0.8 %pad_maximum_fusion.1.refs_3_ = f32[8,16,128]{2,1,0:T(8,128)S(1)} fusion(f32[4,16,128]{2,1,0:T(8,128)S(1)} %collective-permute-done, f32[4,16,128]{2,1,0:T(8,128)} %bitcast.58), kind=kLoop, calls=%fused_computation.5 | loop fusion | flops 16384 | bytes 131072 | tf_op jit(solution)/shard_map/gather_y/concatenate | solution.py:157
  15.0 1.6 %collective-permute-start.1 = (f32[8,16,128]{2,1,0:T(8,128)S(1)}, f32[8,16,128]{2,1,0:T(8,128)S(1)}, u32[]{:S(2)}, u32[]{:S(2)}) collective-permute-start(f32[8,16,128]{2,1,0:T(8,128)S(1)} %pad_maximum_fusion.1.refs_3_), channel_id=1, source_target_pairs={{0,32},{16,48},{32,64},{48,80},{64,96},{80,112},{96,0},{112,16},{1... | collective-permute-start | bytes 196616 | tf_op jit(solution)/shard_map/gather_y/ppermute | solution.py:17
  16.6 0.7 %and_select_fusion = (s32[96]{0:T(128)S(1)}, s32[96]{0:T(128)S(1)}, s32[96]{0:T(128)S(1)}) fusion(s32[1,1,96]{2,1,0:T(1,128)} %param.7, s32[]{:T(128)S(6)} %axis_index.25, s32[]{:T(128)} %bitcast.49, s32[]{:T(128)S(6)} %shift_right_arithmetic.17, s32[]{:T(128)S(6)} %axis_index.23, s32[1,1,96]{2,1,0:T(1,128)} %param.8, s32[96]{0:T(128)S(1)} %get-tuple-element.20, ...), kind=kLoop, calls=%fused_computation.12 | loop fusion | flops 5952 | bytes 2324 | tf_op jit(solution)/shard_map/jit(_where)/select_n | solution.py:150
  17.3 1.0 %collective-permute-start.2 = (f32[8,16,128]{2,1,0:T(8,128)S(1)}, f32[8,16,128]{2,1,0:T(8,128)S(1)}, u32[]{:S(2)}, u32[]{:S(2)}) collective-permute-start(f32[8,16,128]{2,1,0:T(8,128)S(1)} %pad_maximum_fusion.1.refs_3_), channel_id=1, source_target_pairs={{0,64},{16,80},{32,96},{48,112},{64,0},{80,16},{96,32},{112,48},{1... | collective-permute-start | bytes 196616 | tf_op jit(solution)/shard_map/gather_y/ppermute | solution.py:17
  18.3 2.4 %collective-permute-start.3 = (f32[8,16,128]{2,1,0:T(8,128)S(1)}, f32[8,16,128]{2,1,0:T(8,128)S(1)}, u32[]{:S(2)}, u32[]{:S(2)}) collective-permute-start(f32[8,16,128]{2,1,0:T(8,128)S(1)} %pad_maximum_fusion.1.refs_3_), channel_id=1, source_target_pairs={{0,96},{16,112},{32,0},{48,16},{64,32},{80,48},{96,64},{112,80},{1... | collective-permute-start | bytes 196616 | tf_op jit(solution)/shard_map/gather_y/ppermute | solution.py:17
  20.7 0.5 collective-permute-start.5
  21.2 0.8 %pad_maximum_fusion.refs_3_ = f32[16,16,128]{2,1,0:T(8,128)S(1)} fusion(f32[4,16,128]{2,1,0:T(8,128)S(1)} %collective-permute-done.13, f32[4,16,128]{2,1,0:T(8,128)S(1)} %collective-permute-done.12, f32[4,16,128]{2,1,0:T(8,128)S(1)} %collective-permute-done.11, f32[4,16,128]{2,1,0:T(8,128)} %bitcast.59), kind=kLoop, calls=%fused_computation | loop fusion | flops 98304 | bytes 262144 | tf_op jit(solution)/shard_map/gather_x/concatenate | solution.py:162
  22.0 1.6 %collective-permute-start.14 = (f32[16,16,128]{2,1,0:T(8,128)S(1)}, f32[16,16,128]{2,1,0:T(8,128)S(1)}, u32[]{:S(2)}, u32[]{:S(2)}) collective-permute-start(f32[16,16,128]{2,1,0:T(8,128)S(1)} %pad_maximum_fusion.refs_3_), channel_id=1, source_target_pairs={{0,1},{1,2},{2,3},{3,0},{4,5},{5,6},{6,7},{7,4},{8,9},{9,10},{10,1... | collective-permute-start | bytes 393224 | tf_op jit(solution)/shard_map/gather_x/ppermute | solution.py:17
  23.6 2.7 %collective-permute-start.15 = (f32[16,16,128]{2,1,0:T(8,128)S(1)}, f32[16,16,128]{2,1,0:T(8,128)S(1)}, u32[]{:S(2)}, u32[]{:S(2)}) collective-permute-start(f32[16,16,128]{2,1,0:T(8,128)S(1)} %pad_maximum_fusion.refs_3_), channel_id=1, source_target_pairs={{0,2},{1,3},{2,0},{3,1},{4,6},{5,7},{6,4},{7,5},{8,10},{9,11},{10,... | collective-permute-start | bytes 393224 | tf_op jit(solution)/shard_map/gather_x/ppermute | solution.py:17
  26.3 1.4 %collective-permute-start.16 = (f32[16,16,128]{2,1,0:T(8,128)S(1)}, f32[16,16,128]{2,1,0:T(8,128)S(1)}, u32[]{:S(2)}, u32[]{:S(2)}) collective-permute-start(f32[16,16,128]{2,1,0:T(8,128)S(1)} %pad_maximum_fusion.refs_3_), channel_id=1, source_target_pairs={{0,3},{1,0},{2,1},{3,2},{4,7},{5,4},{6,5},{7,6},{8,11},{9,8},{10,9... | collective-permute-start | bytes 393224 | tf_op jit(solution)/shard_map/gather_x/ppermute | solution.py:17
  28.3 0.7 %multiply_add_fusion.1.refs_0_ = s32[96]{0:T(128)S(1)} fusion(s32[96]{0:T(128)S(1)} %get-tuple-element.18, s32[]{:T(128)S(6)} %shift_right_arithmetic.17, s32[]{:T(128)S(6)} %axis_index.23, s32[1,1,96]{2,1,0:T(1,128)} %param.8), kind=kLoop, calls=%fused_computation.30 | loop fusion | flops 2304 | bytes 1160 | tf_op jit(solution)/shard_map/add | solution.py:139
  29.2 2.8 %copy-done = f32[1,1,96,128,128]{4,3,2,1,0:T(8,128)S(1)} copy-done((f32[1,1,96,128,128]{4,3,2,1,0:T(8,128)S(1)}, f32[1,1,96,128,128]{4,3,2,1,0:T(8,128)}, u32[]{:S(2)}) %copy-start) | copy-done | bytes 6291480
  31.9 3.1 %forward.1 = (f32[16,16,128]{2,1,0:T(8,128)S(1)}, f32[16,16,128]{2,1,0:T(8,128)S(1)}, f32[16,16,128]{2,1,0:T(8,128)S(1)}, f32[16,16,128]{2,1,0:T(8,128)S(1)}) custom-call(s32[96]{0:T(128)S(1)} %multiply_add_fusion.1.refs_0_, s32[96]{0:T(128)S(1)} %get-tuple-element.27.refs_1_, s32[1]{0:T(128)} %bitcast.50.refs_2_, ...), custom_call_target="tpu_custom_call" | custom-call | flops 201326592 | bytes 6291456 | tf_op jit(solution)/shard_map/forward/pallas_call | solution.py:105
  35.1 1.9 %collective-permute-start.10 = (f32[16,16,128]{2,1,0:T(8,128)S(1)}, f32[16,16,128]{2,1,0:T(8,128)S(1)}, u32[]{:S(2)}, u32[]{:S(2)}) collective-permute-start(f32[16,16,128]{2,1,0:T(8,128)S(1)} %get-tuple-element.14), channel_id=1, source_target_pairs={{0,3},{1,0},{2,1},{3,2},{4,7},{5,4},{6,5},{7,6},{8,11},{9,8},{10,9... | collective-permute-start | bytes 393224 | tf_op jit(solution)/shard_map/sum_x/ppermute | solution.py:17
  37.2 1.8 %collective-permute-start.9 = (f32[16,16,128]{2,1,0:T(8,128)S(1)}, f32[16,16,128]{2,1,0:T(8,128)S(1)}, u32[]{:S(2)}, u32[]{:S(2)}) collective-permute-start(f32[16,16,128]{2,1,0:T(8,128)S(1)} %get-tuple-element.13), channel_id=1, source_target_pairs={{0,2},{1,3},{2,0},{3,1},{4,6},{5,7},{6,4},{7,5},{8,10},{9,11},{10,... | collective-permute-start | bytes 393224 | tf_op jit(solution)/shard_map/sum_x/ppermute | solution.py:17
  39.0 2.7 %backward.1 = (f32[32,16,128]{2,1,0:T(8,128)S(1)}, f32[32,16,128]{2,1,0:T(8,128)S(1)}) custom-call(s32[96]{0:T(128)S(1)} %get-tuple-element.19.refs_0_, s32[96]{0:T(128)S(1)} %get-tuple-element.17.refs_1_, s32[1]{0:T(128)} %bitcast.51.refs_2_, f32[16,16,128]{2,1,0:T(8,128)S(1)} %pad_maximum_fusion.refs_3_, ...), custom_call_target="tpu_custom_call" | custom-call | flops 201326592 | bytes 6291456 | tf_op jit(solution)/shard_map/backward/pallas_call | solution.py:105
  41.7 1.3 %collective-permute-start.17 = (f32[32,16,128]{2,1,0:T(8,128)S(1)}, f32[32,16,128]{2,1,0:T(8,128)S(1)}, u32[]{:S(2)}, u32[]{:S(2)}) collective-permute-start(f32[32,16,128]{2,1,0:T(8,128)S(1)} %get-tuple-element.16), channel_id=1, source_target_pairs={{0,16},{16,0},{32,48},{48,32},{64,80},{80,64},{96,112},{112,96},{1... | collective-permute-start | bytes 786440 | tf_op jit(solution)/shard_map/sum_core/ppermute | solution.py:17
  43.4 2.8 %collective-permute-done.9 = f32[16,16,128]{2,1,0:T(8,128)S(1)} collective-permute-done((f32[16,16,128]{2,1,0:T(8,128)S(1)}, f32[16,16,128]{2,1,0:T(8,128)S(1)}, u32[]{:S(2)}, u32[]{:S(2)}) %collective-permute-start.9) | collective-permute-done | bytes 131104 | tf_op jit(solution)/shard_map/sum_x/ppermute | solution.py:17
  46.3 1.1 %collective-permute-start.18 = (f32[8,16,128]{2,1,0:T(8,128)S(1)}, f32[8,16,128]{2,1,0:T(8,128)S(1)}, u32[]{:S(2)}, u32[]{:S(2)}) collective-permute-start(f32[8,16,128]{2,1,0:T(8,128)S(1)} %get-tuple-element.21), channel_id=1, source_target_pairs={{0,32},{16,48},{32,64},{48,80},{64,96},{80,112},{96,0},{112,16},{1... | collective-permute-start | bytes 196616 | tf_op jit(solution)/shard_map/sum_y/ppermute | solution.py:17
  47.4 1.6 %collective-permute-start.19 = (f32[8,16,128]{2,1,0:T(8,128)S(1)}, f32[8,16,128]{2,1,0:T(8,128)S(1)}, u32[]{:S(2)}, u32[]{:S(2)}) collective-permute-start(f32[8,16,128]{2,1,0:T(8,128)S(1)} %get-tuple-element.23), channel_id=1, source_target_pairs={{0,64},{16,80},{32,96},{48,112},{64,0},{80,16},{96,32},{112,48},{1... | collective-permute-start | bytes 196616 | tf_op jit(solution)/shard_map/sum_y/ppermute | solution.py:17
  49.0 1.6 %collective-permute-start.20 = (f32[8,16,128]{2,1,0:T(8,128)S(1)}, f32[8,16,128]{2,1,0:T(8,128)S(1)}, u32[]{:S(2)}, u32[]{:S(2)}) collective-permute-start(f32[8,16,128]{2,1,0:T(8,128)S(1)} %get-tuple-element.22), channel_id=1, source_target_pairs={{0,96},{16,112},{32,0},{48,16},{64,32},{80,48},{96,64},{112,80},{1... | collective-permute-start | bytes 196616 | tf_op jit(solution)/shard_map/sum_y/ppermute | solution.py:17
  50.6 2.1 %collective-permute-start.22 = (f32[4,16,128]{2,1,0:T(8,128)S(1)}, f32[4,16,128]{2,1,0:T(8,128)S(1)}, u32[]{:S(2)}, u32[]{:S(2)}) collective-permute-start(f32[4,16,128]{2,1,0:T(8,128)S(1)} %get-tuple-element.24), channel_id=1, source_target_pairs={{0,4},{1,5},{2,6},{3,7},{4,8},{5,9},{6,10},{7,11},{8,12},{9,13},{1... | collective-permute-start | bytes 98312 | tf_op jit(solution)/shard_map/sum_z/ppermute | solution.py:17
  52.8 2.5 %collective-permute-start.24 = (f32[4,16,128]{2,1,0:T(8,128)S(1)}, f32[4,16,128]{2,1,0:T(8,128)S(1)}, u32[]{:S(2)}, u32[]{:S(2)}) collective-permute-start(f32[4,16,128]{2,1,0:T(8,128)S(1)} %get-tuple-element.25), channel_id=1, source_target_pairs={{0,12},{1,13},{2,14},{3,15},{4,0},{5,1},{6,2},{7,3},{8,4},{9,5},{1... | collective-permute-start | bytes 98312 | tf_op jit(solution)/shard_map/sum_z/ppermute | solution.py:17
  55.3 5.3 %collective-permute-start.21 = (f32[4,16,128]{2,1,0:T(8,128)S(1)}, f32[4,16,128]{2,1,0:T(8,128)S(1)}, u32[]{:S(2)}, u32[]{:S(2)}) collective-permute-start(f32[4,16,128]{2,1,0:T(8,128)S(1)} %slice.54), channel_id=1, source_target_pairs={{0,128},{16,144},{32,160},{48,176},{64,192},{80,208},{96,224},{112... | collective-permute-start | bytes 98312 | tf_op jit(solution)/shard_map/sum_z/ppermute | solution.py:17
  60.6 2.6 %collective-permute-done.21 = f32[4,16,128]{2,1,0:T(8,128)S(1)} collective-permute-done((f32[4,16,128]{2,1,0:T(8,128)S(1)}, f32[4,16,128]{2,1,0:T(8,128)S(1)}, u32[]{:S(2)}, u32[]{:S(2)}) %collective-permute-start.21) | collective-permute-done | bytes 32800 | tf_op jit(solution)/shard_map/sum_z/ppermute | solution.py:17
  63.2 0.6 fusion.6
  (36 shorter events, 1.5 us)
Async XLA Ops:
  0.0 18.3 %collective-permute-start.11 = (f32[4,16,128]{2,1,0:T(8,128)}, f32[4,16,128]{2,1,0:T(8,128)S(1)}, u32[]{:S(2)}, u32[]{:S(2)}) collective-permute-start(f32[4,16,128]{2,1,0:T(8,128)} %bitcast.54), channel_id=1, source_target_pairs={{0,4},{1,5},{2,6},{3,7},{4,8},{5,9},{6,10},{7,11},{8,12},{9,13},{1... | collective-permute-start | bytes 98312 | tf_op jit(solution)/shard_map/gather_z/ppermute | solution.py:17
  1.9 18.8 %collective-permute-start.12 = (f32[4,16,128]{2,1,0:T(8,128)}, f32[4,16,128]{2,1,0:T(8,128)S(1)}, u32[]{:S(2)}, u32[]{:S(2)}) collective-permute-start(f32[4,16,128]{2,1,0:T(8,128)} %bitcast.55), channel_id=1, source_target_pairs={{0,8},{1,9},{2,10},{3,11},{4,12},{5,13},{6,14},{7,15},{8,0},{9,1},... | collective-permute-start | bytes 98312 | tf_op jit(solution)/shard_map/gather_z/ppermute | solution.py:17
  5.2 16.0 %collective-permute-start.13 = (f32[4,16,128]{2,1,0:T(8,128)}, f32[4,16,128]{2,1,0:T(8,128)S(1)}, u32[]{:S(2)}, u32[]{:S(2)}) collective-permute-start(f32[4,16,128]{2,1,0:T(8,128)} %bitcast.56), channel_id=1, source_target_pairs={{0,12},{1,13},{2,14},{3,15},{4,0},{5,1},{6,2},{7,3},{8,4},{9,5},{1... | collective-permute-start | bytes 98312 | tf_op jit(solution)/shard_map/gather_z/ppermute | solution.py:17
  6.2 8.0 %collective-permute-start = (f32[4,16,128]{2,1,0:T(8,128)}, f32[4,16,128]{2,1,0:T(8,128)S(1)}, u32[]{:S(2)}, u32[]{:S(2)}) collective-permute-start(f32[4,16,128]{2,1,0:T(8,128)} %bitcast.57), channel_id=1, source_target_pairs={{0,128},{16,144},{32,160},{48,176},{64,192},{80,208},{96,224},{112... | collective-permute-start | bytes 98312 | tf_op jit(solution)/shard_map/gather_z/ppermute | solution.py:17
  15.0 5.7 %collective-permute-start.1 = (f32[8,16,128]{2,1,0:T(8,128)S(1)}, f32[8,16,128]{2,1,0:T(8,128)S(1)}, u32[]{:S(2)}, u32[]{:S(2)}) collective-permute-start(f32[8,16,128]{2,1,0:T(8,128)S(1)} %pad_maximum_fusion.1.refs_3_), channel_id=1, source_target_pairs={{0,32},{16,48},{32,64},{48,80},{64,96},{80,112},{96,0},{112,16},{1... | collective-permute-start | bytes 196616 | tf_op jit(solution)/shard_map/gather_y/ppermute | solution.py:17
  17.3 6.3 %collective-permute-start.2 = (f32[8,16,128]{2,1,0:T(8,128)S(1)}, f32[8,16,128]{2,1,0:T(8,128)S(1)}, u32[]{:S(2)}, u32[]{:S(2)}) collective-permute-start(f32[8,16,128]{2,1,0:T(8,128)S(1)} %pad_maximum_fusion.1.refs_3_), channel_id=1, source_target_pairs={{0,64},{16,80},{32,96},{48,112},{64,0},{80,16},{96,32},{112,48},{1... | collective-permute-start | bytes 196616 | tf_op jit(solution)/shard_map/gather_y/ppermute | solution.py:17
  18.3 8.0 %collective-permute-start.3 = (f32[8,16,128]{2,1,0:T(8,128)S(1)}, f32[8,16,128]{2,1,0:T(8,128)S(1)}, u32[]{:S(2)}, u32[]{:S(2)}) collective-permute-start(f32[8,16,128]{2,1,0:T(8,128)S(1)} %pad_maximum_fusion.1.refs_3_), channel_id=1, source_target_pairs={{0,96},{16,112},{32,0},{48,16},{64,32},{80,48},{96,64},{112,80},{1... | collective-permute-start | bytes 196616 | tf_op jit(solution)/shard_map/gather_y/ppermute | solution.py:17
  20.7 7.0 %collective-permute-start.4 = (f32[8,16,128]{2,1,0:T(8,128)S(1)}, f32[8,16,128]{2,1,0:T(8,128)S(1)}, u32[]{:S(2)}, u32[]{:S(2)}) collective-permute-start(f32[8,16,128]{2,1,0:T(8,128)S(1)} %pad_maximum_fusion.1.refs_3_), channel_id=1, source_target_pairs={{0,16},{16,0},{32,48},{48,32},{64,80},{80,64},{96,112},{112,96},{1... | collective-permute-start | bytes 196616 | tf_op jit(solution)/shard_map/gather_core/ppermute | solution.py:17
  20.7 7.0 %collective-permute-start.5 = (f32[8,16,128]{2,1,0:T(8,128)S(1)}, f32[8,16,128]{2,1,0:T(8,128)S(1)}, u32[]{:S(2)}, u32[]{:S(2)}) collective-permute-start(f32[8,16,128]{2,1,0:T(8,128)S(1)} %collective-permute-done.1.refs_4_), channel_id=1, source_target_pairs={{0,16},{16,0},{32,48},{48,32},{64,80},{80,64},{96,112},{112,96},{1... | collective-permute-start | bytes 196616 | tf_op jit(solution)/shard_map/gather_core/ppermute | solution.py:17
  22.0 15.2 %collective-permute-start.14 = (f32[16,16,128]{2,1,0:T(8,128)S(1)}, f32[16,16,128]{2,1,0:T(8,128)S(1)}, u32[]{:S(2)}, u32[]{:S(2)}) collective-permute-start(f32[16,16,128]{2,1,0:T(8,128)S(1)} %pad_maximum_fusion.refs_3_), channel_id=1, source_target_pairs={{0,1},{1,2},{2,3},{3,0},{4,5},{5,6},{6,7},{7,4},{8,9},{9,10},{10,1... | collective-permute-start | bytes 393224 | tf_op jit(solution)/shard_map/gather_x/ppermute | solution.py:17
  23.6 15.4 %collective-permute-start.15 = (f32[16,16,128]{2,1,0:T(8,128)S(1)}, f32[16,16,128]{2,1,0:T(8,128)S(1)}, u32[]{:S(2)}, u32[]{:S(2)}) collective-permute-start(f32[16,16,128]{2,1,0:T(8,128)S(1)} %pad_maximum_fusion.refs_3_), channel_id=1, source_target_pairs={{0,2},{1,3},{2,0},{3,1},{4,6},{5,7},{6,4},{7,5},{8,10},{9,11},{10,... | collective-permute-start | bytes 393224 | tf_op jit(solution)/shard_map/gather_x/ppermute | solution.py:17
  26.3 12.7 %collective-permute-start.16 = (f32[16,16,128]{2,1,0:T(8,128)S(1)}, f32[16,16,128]{2,1,0:T(8,128)S(1)}, u32[]{:S(2)}, u32[]{:S(2)}) collective-permute-start(f32[16,16,128]{2,1,0:T(8,128)S(1)} %pad_maximum_fusion.refs_3_), channel_id=1, source_target_pairs={{0,3},{1,0},{2,1},{3,2},{4,7},{5,4},{6,5},{7,6},{8,11},{9,8},{10,9... | collective-permute-start | bytes 393224 | tf_op jit(solution)/shard_map/gather_x/ppermute | solution.py:17
  27.7 1.3 %collective-permute-start.6 = (f32[8,16,128]{2,1,0:T(8,128)S(1)}, f32[8,16,128]{2,1,0:T(8,128)S(1)}, u32[]{:S(2)}, u32[]{:S(2)}) collective-permute-start(f32[8,16,128]{2,1,0:T(8,128)S(1)} %collective-permute-done.2.refs_5_), channel_id=1, source_target_pairs={{0,16},{16,0},{32,48},{48,32},{64,80},{80,64},{96,112},{112,96},{1... | collective-permute-start | bytes 196616 | tf_op jit(solution)/shard_map/gather_core/ppermute | solution.py:17
  27.8 1.4 %collective-permute-start.7 = (f32[8,16,128]{2,1,0:T(8,128)S(1)}, f32[8,16,128]{2,1,0:T(8,128)S(1)}, u32[]{:S(2)}, u32[]{:S(2)}) collective-permute-start(f32[8,16,128]{2,1,0:T(8,128)S(1)} %collective-permute-done.3.refs_6_), channel_id=1, source_target_pairs={{0,16},{16,0},{32,48},{48,32},{64,80},{80,64},{96,112},{112,96},{1... | collective-permute-start | bytes 196616 | tf_op jit(solution)/shard_map/gather_core/ppermute | solution.py:17
  29.2 2.8 %copy-start = (f32[1,1,96,128,128]{4,3,2,1,0:T(8,128)S(1)}, f32[1,1,96,128,128]{4,3,2,1,0:T(8,128)}, u32[]{:S(2)}) copy-start(f32[1,1,96,128,128]{4,3,2,1,0:T(8,128)} %param.6) | copy-start | bytes 18874372
  31.9 7.0 %copy-start.1 = (f32[1,1,96,128,128]{4,3,2,1,0:T(8,128)S(1)}, f32[1,1,96,128,128]{4,3,2,1,0:T(8,128)}, u32[]{:S(2)}) copy-start(f32[1,1,96,128,128]{4,3,2,1,0:T(8,128)} %param.6) | copy-start | bytes 18874372
  35.1 7.9 %collective-permute-start.10 = (f32[16,16,128]{2,1,0:T(8,128)S(1)}, f32[16,16,128]{2,1,0:T(8,128)S(1)}, u32[]{:S(2)}, u32[]{:S(2)}) collective-permute-start(f32[16,16,128]{2,1,0:T(8,128)S(1)} %get-tuple-element.14), channel_id=1, source_target_pairs={{0,3},{1,0},{2,1},{3,2},{4,7},{5,4},{6,5},{7,6},{8,11},{9,8},{10,9... | collective-permute-start | bytes 393224 | tf_op jit(solution)/shard_map/sum_x/ppermute | solution.py:17
  37.0 6.4 %collective-permute-start.8 = (f32[16,16,128]{2,1,0:T(8,128)S(1)}, f32[16,16,128]{2,1,0:T(8,128)S(1)}, u32[]{:S(2)}, u32[]{:S(2)}) collective-permute-start(f32[16,16,128]{2,1,0:T(8,128)S(1)} %get-tuple-element.12), channel_id=1, source_target_pairs={{0,1},{1,2},{2,3},{3,0},{4,5},{5,6},{6,7},{7,4},{8,9},{9,10},{10,1... | collective-permute-start | bytes 393224 | tf_op jit(solution)/shard_map/sum_x/ppermute | solution.py:17
  37.2 9.0 %collective-permute-start.9 = (f32[16,16,128]{2,1,0:T(8,128)S(1)}, f32[16,16,128]{2,1,0:T(8,128)S(1)}, u32[]{:S(2)}, u32[]{:S(2)}) collective-permute-start(f32[16,16,128]{2,1,0:T(8,128)S(1)} %get-tuple-element.13), channel_id=1, source_target_pairs={{0,2},{1,3},{2,0},{3,1},{4,6},{5,7},{6,4},{7,5},{8,10},{9,11},{10,... | collective-permute-start | bytes 393224 | tf_op jit(solution)/shard_map/sum_x/ppermute | solution.py:17
  41.7 4.5 %collective-permute-start.17 = (f32[32,16,128]{2,1,0:T(8,128)S(1)}, f32[32,16,128]{2,1,0:T(8,128)S(1)}, u32[]{:S(2)}, u32[]{:S(2)}) collective-permute-start(f32[32,16,128]{2,1,0:T(8,128)S(1)} %get-tuple-element.16), channel_id=1, source_target_pairs={{0,16},{16,0},{32,48},{48,32},{64,80},{80,64},{96,112},{112,96},{1... | collective-permute-start | bytes 786440 | tf_op jit(solution)/shard_map/sum_core/ppermute | solution.py:17
  46.3 6.5 %collective-permute-start.18 = (f32[8,16,128]{2,1,0:T(8,128)S(1)}, f32[8,16,128]{2,1,0:T(8,128)S(1)}, u32[]{:S(2)}, u32[]{:S(2)}) collective-permute-start(f32[8,16,128]{2,1,0:T(8,128)S(1)} %get-tuple-element.21), channel_id=1, source_target_pairs={{0,32},{16,48},{32,64},{48,80},{64,96},{80,112},{96,0},{112,16},{1... | collective-permute-start | bytes 196616 | tf_op jit(solution)/shard_map/sum_y/ppermute | solution.py:17
  47.4 7.8 %collective-permute-start.19 = (f32[8,16,128]{2,1,0:T(8,128)S(1)}, f32[8,16,128]{2,1,0:T(8,128)S(1)}, u32[]{:S(2)}, u32[]{:S(2)}) collective-permute-start(f32[8,16,128]{2,1,0:T(8,128)S(1)} %get-tuple-element.23), channel_id=1, source_target_pairs={{0,64},{16,80},{32,96},{48,112},{64,0},{80,16},{96,32},{112,48},{1... | collective-permute-start | bytes 196616 | tf_op jit(solution)/shard_map/sum_y/ppermute | solution.py:17
  49.0 6.3 %collective-permute-start.20 = (f32[8,16,128]{2,1,0:T(8,128)S(1)}, f32[8,16,128]{2,1,0:T(8,128)S(1)}, u32[]{:S(2)}, u32[]{:S(2)}) collective-permute-start(f32[8,16,128]{2,1,0:T(8,128)S(1)} %get-tuple-element.22), channel_id=1, source_target_pairs={{0,96},{16,112},{32,0},{48,16},{64,32},{80,48},{96,64},{112,80},{1... | collective-permute-start | bytes 196616 | tf_op jit(solution)/shard_map/sum_y/ppermute | solution.py:17
  50.6 9.9 %collective-permute-start.22 = (f32[4,16,128]{2,1,0:T(8,128)S(1)}, f32[4,16,128]{2,1,0:T(8,128)S(1)}, u32[]{:S(2)}, u32[]{:S(2)}) collective-permute-start(f32[4,16,128]{2,1,0:T(8,128)S(1)} %get-tuple-element.24), channel_id=1, source_target_pairs={{0,4},{1,5},{2,6},{3,7},{4,8},{5,9},{6,10},{7,11},{8,12},{9,13},{1... | collective-permute-start | bytes 98312 | tf_op jit(solution)/shard_map/sum_z/ppermute | solution.py:17
  52.8 7.8 %collective-permute-start.23 = (f32[4,16,128]{2,1,0:T(8,128)S(1)}, f32[4,16,128]{2,1,0:T(8,128)S(1)}, u32[]{:S(2)}, u32[]{:S(2)}) collective-permute-start(f32[4,16,128]{2,1,0:T(8,128)S(1)} %get-tuple-element.26), channel_id=1, source_target_pairs={{0,8},{1,9},{2,10},{3,11},{4,12},{5,13},{6,14},{7,15},{8,0},{9,1},... | collective-permute-start | bytes 98312 | tf_op jit(solution)/shard_map/sum_z/ppermute | solution.py:17
  52.8 7.8 %collective-permute-start.24 = (f32[4,16,128]{2,1,0:T(8,128)S(1)}, f32[4,16,128]{2,1,0:T(8,128)S(1)}, u32[]{:S(2)}, u32[]{:S(2)}) collective-permute-start(f32[4,16,128]{2,1,0:T(8,128)S(1)} %get-tuple-element.25), channel_id=1, source_target_pairs={{0,12},{1,13},{2,14},{3,15},{4,0},{5,1},{6,2},{7,3},{8,4},{9,5},{1... | collective-permute-start | bytes 98312 | tf_op jit(solution)/shard_map/sum_z/ppermute | solution.py:17
  55.3 7.9 %collective-permute-start.21 = (f32[4,16,128]{2,1,0:T(8,128)S(1)}, f32[4,16,128]{2,1,0:T(8,128)S(1)}, u32[]{:S(2)}, u32[]{:S(2)}) collective-permute-start(f32[4,16,128]{2,1,0:T(8,128)S(1)} %slice.54), channel_id=1, source_target_pairs={{0,128},{16,144},{32,160},{48,176},{64,192},{80,208},{96,224},{112... | collective-permute-start | bytes 98312 | tf_op jit(solution)/shard_map/sum_z/ppermute | solution.py:17

commit v3 on v2

v3 whole, which is shorter than its diff:
```python
import functools
import jax
import jax.numpy as jnp
from jax import lax
from jax.experimental import pallas as pl
from jax.experimental.pallas import tpu as pltpu
from jax.sharding import PartitionSpec as P

AXIS = 16
GROUP = 4
CHUNK = 8
BF16 = jnp.bfloat16
F32 = jnp.float32
AXES = ("row", "col")


def send(value, target):
    pairs = []
    for row in range(AXIS):
        for col in range(AXIS):
            place = target(row, col)
            if place is not None:
                pairs.append((row * AXIS + col, place[0] * AXIS + place[1]))
    return lax.ppermute(value, AXES, pairs)


def to_other_core(row, col):
    return row ^ 1, col


def along_z(step):
    def target(row, col):
        if row % 2 == 1:
            return row, (col + 4 * step) % AXIS
        return (row ^ 8, col) if step == 1 else None

    return target


def along_side(step):
    def target(row, col):
        if row % 2 == 1:
            return row, col // 4 * 4 + (col + step) % 4
        return row // 8 * 8 + (row // 2 + step) % 4 * 2, col

    return target


def multiply_kernel(held, *refs):
    core, source, target, live = refs[:4]
    parts = refs[4:8]
    tiles = refs[8]
    outs = refs[9:13]
    split, total, block, arrived = refs[13:]
    chunks = block.shape[0] // CHUNK
    vecs = split.shape[1] // 2
    edge = split.shape[2] // 2
    count = outs[0].shape[0]
    blocks = count // GROUP

    def fetch(chunk):
        span = pl.ds(chunk * CHUNK, CHUNK)
        return pltpu.make_async_copy(tiles.at[span], block.at[span], arrived.at[chunk])

    for chunk in range(chunks):
        fetch(chunk).start()

    def put(place, values):
        high = values.astype(BF16)
        low = (values - high.astype(F32)).astype(BF16)
        span = slice(place, place + values.shape[0])
        split[span, :vecs, :edge] = high
        split[span, :vecs, edge:] = high
        split[span, vecs:, :edge] = low
        split[span, vecs:, edge:] = low

    def one_slot(transposed, slot):
        tile = block[slot]
        high = tile.astype(BF16)
        low = (tile - high.astype(F32)).astype(BF16)
        both = jnp.concatenate([high, low], axis=0 if transposed else 1)
        product = lax.dot_general(
            split[source[slot]],
            both,
            (((1,), (0 if transposed else 1,)), ((), ())),
            preferred_element_type=F32,
        )
        total[target[slot]] += product[:vecs] + product[vecs:]

    def run(transposed):
        def one_chunk(chunk, carry):
            fetch(chunk).wait()

            @pl.when(chunk * CHUNK < live[0])
            def _():
                for step in range(CHUNK):
                    one_slot(transposed, chunk * CHUNK + step)

            return carry

        lax.fori_loop(0, chunks, one_chunk, 0)

    total[...] = jnp.zeros_like(total)

    @pl.when(core[0] == 0)
    def _():
        for index, part in enumerate(parts):
            put(index * count, part[:count])
        run(not held)

    @pl.when(core[0] != 0)
    def _():
        for index, part in enumerate(parts):
            if held:
                for step in range(GROUP):
                    span = slice(2 * step * blocks, (2 * step + 1) * blocks)
                    put(index * count + step * blocks, part[span])
            else:
                put(index * count, part[...])
        run(held)

    for index, out in enumerate(outs):
        out[...] = total[index * count : (index + 1) * count]


def multiply(held, core, source, target, live, parts, tiles):
    slots, edge = tiles.shape[0], tiles.shape[1]
    vecs = parts[0].shape[1]
    count = parts[0].shape[0] // (2 if held else 1)
    places = GROUP * count
    scalars = [pl.BlockSpec(memory_space=pltpu.SMEM)] * 4
    vector = pl.BlockSpec(memory_space=pltpu.VMEM)
    return pl.pallas_call(
        functools.partial(multiply_kernel, held),
        out_shape=[jax.ShapeDtypeStruct((count, vecs, edge), F32)] * GROUP,
        in_specs=scalars + [vector] * GROUP + [pl.BlockSpec(memory_space=pl.ANY)],
        out_specs=[vector] * GROUP,
        scratch_shapes=[
            pltpu.VMEM((places, 2 * vecs, 2 * edge), BF16),
            pltpu.VMEM((places + 8, vecs, edge), F32),
            pltpu.VMEM((slots, edge, edge), F32),
            pltpu.SemaphoreType.DMA((slots // CHUNK,)),
        ],
        compiler_params=pltpu.CompilerParams(vmem_limit_bytes=20 * 1024 * 1024),
        cost_estimate=pl.CostEstimate(
            flops=8 * slots * vecs * edge * edge, bytes_accessed=4 * slots * edge * edge, transcendentals=0
        ),
        name="first" if held else "second",
    )(core, source, target, live, *parts, tiles)


def merge_kernel(core, *refs):
    kept, got, outs = refs[:4], refs[4:8], refs[8:12]
    count = kept[0].shape[0]
    blocks = count // GROUP

    @pl.when(core[0] == 0)
    def _():
        for index in range(GROUP):
            outs[index][:count] = kept[index][...] + got[index][...]
            outs[index][count:] = jnp.zeros_like(got[index])

    @pl.when(core[0] != 0)
    def _():
        for index in range(GROUP):
            for step in range(GROUP):
                span = slice(step * blocks, (step + 1) * blocks)
                low = 2 * step * blocks
                outs[index][low : low + blocks] = kept[index][span]
                outs[index][low + blocks : low + 2 * blocks] = got[index][span]


def merge(core, kept, got):
    count, vecs, edge = kept[0].shape
    vector = pl.BlockSpec(memory_space=pltpu.VMEM)
    return pl.pallas_call(
        merge_kernel,
        out_shape=[jax.ShapeDtypeStruct((2 * count, vecs, edge), F32)] * GROUP,
        in_specs=[pl.BlockSpec(memory_space=pltpu.SMEM)] + [vector] * (2 * GROUP),
        out_specs=[vector] * GROUP,
        compiler_params=pltpu.CompilerParams(vmem_limit_bytes=8 * 1024 * 1024),
        name="merge",
    )(core, *kept, *got)


def shards(vectors, tiles, tile_rows, tile_cols, counts):
    blocks = vectors.shape[0]
    vecs, edge = vectors.shape[3], vectors.shape[4]
    slots = tiles.shape[2]
    row, col = lax.axis_index("row"), lax.axis_index("col")
    core = (row & 1).reshape(1)
    tiles = tiles.reshape(slots, edge, edge)
    rows, cols = tile_rows.reshape(slots), tile_cols.reshape(slots)
    live = counts.reshape(1)
    row_block, row_col = rows // AXIS, rows % AXIS
    col_block, col_row = cols // AXIS, cols % AXIS
    is_live = jnp.arange(slots, dtype=jnp.int32) < live
    mirror = is_live & (rows * AXIS + row < (col_block * AXIS + col) * AXIS + col_row)

    def row_place(step_y):
        z, inside = (col_row ^ row) >> 3, col_row & 1
        return (((step_y & 3) * 2 + z) * 2 + inside) * blocks + col_block

    def col_place(step_x, step_z):
        return ((step_x & 3) * GROUP + (step_z & 3)) * blocks + row_block

    nowhere = blocks * AXIS
    step_y = (col_row >> 1) - (row >> 1)
    step_x, step_z = row_col - col, (row_col >> 2) - (col >> 2)
    forward_source = row_place(-step_y)
    forward_target = jnp.where(is_live, col_place(step_x, step_z), nowhere)
    backward_source = col_place(-step_x, -step_z)
    backward_target = jnp.where(mirror, row_place(step_y), nowhere)
    even = core == 0
    first_source = jnp.where(even, forward_source, backward_source)
    first_target = jnp.where(even, forward_target, backward_target)
    second_source = jnp.where(even, backward_source, forward_source)
    second_target = jnp.where(even, backward_target, forward_target)

    own = vectors.reshape(blocks, vecs, edge)
    with jax.named_scope("gather_core"):
        pair = jnp.concatenate([own, send(own, to_other_core)])
    with jax.named_scope("gather_z"):
        column = jnp.concatenate([pair] + [send(pair, along_z(step)) for step in (1, 2, 3)])
    with jax.named_scope("gather_side"):
        held = [column] + [send(column, along_side(step)) for step in (1, 2, 3)]
    with jax.named_scope("gather_swap"):
        swapped = []
        for part in held:
            partner = part.reshape(GROUP, 2, blocks, vecs, edge)[:, 1].reshape(GROUP * blocks, vecs, edge)
            swapped.append(send(jnp.where(even, part[: GROUP * blocks], partner), to_other_core))
    given = multiply(True, core, first_source, first_target, live, held, tiles)
    with jax.named_scope("sum_swap"):
        got = [send(part, to_other_core) for part in given]
    kept = multiply(False, core, second_source, second_target, live, swapped, tiles)
    merged = merge(core, kept, got)
    with jax.named_scope("sum_side"):
        column = merged[0]
        for step in (1, 2, 3):
            column = column + send(merged[step], along_side(step))
    with jax.named_scope("sum_z"):
        column = column.reshape(GROUP, 2 * blocks, vecs, edge)
        pair = column[0]
        for step in (1, 2, 3):
            pair = pair + send(column[step], along_z(step))
    with jax.named_scope("sum_core"):
        result = pair[:blocks] + send(pair[blocks:], to_other_core)
    return result.reshape(blocks, 1, 1, vecs, edge)


def solution(mesh):
    in_specs = (
        P(None, "col", "row", None, None),
        P("row", "col", None, None, None),
        P("row", "col", None),
        P("row", "col", None),
        P("row", "col"),
    )
    out_specs = P(None, "col", "row", None, None)
    return jax.shard_map(shards, mesh=mesh, in_specs=in_specs, out_specs=out_specs, check_vma=False)
```

time: 64 us -> 67.9 us (1.061)
  the two profiles are of different devices: /device:TPU:8 before, /device:TPU:1 now
where the time goes in v3:
time: 67.9 us; the launch traced here: 67.5 us
  starting transfers between devices  25.4 us (37%)
  waiting for transfers between devices  25 us (37%)
  Pallas kernels  8.88 us (13%)
  other arithmetic  3.69 us (5%)
  local copies, waits for them, and re-layouts  3.62 us (5%)
  between operations  0.93 us (1%)
    ppermute x22, starting transfers between devices, send(): return lax.ppermute(value, AXES, pairs)  25.4 us
    ppermute x22, waiting for transfers between devices, send(): return lax.ppermute(value, AXES, pairs)  25 us
    pallas_call x2, Pallas kernels, multiply(): pl.pallas_call(functools.partial(multiply_kernel, held), out_shape=[jax.S...  8.79 us
    unnamed x8, local copies, waits for them, and re-layouts  3.56 us
  transfers between devices with their start and end apart: 22, of which 9 were waited for; matrix products, arithmetic and copies ran while one was open for 4% of the time, Pallas kernels for 13%

profile of v3, /device:TPU:1, one launch (start us, length us, event | category | flops | bytes accessed | tf_op | source)
XLA Modules:
  0.0 67.5 jit_solution(10165771732267484760)
XLA Ops:
  0.0 3.2 %collective-permute-start = (f32[4,16,128]{2,1,0:T(8,128)}, f32[4,16,128]{2,1,0:T(8,128)S(1)}, u32[]{:S(2)}, u32[]{:S(2)}) collective-permute-start(f32[4,16,128]{2,1,0:T(8,128)} %bitcast.80), channel_id=1, source_target_pairs={{0,16},{1,17},{2,18},{3,19},{4,20},{5,21},{6,22},{7,23},{8,24},{9,... | collective-permute-start | bytes 98312 | tf_op jit(solution)/shard_map/gather_core/ppermute | solution.py:24
  3.2 0.8 %constant_dynamic-update-slice_fusion.4 = f32[32,16,128]{2,1,0:T(8,128)S(1)} fusion(f32[4,1,1,16,128]{4,3,2,1,0:T(8,128)} %param.5), kind=kLoop, calls=%fused_computation.15 | loop fusion | bytes 65536
  4.7 0.7 %broadcast_select_fusion = (s32[96]{0:T(128)S(1)}, s32[96]{0:T(128)S(1)}, s32[96]{0:T(128)S(1)}, s32[96]{0:T(128)S(1)}, s32[96]{0:T(128)S(1)}) fusion(pred[]{:T(512)} %bitcast.1, s32[]{:T(128)S(6)} %shift_right_arithmetic.17, s32[]{:T(128)S(6)} %axis_index.25, s32[1,1,96]{2,1,0:T(1,128)} %param.7, s32[]{:T(128)} %bitcast.71, s32[]{:T(128)S(6)} %shift_right_arithmetic.19, ...), kind=kLoop, calls=%fused_computation.28 | loop fusion | flops 6816 | bytes 2709 | tf_op jit(solution)/shard_map/jit(_where)/select_n | solution.py:216
  5.4 0.8 %pad_maximum_fusion = f32[8,16,128]{2,1,0:T(8,128)S(1)} fusion(f32[4,16,128]{2,1,0:T(8,128)S(1)} %collective-permute-done, f32[4,16,128]{2,1,0:T(8,128)} %bitcast.81), kind=kLoop, calls=%fused_computation.8 | loop fusion | flops 16384 | bytes 131072 | tf_op jit(solution)/shard_map/gather_core/concatenate | solution.py:222
  6.1 4.5 %collective-permute-start.3 = (f32[8,16,128]{2,1,0:T(8,128)S(1)}, f32[8,16,128]{2,1,0:T(8,128)S(1)}, u32[]{:S(2)}, u32[]{:S(2)}) collective-permute-start(f32[8,16,128]{2,1,0:T(8,128)S(1)} %pad_maximum_fusion), channel_id=1, source_target_pairs={{16,28},{17,29},{18,30},{19,31},{20,16},{21,17},{22,18},{23,19},{2... | collective-permute-start | bytes 196616 | tf_op jit(solution)/shard_map/gather_z/ppermute | solution.py:24
  10.7 1.9 %collective-permute-start.2 = (f32[8,16,128]{2,1,0:T(8,128)S(1)}, f32[8,16,128]{2,1,0:T(8,128)S(1)}, u32[]{:S(2)}, u32[]{:S(2)}) collective-permute-start(f32[8,16,128]{2,1,0:T(8,128)S(1)} %pad_maximum_fusion), channel_id=1, source_target_pairs={{16,24},{17,25},{18,26},{19,27},{20,28},{21,29},{22,30},{23,31},{2... | collective-permute-start | bytes 196616 | tf_op jit(solution)/shard_map/gather_z/ppermute | solution.py:24
  12.6 0.4 collective-permute-start.1
  12.9 4.6 %collective-permute-done.1 = f32[8,16,128]{2,1,0:T(8,128)S(1)} collective-permute-done((f32[8,16,128]{2,1,0:T(8,128)S(1)}, f32[8,16,128]{2,1,0:T(8,128)S(1)}, u32[]{:S(2)}, u32[]{:S(2)}) %collective-permute-start.1) | collective-permute-done | bytes 65568 | tf_op jit(solution)/shard_map/gather_z/ppermute | solution.py:24
  17.6 0.3 collective-permute-done.2
  17.9 2.6 %collective-permute-start.9 = (f32[32,16,128]{2,1,0:T(8,128)S(1)}, f32[32,16,128]{2,1,0:T(8,128)S(1)}, u32[]{:S(2)}, u32[]{:S(2)}) collective-permute-start(f32[32,16,128]{2,1,0:T(8,128)S(1)} %constant_dynamic-update-slice_fusion.refs_4_), channel_id=1, source_target_pairs={{0,96},{1,97},{2,98},{3,99},{4,100},{5,101},{6,102},{7,103},{8,104... | collective-permute-start | bytes 786440 | tf_op jit(solution)/shard_map/gather_side/ppermute | solution.py:24
  20.5 0.7 %broadcast_select_fusion.1 = (s32[96]{0:T(128)S(1)}, s32[96]{0:T(128)S(1)}, s32[96]{0:T(128)S(1)}) fusion(pred[]{:T(512)} %bitcast.1, s32[96]{0:T(128)S(1)} %get-tuple-element.32, s32[]{:T(128)S(6)} %axis_index.23, s32[]{:T(128)S(6)} %shift_right_arithmetic.19, s32[1,1,96]{2,1,0:T(1,128)} %param.8, s32[96]{0:T(128)S(1)} %get-tuple-element.33, ...), kind=kLoop, calls=%fused_computation.29 | loop fusion | flops 4512 | bytes 2705 | tf_op jit(solution)/shard_map/jit(_where)/select_n | solution.py:215
  21.2 0.6 collective-permute-start.7
  21.8 0.6 collective-permute-start.5
  22.4 0.8 %maximum_select_fusion = f32[16,16,128]{2,1,0:T(8,128)S(1)} fusion(f32[8,16,128]{2,1,0:T(8,128)S(1)} %collective-permute-done.1, f32[4,16,128]{2,1,0:T(8,128)S(1)} %collective-permute-done, f32[4,16,128]{2,1,0:T(8,128)} %bitcast.82, f32[4,1,4,16,128]{4,3,2,1,0:T(8,128)S(1)} %slice.58, pred[]{:T(512)} %bitcast.1), kind=kLoop, calls=%fused_computation.4 | loop fusion | flops 98304 | bytes 393217 | tf_op jit(solution)/shard_map/gather_swap/jit(_where)/select_n | solution.py:231
  23.3 3.3 %collective-permute-done.9.refs_7_ = f32[32,16,128]{2,1,0:T(8,128)S(1)} collective-permute-done((f32[32,16,128]{2,1,0:T(8,128)S(1)}, f32[32,16,128]{2,1,0:T(8,128)S(1)}, u32[]{:S(2)}, u32[]{:S(2)}) %collective-permute-start.9) | collective-permute-done | bytes 262176 | tf_op jit(solution)/shard_map/gather_side/ppermute | solution.py:24
  26.7 1.3 %collective-permute-done.7.refs_6_ = f32[32,16,128]{2,1,0:T(8,128)S(1)} collective-permute-done((f32[32,16,128]{2,1,0:T(8,128)S(1)}, f32[32,16,128]{2,1,0:T(8,128)S(1)}, u32[]{:S(2)}, u32[]{:S(2)}) %collective-permute-start.7) | collective-permute-done | bytes 262176 | tf_op jit(solution)/shard_map/gather_side/ppermute | solution.py:24
  28.2 2.6 %collective-permute-done.5.refs_5_ = f32[32,16,128]{2,1,0:T(8,128)S(1)} collective-permute-done((f32[32,16,128]{2,1,0:T(8,128)S(1)}, f32[32,16,128]{2,1,0:T(8,128)S(1)}, u32[]{:S(2)}, u32[]{:S(2)}) %collective-permute-start.5) | collective-permute-done | bytes 262176 | tf_op jit(solution)/shard_map/gather_side/ppermute | solution.py:24
  30.9 2.8 %copy-done = f32[1,1,96,128,128]{4,3,2,1,0:T(8,128)S(1)} copy-done((f32[1,1,96,128,128]{4,3,2,1,0:T(8,128)S(1)}, f32[1,1,96,128,128]{4,3,2,1,0:T(8,128)}, u32[]{:S(2)}) %copy-start) | copy-done | bytes 6291480
  33.7 3.9 %first.1 = (f32[16,16,128]{2,1,0:T(8,128)S(1)}, f32[16,16,128]{2,1,0:T(8,128)S(1)}, f32[16,16,128]{2,1,0:T(8,128)S(1)}, f32[16,16,128]{2,1,0:T(8,128)S(1)}) custom-call(s32[1]{0:T(128)} %bitcast.refs_0_.core, s32[96]{0:T(128)S(1)} %get-tuple-element.34.refs_1_, s32[96]{0:T(128)S(1)} %get-tuple-element.29.refs_2_, s32[1]{0:T(128)} %bitcast.73.refs_3_, ...), custom_call_target="tpu_custom_call" | custom-call | flops 201326592 | bytes 6291456 | tf_op jit(solution)/shard_map/first/pallas_call | solution.py:133
  37.7 0.6 collective-permute-start.11
  38.3 0.1 collective-permute-start.12
  38.4 0.4 collective-permute-start.13
  38.9 4.9 %second.1 = (f32[16,16,128]{2,1,0:T(8,128)S(1)}, f32[16,16,128]{2,1,0:T(8,128)S(1)}, f32[16,16,128]{2,1,0:T(8,128)S(1)}, f32[16,16,128]{2,1,0:T(8,128)S(1)}) custom-call(s32[1]{0:T(128)} %bitcast.refs_0_.core, s32[96]{0:T(128)S(1)} %get-tuple-element.41.refs_1_, s32[96]{0:T(128)S(1)} %get-tuple-element.40.refs_2_, s32[1]{0:T(128)} %bitcast.72.refs_3_, ...), custom_call_target="tpu_custom_call" | custom-call | flops 201326592 | bytes 6291456 | tf_op jit(solution)/shard_map/second/pallas_call | solution.py:133
  44.0 1.0 %collective-permute-start.16 = (f32[32,16,128]{2,1,0:T(8,128)S(1)}, f32[32,16,128]{2,1,0:T(8,128)S(1)}, u32[]{:S(2)}, u32[]{:S(2)}) collective-permute-start(f32[32,16,128]{2,1,0:T(8,128)S(1)} %get-tuple-element.27), channel_id=1, source_target_pairs={{0,64},{1,65},{2,66},{3,67},{4,68},{5,69},{6,70},{7,71},{8,72},{9,... | collective-permute-start | bytes 786440 | tf_op jit(solution)/shard_map/sum_side/ppermute | solution.py:24
  45.1 1.6 %collective-permute-start.17 = (f32[32,16,128]{2,1,0:T(8,128)S(1)}, f32[32,16,128]{2,1,0:T(8,128)S(1)}, u32[]{:S(2)}, u32[]{:S(2)}) collective-permute-start(f32[32,16,128]{2,1,0:T(8,128)S(1)} %get-tuple-element.28), channel_id=1, source_target_pairs={{0,96},{1,97},{2,98},{3,99},{4,100},{5,101},{6,102},{7,103},{8,104... | collective-permute-start | bytes 786440 | tf_op jit(solution)/shard_map/sum_side/ppermute | solution.py:24
  46.7 6.9 %collective-permute-done.15 = f32[32,16,128]{2,1,0:T(8,128)S(1)} collective-permute-done((f32[32,16,128]{2,1,0:T(8,128)S(1)}, f32[32,16,128]{2,1,0:T(8,128)S(1)}, u32[]{:S(2)}, u32[]{:S(2)}) %collective-permute-start.15) | collective-permute-done | bytes 262176 | tf_op jit(solution)/shard_map/sum_side/ppermute | solution.py:24
  53.6 0.6 collective-permute-done.17
  54.4 5.1 %collective-permute-start.20 = (f32[8,16,128]{2,1,0:T(8,128)S(1)}, f32[8,16,128]{2,1,0:T(8,128)S(1)}, u32[]{:S(2)}, u32[]{:S(2)}) collective-permute-start(f32[8,16,128]{2,1,0:T(8,128)S(1)} %get-tuple-element.38), channel_id=1, source_target_pairs={{16,28},{17,29},{18,30},{19,31},{20,16},{21,17},{22,18},{23,19},{2... | collective-permute-start | bytes 196616 | tf_op jit(solution)/shard_map/sum_z/ppermute | solution.py:24
  59.5 1.9 %collective-permute-start.19 = (f32[8,16,128]{2,1,0:T(8,128)S(1)}, f32[8,16,128]{2,1,0:T(8,128)S(1)}, u32[]{:S(2)}, u32[]{:S(2)}) collective-permute-start(f32[8,16,128]{2,1,0:T(8,128)S(1)} %get-tuple-element.39), channel_id=1, source_target_pairs={{16,24},{17,25},{18,26},{19,27},{20,28},{21,29},{22,30},{23,31},{2... | collective-permute-start | bytes 196616 | tf_op jit(solution)/shard_map/sum_z/ppermute | solution.py:24
  61.5 4.1 %collective-permute-done.19 = f32[8,16,128]{2,1,0:T(8,128)S(1)} collective-permute-done((f32[8,16,128]{2,1,0:T(8,128)S(1)}, f32[8,16,128]{2,1,0:T(8,128)S(1)}, u32[]{:S(2)}, u32[]{:S(2)}) %collective-permute-start.19) | collective-permute-done | bytes 65568 | tf_op jit(solution)/shard_map/sum_z/ppermute | solution.py:24
  65.7 1.2 %collective-permute-done.21 = f32[4,16,128]{2,1,0:T(8,128)S(1)} collective-permute-done((f32[4,16,128]{2,1,0:T(8,128)S(1)}, f32[4,16,128]{2,1,0:T(8,128)S(1)}, u32[]{:S(2)}, u32[]{:S(2)}) %collective-permute-start.21) | collective-permute-done | bytes 32800 | tf_op jit(solution)/shard_map/sum_core/ppermute | solution.py:24
  66.9 0.6 fusion.2
  (41 shorter events, 1.1 us)
Async XLA Ops:
  0.0 5.4 %collective-permute-start = (f32[4,16,128]{2,1,0:T(8,128)}, f32[4,16,128]{2,1,0:T(8,128)S(1)}, u32[]{:S(2)}, u32[]{:S(2)}) collective-permute-start(f32[4,16,128]{2,1,0:T(8,128)} %bitcast.80), channel_id=1, source_target_pairs={{0,16},{1,17},{2,18},{3,19},{4,20},{5,21},{6,22},{7,23},{8,24},{9,... | collective-permute-start | bytes 98312 | tf_op jit(solution)/shard_map/gather_core/ppermute | solution.py:24
  6.1 11.8 %collective-permute-start.3 = (f32[8,16,128]{2,1,0:T(8,128)S(1)}, f32[8,16,128]{2,1,0:T(8,128)S(1)}, u32[]{:S(2)}, u32[]{:S(2)}) collective-permute-start(f32[8,16,128]{2,1,0:T(8,128)S(1)} %pad_maximum_fusion), channel_id=1, source_target_pairs={{16,28},{17,29},{18,30},{19,31},{20,16},{21,17},{22,18},{23,19},{2... | collective-permute-start | bytes 196616 | tf_op jit(solution)/shard_map/gather_z/ppermute | solution.py:24
  10.7 7.2 %collective-permute-start.2 = (f32[8,16,128]{2,1,0:T(8,128)S(1)}, f32[8,16,128]{2,1,0:T(8,128)S(1)}, u32[]{:S(2)}, u32[]{:S(2)}) collective-permute-start(f32[8,16,128]{2,1,0:T(8,128)S(1)} %pad_maximum_fusion), channel_id=1, source_target_pairs={{16,24},{17,25},{18,26},{19,27},{20,28},{21,29},{22,30},{23,31},{2... | collective-permute-start | bytes 196616 | tf_op jit(solution)/shard_map/gather_z/ppermute | solution.py:24
  12.6 5.0 %collective-permute-start.1 = (f32[8,16,128]{2,1,0:T(8,128)S(1)}, f32[8,16,128]{2,1,0:T(8,128)S(1)}, u32[]{:S(2)}, u32[]{:S(2)}) collective-permute-start(f32[8,16,128]{2,1,0:T(8,128)S(1)} %pad_maximum_fusion), channel_id=1, source_target_pairs={{0,128},{1,129},{2,130},{3,131},{4,132},{5,133},{6,134},{7,135},{8... | collective-permute-start | bytes 196616 | tf_op jit(solution)/shard_map/gather_z/ppermute | solution.py:24
  17.9 8.7 %collective-permute-start.9 = (f32[32,16,128]{2,1,0:T(8,128)S(1)}, f32[32,16,128]{2,1,0:T(8,128)S(1)}, u32[]{:S(2)}, u32[]{:S(2)}) collective-permute-start(f32[32,16,128]{2,1,0:T(8,128)S(1)} %constant_dynamic-update-slice_fusion.refs_4_), channel_id=1, source_target_pairs={{0,96},{1,97},{2,98},{3,99},{4,100},{5,101},{6,102},{7,103},{8,104... | collective-permute-start | bytes 786440 | tf_op jit(solution)/shard_map/gather_side/ppermute | solution.py:24
  21.2 6.9 %collective-permute-start.7 = (f32[32,16,128]{2,1,0:T(8,128)S(1)}, f32[32,16,128]{2,1,0:T(8,128)S(1)}, u32[]{:S(2)}, u32[]{:S(2)}) collective-permute-start(f32[32,16,128]{2,1,0:T(8,128)S(1)} %constant_dynamic-update-slice_fusion.refs_4_), channel_id=1, source_target_pairs={{0,64},{1,65},{2,66},{3,67},{4,68},{5,69},{6,70},{7,71},{8,72},{9,... | collective-permute-start | bytes 786440 | tf_op jit(solution)/shard_map/gather_side/ppermute | solution.py:24
  21.8 9.0 %collective-permute-start.5 = (f32[32,16,128]{2,1,0:T(8,128)S(1)}, f32[32,16,128]{2,1,0:T(8,128)S(1)}, u32[]{:S(2)}, u32[]{:S(2)}) collective-permute-start(f32[32,16,128]{2,1,0:T(8,128)S(1)} %constant_dynamic-update-slice_fusion.refs_4_), channel_id=1, source_target_pairs={{0,32},{1,33},{2,34},{3,35},{4,36},{5,37},{6,38},{7,39},{8,40},{9,... | collective-permute-start | bytes 786440 | tf_op jit(solution)/shard_map/gather_side/ppermute | solution.py:24
  23.2 15.1 %collective-permute-start.4 = (f32[16,16,128]{2,1,0:T(8,128)S(1)}, f32[16,16,128]{2,1,0:T(8,128)S(1)}, u32[]{:S(2)}, u32[]{:S(2)}) collective-permute-start(f32[16,16,128]{2,1,0:T(8,128)S(1)} %maximum_select_fusion), channel_id=1, source_target_pairs={{0,16},{1,17},{2,18},{3,19},{4,20},{5,21},{6,22},{7,23},{8,24},{9,... | collective-permute-start | bytes 393224 | tf_op jit(solution)/shard_map/gather_swap/ppermute | solution.py:24
  26.6 11.8 %collective-permute-start.10 = (f32[16,16,128]{2,1,0:T(8,128)S(1)}, f32[16,16,128]{2,1,0:T(8,128)S(1)}, u32[]{:S(2)}, u32[]{:S(2)}) collective-permute-start(f32[16,16,128]{2,1,0:T(8,128)S(1)} %slice_select_fusion), channel_id=1, source_target_pairs={{0,16},{1,17},{2,18},{3,19},{4,20},{5,21},{6,22},{7,23},{8,24},{9,... | collective-permute-start | bytes 393224 | tf_op jit(solution)/shard_map/gather_swap/ppermute | solution.py:24
  28.1 10.7 %collective-permute-start.8 = (f32[16,16,128]{2,1,0:T(8,128)S(1)}, f32[16,16,128]{2,1,0:T(8,128)S(1)}, u32[]{:S(2)}, u32[]{:S(2)}) collective-permute-start(f32[16,16,128]{2,1,0:T(8,128)S(1)} %slice_select_fusion.1), channel_id=1, source_target_pairs={{0,16},{1,17},{2,18},{3,19},{4,20},{5,21},{6,22},{7,23},{8,24},{9,... | collective-permute-start | bytes 393224 | tf_op jit(solution)/shard_map/gather_swap/ppermute | solution.py:24
  30.8 8.1 %collective-permute-start.6 = (f32[16,16,128]{2,1,0:T(8,128)S(1)}, f32[16,16,128]{2,1,0:T(8,128)S(1)}, u32[]{:S(2)}, u32[]{:S(2)}) collective-permute-start(f32[16,16,128]{2,1,0:T(8,128)S(1)} %slice_select_fusion.2), channel_id=1, source_target_pairs={{0,16},{1,17},{2,18},{3,19},{4,20},{5,21},{6,22},{7,23},{8,24},{9,... | collective-permute-start | bytes 393224 | tf_op jit(solution)/shard_map/gather_swap/ppermute | solution.py:24
  30.9 2.8 %copy-start = (f32[1,1,96,128,128]{4,3,2,1,0:T(8,128)S(1)}, f32[1,1,96,128,128]{4,3,2,1,0:T(8,128)}, u32[]{:S(2)}) copy-start(f32[1,1,96,128,128]{4,3,2,1,0:T(8,128)} %param.6) | copy-start | bytes 18874372
  33.7 5.2 %copy-start.1 = (f32[1,1,96,128,128]{4,3,2,1,0:T(8,128)S(1)}, f32[1,1,96,128,128]{4,3,2,1,0:T(8,128)}, u32[]{:S(2)}) copy-start(f32[1,1,96,128,128]{4,3,2,1,0:T(8,128)} %param.6) | copy-start | bytes 18874372
  37.7 6.1 %collective-permute-start.11 = (f32[16,16,128]{2,1,0:T(8,128)S(1)}, f32[16,16,128]{2,1,0:T(8,128)S(1)}, u32[]{:S(2)}, u32[]{:S(2)}) collective-permute-start(f32[16,16,128]{2,1,0:T(8,128)S(1)} %get-tuple-element.21), channel_id=1, source_target_pairs={{0,16},{1,17},{2,18},{3,19},{4,20},{5,21},{6,22},{7,23},{8,24},{9,... | collective-permute-start | bytes 393224 | tf_op jit(solution)/shard_map/sum_swap/ppermute | solution.py:24
  38.3 5.5 %collective-permute-start.12 = (f32[16,16,128]{2,1,0:T(8,128)S(1)}, f32[16,16,128]{2,1,0:T(8,128)S(1)}, u32[]{:S(2)}, u32[]{:S(2)}) collective-permute-start(f32[16,16,128]{2,1,0:T(8,128)S(1)} %get-tuple-element.22), channel_id=1, source_target_pairs={{0,16},{1,17},{2,18},{3,19},{4,20},{5,21},{6,22},{7,23},{8,24},{9,... | collective-permute-start | bytes 393224 | tf_op jit(solution)/shard_map/sum_swap/ppermute | solution.py:24
  38.4 5.4 %collective-permute-start.13 = (f32[16,16,128]{2,1,0:T(8,128)S(1)}, f32[16,16,128]{2,1,0:T(8,128)S(1)}, u32[]{:S(2)}, u32[]{:S(2)}) collective-permute-start(f32[16,16,128]{2,1,0:T(8,128)S(1)} %get-tuple-element.23), channel_id=1, source_target_pairs={{0,16},{1,17},{2,18},{3,19},{4,20},{5,21},{6,22},{7,23},{8,24},{9,... | collective-permute-start | bytes 393224 | tf_op jit(solution)/shard_map/sum_swap/ppermute | solution.py:24
  38.8 5.0 %collective-permute-start.14 = (f32[16,16,128]{2,1,0:T(8,128)S(1)}, f32[16,16,128]{2,1,0:T(8,128)S(1)}, u32[]{:S(2)}, u32[]{:S(2)}) collective-permute-start(f32[16,16,128]{2,1,0:T(8,128)S(1)} %get-tuple-element.24), channel_id=1, source_target_pairs={{0,16},{1,17},{2,18},{3,19},{4,20},{5,21},{6,22},{7,23},{8,24},{9,... | collective-permute-start | bytes 393224 | tf_op jit(solution)/shard_map/sum_swap/ppermute | solution.py:24
  43.9 9.6 %collective-permute-start.15 = (f32[32,16,128]{2,1,0:T(8,128)S(1)}, f32[32,16,128]{2,1,0:T(8,128)S(1)}, u32[]{:S(2)}, u32[]{:S(2)}) collective-permute-start(f32[32,16,128]{2,1,0:T(8,128)S(1)} %get-tuple-element.26), channel_id=1, source_target_pairs={{0,32},{1,33},{2,34},{3,35},{4,36},{5,37},{6,38},{7,39},{8,40},{9,... | collective-permute-start | bytes 786440 | tf_op jit(solution)/shard_map/sum_side/ppermute | solution.py:24
  44.0 9.5 %collective-permute-start.16 = (f32[32,16,128]{2,1,0:T(8,128)S(1)}, f32[32,16,128]{2,1,0:T(8,128)S(1)}, u32[]{:S(2)}, u32[]{:S(2)}) collective-permute-start(f32[32,16,128]{2,1,0:T(8,128)S(1)} %get-tuple-element.27), channel_id=1, source_target_pairs={{0,64},{1,65},{2,66},{3,67},{4,68},{5,69},{6,70},{7,71},{8,72},{9,... | collective-permute-start | bytes 786440 | tf_op jit(solution)/shard_map/sum_side/ppermute | solution.py:24
  45.1 9.1 %collective-permute-start.17 = (f32[32,16,128]{2,1,0:T(8,128)S(1)}, f32[32,16,128]{2,1,0:T(8,128)S(1)}, u32[]{:S(2)}, u32[]{:S(2)}) collective-permute-start(f32[32,16,128]{2,1,0:T(8,128)S(1)} %get-tuple-element.28), channel_id=1, source_target_pairs={{0,96},{1,97},{2,98},{3,99},{4,100},{5,101},{6,102},{7,103},{8,104... | collective-permute-start | bytes 786440 | tf_op jit(solution)/shard_map/sum_side/ppermute | solution.py:24
  54.3 7.2 %collective-permute-start.18 = (f32[8,16,128]{2,1,0:T(8,128)S(1)}, f32[8,16,128]{2,1,0:T(8,128)S(1)}, u32[]{:S(2)}, u32[]{:S(2)}) collective-permute-start(f32[8,16,128]{2,1,0:T(8,128)S(1)} %get-tuple-element.37), channel_id=1, source_target_pairs={{0,128},{1,129},{2,130},{3,131},{4,132},{5,133},{6,134},{7,135},{8... | collective-permute-start | bytes 196616 | tf_op jit(solution)/shard_map/sum_z/ppermute | solution.py:24
  54.4 7.1 %collective-permute-start.20 = (f32[8,16,128]{2,1,0:T(8,128)S(1)}, f32[8,16,128]{2,1,0:T(8,128)S(1)}, u32[]{:S(2)}, u32[]{:S(2)}) collective-permute-start(f32[8,16,128]{2,1,0:T(8,128)S(1)} %get-tuple-element.38), channel_id=1, source_target_pairs={{16,28},{17,29},{18,30},{19,31},{20,16},{21,17},{22,18},{23,19},{2... | collective-permute-start | bytes 196616 | tf_op jit(solution)/shard_map/sum_z/ppermute | solution.py:24
  59.5 6.1 %collective-permute-start.19 = (f32[8,16,128]{2,1,0:T(8,128)S(1)}, f32[8,16,128]{2,1,0:T(8,128)S(1)}, u32[]{:S(2)}, u32[]{:S(2)}) collective-permute-start(f32[8,16,128]{2,1,0:T(8,128)S(1)} %get-tuple-element.39), channel_id=1, source_target_pairs={{16,24},{17,25},{18,26},{19,27},{20,28},{21,29},{22,30},{23,31},{2... | collective-permute-start | bytes 196616 | tf_op jit(solution)/shard_map/sum_z/ppermute | solution.py:24
  65.6 1.3 %collective-permute-start.21 = (f32[4,16,128]{2,1,0:T(8,128)S(1)}, f32[4,16,128]{2,1,0:T(8,128)S(1)}, u32[]{:S(2)}, u32[]{:S(2)}) collective-permute-start(f32[4,16,128]{2,1,0:T(8,128)S(1)} %slice.70), channel_id=1, source_target_pairs={{0,16},{1,17},{2,18},{3,19},{4,20},{5,21},{6,22},{7,23},{8,24},{9,... | collective-permute-start | bytes 98312 | tf_op jit(solution)/shard_map/sum_core/ppermute | solution.py:24

commit v4 on v1

v4 whole, which is shorter than its diff:
```python
import functools
import jax
import jax.numpy as jnp
from jax import lax
from jax.experimental import pallas as pl
from jax.experimental.pallas import tpu as pltpu
from jax.sharding import PartitionSpec as P

AXIS = 16
GROUP = 4
CHUNK = 8
BF16 = jnp.bfloat16
F32 = jnp.float32
AXES = ("row", "col")
SIDES = (2, 1, 3)
GSIDES = (2, 1, 3)
VECTOR = pl.BlockSpec(memory_space=pltpu.VMEM)
SCALAR = pl.BlockSpec(memory_space=pltpu.SMEM)
ANYWHERE = pl.BlockSpec(memory_space=pl.ANY)


def send(value, row_flips, col_flips):
    pairs = []
    for row in range(AXIS):
        for col in range(AXIS):
            core = row % 2
            there = (row ^ row_flips[core]) * AXIS + (col ^ col_flips[core])
            pairs.append((row * AXIS + col, there))
    return lax.ppermute(value, AXES, pairs)


def to_other_core(value):
    return send(value, (1, 1), (0, 0))


def along_z(value, step, far_step):
    return send(value, (8 if step == far_step else 2, 0), (0, 4 * step))


def along_side(value, step):
    return send(value, (2 * step, 0), (0, step))


def call(kernel, out_shape, in_specs, args, out_specs=None, scratch=(), limit=8, name=None, cost=0, aliases=None):
    return pl.pallas_call(
        kernel,
        out_shape=out_shape,
        in_specs=in_specs,
        out_specs=[VECTOR] * len(out_shape) if out_specs is None else out_specs,
        scratch_shapes=list(scratch),
        input_output_aliases=aliases or {},
        compiler_params=pltpu.CompilerParams(vmem_limit_bytes=limit * 1024 * 1024),
        cost_estimate=pl.CostEstimate(flops=0, bytes_accessed=cost, transcendentals=0),
        name=name,
    )(*args)


def is_core_0():
    return lax.axis_index("row") % 2 == 0


def stage_kernel(tiles, *refs):
    high_out, low_out = refs[-2:]

    def one_chunk(chunk, carry):
        span = pl.ds(chunk * CHUNK, CHUNK)
        tile = tiles[span]
        high = tile.astype(BF16)
        high_out[span] = high
        low_out[span] = (tile - high.astype(F32)).astype(BF16)
        return carry

    lax.fori_loop(0, tiles.shape[0] // CHUNK, one_chunk, 0)


def stage(tiles, after):
    return call(
        stage_kernel,
        [jax.ShapeDtypeStruct(tiles.shape, BF16)] * 2,
        [VECTOR] + [ANYWHERE] * len(after),
        (tiles, *after),
        name="stage",
    )


def plan(key, source, target):
    slots = key.shape[0]
    slot = jnp.arange(slots, dtype=jnp.int32)
    code = jnp.where(key < GROUP, (slot << 16) | (source << 8) | target, 0)
    before = (key[None, :] < key[:, None]) | ((key[None, :] == key[:, None]) & (slot[None, :] < slot[:, None]))
    rank = jnp.sum(before.astype(jnp.int32), axis=1)
    place = jnp.arange(128, dtype=jnp.int32)[:, None]
    ordered = jnp.where(place == rank[None, :], code[None, :], 0)
    below = jnp.where((place >= slots) & (key[None, :] < place - slots), 1, 0)
    return jnp.sum(ordered + below, axis=1).reshape(1, 128)


def plans(blocks, live, rows, cols):
    slots = rows.shape[0]
    row, col = lax.axis_index("row"), lax.axis_index("col")
    row_block, row_col = rows // AXIS, rows % AXIS
    col_block, col_row = cols // AXIS, cols % AXIS
    is_live = jnp.arange(slots, dtype=jnp.int32) < live
    mirror = is_live & (rows * AXIS + row < (col_block * AXIS + col) * AXIS + col_row)
    across, over = col_row ^ row, row_col ^ col
    row_place = (((across >> 1 & 3) * 2 + (across >> 3)) * 2 + (col_row & 1)) * blocks + col_block
    col_place = ((over & 3) * GROUP + (over >> 2)) * blocks + row_block
    even = row % 2 == 0
    first = jnp.where(even, row_place, col_place), jnp.where(even, col_place, row_place)
    second = first[1], first[0]
    first_kept = jnp.where(even, is_live, mirror)
    second_kept = jnp.where(even, mirror, is_live)
    part = GROUP * blocks
    return (
        plan(jnp.where(first_kept, first[0] // part, GROUP), *first),
        plan(jnp.where(second_kept, second[1] // part, GROUP), *second),
    )


def pair_kernel(own, other, out):
    blocks = own.shape[0]
    out[:blocks] = own[...]
    out[blocks:] = other[...]


def lift_kernel(own, out):
    out[...] = own[...]


def place_kernel(rows, cols, after, rows_out, cols_out):
    rows_out[...] = rows[...]
    cols_out[...] = cols[...]


def column_kernel(*refs):
    parts, out = refs[:GROUP], refs[-1]
    count = parts[0].shape[0]
    blocks = count // 2

    @pl.when(is_core_0())
    def _():
        for index in range(2):
            out[index * count : (index + 1) * count] = parts[index * 3][...]
        out[2 * count :] = jnp.zeros((2 * count,) + out.shape[1:], out.dtype)

    @pl.when(jnp.logical_not(is_core_0()))
    def _():
        for index, part in enumerate(parts):
            out[index * blocks : (index + 1) * blocks] = part[blocks:]
            out[2 * count + index * blocks : 2 * count + (index + 1) * blocks] = part[:blocks]


def put(split, place, values):
    vecs, edge = values.shape[1:]
    high = values.astype(BF16)
    low = (values - high.astype(F32)).astype(BF16)
    span = slice(place, place + values.shape[0])
    split[span, :vecs, :edge] = high
    split[span, :vecs, edge:] = high
    split[span, vecs:, :edge] = low
    split[span, vecs:, edge:] = low


def add_slots(transposed, bucket, plan, staged, split, total, source_mask, target_mask):
    slots = staged[0].shape[0]
    vecs = total.shape[1]
    start, end = plan[0, slots + bucket], plan[0, slots + bucket + 1]

    def one_slot(place):
        code = plan[0, place]
        slot = code >> 16
        both = jnp.concatenate([staged[0][slot], staged[1][slot]], axis=0 if transposed else 1)
        product = lax.dot_general(
            split[(code >> 8) & source_mask],
            both,
            (((1,), (0 if transposed else 1,)), ((), ())),
            preferred_element_type=F32,
        )
        target = jnp.where(place < end, code & target_mask, target_mask + 1)
        total[target] += product[:vecs] + product[vecs:]

    def one_chunk(chunk, carry):
        for step in range(CHUNK):
            one_slot(start + chunk * CHUNK + step)
        return carry

    lax.fori_loop(0, (end - start + CHUNK - 1) // CHUNK, one_chunk, 0)


def first_kernel(bucket, begin, plan, high, low, part, *refs):
    total, give, split = refs[-3:]
    count = part.shape[0] // 2
    give[...] = part[:count]
    if begin:
        total[...] = jnp.zeros_like(total)

    @pl.when(is_core_0())
    def _():
        put(split, 0, part[:count])
        add_slots(False, bucket, plan, (high, low), split, total, count - 1, GROUP * count - 1)

    @pl.when(jnp.logical_not(is_core_0()))
    def _():
        put(split, 0, part[count:])
        add_slots(True, bucket, plan, (high, low), split, total, count - 1, GROUP * count - 1)


def first(bucket, plan, staged, part, total, after):
    count, vecs, edge = part.shape[0] // 2, part.shape[1], part.shape[2]
    shape = jax.ShapeDtypeStruct((GROUP * count + 8, vecs, edge), F32)
    begin = total is None
    return call(
        functools.partial(first_kernel, bucket, begin),
        [shape, jax.ShapeDtypeStruct((count, vecs, edge), F32)],
        [SCALAR] + [VECTOR] * (3 if begin else 4) + [ANYWHERE] * len(after),
        (plan, *staged, part, *(() if begin else (total,)), *after),
        scratch=[pltpu.VMEM((count, 2 * vecs, 2 * edge), BF16)],
        aliases=None if begin else {4: 0},
        name="first",
        cost=8 << 20,
    )


def split_kernel(place, part, *refs):
    put(refs[-1], place, part[...])


def split_in(place, part, whole):
    count, vecs, edge = part.shape
    return call(
        functools.partial(split_kernel, place),
        [jax.ShapeDtypeStruct((GROUP * count, 2 * vecs, 2 * edge), BF16)],
        [VECTOR] * (1 + len(whole)),
        (part, *whole),
        aliases={1: 0} if whole else None,
        name="split",
        cost=8 << 20,
    )


def second_kernel(bucket, plan, high, low, split, got, *refs):
    out, total = refs[-2:]
    count = got.shape[0]
    blocks = count // GROUP
    total[...] = jnp.zeros_like(total)

    @pl.when(is_core_0())
    def _():
        add_slots(True, bucket, plan, (high, low), split, total, GROUP * count - 1, count - 1)
        out[:count] = total[:count] + got[...]
        out[count:] = jnp.zeros_like(got)

    @pl.when(jnp.logical_not(is_core_0()))
    def _():
        add_slots(False, bucket, plan, (high, low), split, total, GROUP * count - 1, count - 1)
        for step in range(GROUP):
            span = slice(step * blocks, (step + 1) * blocks)
            low_end = 2 * step * blocks
            out[low_end : low_end + blocks] = total[span]
            out[low_end + blocks : low_end + 2 * blocks] = got[span]


def second(bucket, plan, staged, split, got, after):
    count, vecs, edge = got.shape
    return call(
        functools.partial(second_kernel, bucket),
        [jax.ShapeDtypeStruct((2 * count, vecs, edge), F32)],
        [SCALAR] + [VECTOR] * 4 + [ANYWHERE] * len(after),
        (plan, *staged, split, got, *after),
        scratch=[pltpu.VMEM((count + 8, vecs, edge), F32)],
        name="second",
        cost=8 << 20,
    )[0]


def add_kernel(one, two, out):
    out[...] = one[...] + two[...]


def add(one, two):
    return call(add_kernel, [jax.ShapeDtypeStruct(one.shape, F32)], [VECTOR] * 2, (one, two), name="add", cost=8 << 20)[0]


def shards(vectors, tiles, tile_rows, tile_cols, counts):
    blocks = vectors.shape[0]
    vecs, edge = vectors.shape[3], vectors.shape[4]
    slots = tiles.shape[2]
    block_of = lambda count: jax.ShapeDtypeStruct((count * blocks, vecs, edge), F32)
    own = vectors.reshape(blocks, vecs, edge)
    (here,) = call(lift_kernel, [block_of(1)], [VECTOR], (own,), name="lift")
    with jax.named_scope("gather_core"):
        (pair,) = call(
            pair_kernel, [block_of(2)], [VECTOR] * 2, (here, to_other_core(own)), name="pair", cost=0
        )
    with jax.named_scope("gather_z"):
        far = [along_z(pair, step, 3) for step in (1, 2, 3)]
    staged = stage(tiles.reshape(slots, edge, edge), (pair,))
    with jax.named_scope("gather_side"):
        (column,) = call(
            column_kernel,
            [block_of(8)],
            [VECTOR] * GROUP + [ANYWHERE],
            (pair, *far, staged[0]),
            name="column",
        )
        held = {0: column}
        for step in GSIDES:
            held[step] = along_side(column, step)
    rows, cols = call(
        place_kernel,
        [jax.ShapeDtypeStruct((1, slots), jnp.int32)] * 2,
        [VECTOR] * 2 + [ANYWHERE],
        (tile_rows.reshape(1, slots), tile_cols.reshape(1, slots), column),
        name="places",
    )
    first_plan, second_plan = plans(blocks, counts.reshape(1), rows.reshape(slots), cols.reshape(slots))
    part = GROUP * blocks
    total, split, swapped = None, [], []
    for index, step in enumerate((0,) + GSIDES):
        if index >= 2:
            split = split_in(*swapped[index - 2], split)
        total, gift = first(step, first_plan, staged, held[step], total, split)
        with jax.named_scope("gather_swap"):
            swapped.append((step * part, to_other_core(gift)))
    for done in swapped[-2:]:
        split = split_in(*done, split)
    (split,) = split
    with jax.named_scope("sum_swap"):
        got = {step: to_other_core(total[step * part : (step + 1) * part]) for step in SIDES + (0,)}
    merged, after = {}, ()
    for step in SIDES + (0,):
        merged[step] = second(step, second_plan, staged, split, got[step], after)
        after = (merged[step],)
    with jax.named_scope("sum_side"):
        column = merged[0]
        for step in SIDES:
            column = add(column, along_side(merged[step], step))
    with jax.named_scope("sum_z"):
        column = column.reshape(GROUP, 2 * blocks, vecs, edge)
        pair = column[0]
        for step in (1, 2, 3):
            pair = pair + along_z(column[step], step, 1)
    with jax.named_scope("sum_core"):
        result = pair[:blocks] + to_other_core(pair[blocks:])
    return result.reshape(blocks, 1, 1, vecs, edge)


def solution(mesh):
    in_specs = (
        P(None, "col", "row", None, None),
        P("row", "col", None, None, None),
        P("row", "col", None),
        P("row", "col", None),
        P("row", "col"),
    )
    out_specs = P(None, "col", "row", None, None)
    return jax.shard_map(shards, mesh=mesh, in_specs=in_specs, out_specs=out_specs, check_vma=False)
```

time: 99.3 us -> 56.9 us (0.57)
  the two profiles are of different devices: /device:TPU:32 before, /device:TPU:1 now
where the time goes in v4:
time: 56.9 us; the launch traced here: 56.7 us
  starting transfers between devices  32 us (56%)
  waiting for transfers between devices  9.74 us (17%)
  Pallas kernels  9.3 us (16%)
  local copies, waits for them, and re-layouts  3.61 us (6%)
  other arithmetic  1.07 us (2%)
  between operations  0.91 us (2%)
    ppermute x22, starting transfers between devices, send(): return lax.ppermute(value, AXES, pairs)  32 us
    ppermute x22, waiting for transfers between devices, send(): return lax.ppermute(value, AXES, pairs)  9.74 us
    pallas_call x20, Pallas kernels, call(): pl.pallas_call(kernel, out_shape=out_shape, in_specs=in_specs, out_specs=...  9.3 us
    unnamed x8, local copies, waits for them, and re-layouts  3.55 us
  transfers between devices with their start and end apart: 22, of which 7 were waited for; matrix products, arithmetic and copies ran while one was open for 1% of the time, Pallas kernels for 16%

profile of v4, /device:TPU:1, one launch (start us, length us, event | category | flops | bytes accessed | tf_op | source)
XLA Modules:
  0.0 56.7 jit_solution(391769943348612195)
XLA Ops:
  0.0 3.2 %collective-permute-start = (f32[4,16,128]{2,1,0:T(8,128)}, f32[4,16,128]{2,1,0:T(8,128)S(1)}, u32[]{:S(2)}, u32[]{:S(2)}) collective-permute-start(f32[4,16,128]{2,1,0:T(8,128)} %bitcast.61), channel_id=1, source_target_pairs={{0,16},{1,17},{2,18},{3,19},{4,20},{5,21},{6,22},{7,23},{8,24},{9,... | collective-permute-start | bytes 98312 | tf_op jit(solution)/shard_map/gather_core/ppermute | solution.py:29
  3.2 0.8 %copy-done.1 = f32[4,1,1,16,128]{4,3,2,1,0:T(8,128)S(1)} copy-done((f32[4,1,1,16,128]{4,3,2,1,0:T(8,128)S(1)}, f32[4,1,1,16,128]{4,3,2,1,0:T(8,128)}, u32[]{:S(2)}) %copy-start.1) | copy-done | bytes 32792
  4.7 2.7 %collective-permute-start.3 = (f32[8,16,128]{2,1,0:T(8,128)S(1)}, f32[8,16,128]{2,1,0:T(8,128)S(1)}, u32[]{:S(2)}, u32[]{:S(2)}) collective-permute-start(f32[8,16,128]{2,1,0:T(8,128)S(1)} %pair.1.refs_0_), channel_id=1, source_target_pairs={{0,128},{1,129},{2,130},{3,131},{4,132},{5,133},{6,134},{7,135},{8... | collective-permute-start | bytes 196616 | tf_op jit(solution)/shard_map/gather_z/ppermute | solution.py:29
  7.4 0.9 %collective-permute-start.1 = (f32[8,16,128]{2,1,0:T(8,128)S(1)}, f32[8,16,128]{2,1,0:T(8,128)S(1)}, u32[]{:S(2)}, u32[]{:S(2)}) collective-permute-start(f32[8,16,128]{2,1,0:T(8,128)S(1)} %pair.1.refs_0_), channel_id=1, source_target_pairs={{0,32},{1,33},{2,34},{3,35},{4,36},{5,37},{6,38},{7,39},{8,40},{9,... | collective-permute-start | bytes 196616 | tf_op jit(solution)/shard_map/gather_z/ppermute | solution.py:29
  8.3 2.8 %copy-done = f32[1,1,96,128,128]{4,3,2,1,0:T(8,128)S(1)} copy-done((f32[1,1,96,128,128]{4,3,2,1,0:T(8,128)S(1)}, f32[1,1,96,128,128]{4,3,2,1,0:T(8,128)}, u32[]{:S(2)}) %copy-start) | copy-done | bytes 6291480
  11.1 0.9 %stage.1 = (bf16[96,128,128]{2,1,0:T(8,128)(2,1)S(1)}, bf16[96,128,128]{2,1,0:T(8,128)(2,1)S(1)}) custom-call(f32[96,128,128]{2,1,0:T(8,128)S(1)} %bitcast.60, f32[8,16,128]{2,1,0:T(8,128)S(1)} %pair.1.refs_0_), custom_call_target="tpu_custom_call" | custom-call | tf_op jit(solution)/shard_map/stage/pallas_call | solution.py:45
  12.1 2.4 %collective-permute-start.6 = (f32[32,16,128]{2,1,0:T(8,128)S(1)}, f32[32,16,128]{2,1,0:T(8,128)S(1)}, u32[]{:S(2)}, u32[]{:S(2)}) collective-permute-start(f32[32,16,128]{2,1,0:T(8,128)S(1)} %column.1.after.part), channel_id=1, source_target_pairs={{0,64},{1,65},{2,66},{3,67},{4,68},{5,69},{6,70},{7,71},{8,72},{9,... | collective-permute-start | bytes 786440 | tf_op jit(solution)/shard_map/gather_side/ppermute | solution.py:29
  14.9 0.6 %collective-permute-start.4 = (f32[32,16,128]{2,1,0:T(8,128)S(1)}, f32[32,16,128]{2,1,0:T(8,128)S(1)}, u32[]{:S(2)}, u32[]{:S(2)}) collective-permute-start(f32[32,16,128]{2,1,0:T(8,128)S(1)} %column.1.after.part), channel_id=1, source_target_pairs={{0,96},{1,97},{2,98},{3,99},{4,100},{5,101},{6,102},{7,103},{8,104... | collective-permute-start | bytes 786440 | tf_op jit(solution)/shard_map/gather_side/ppermute | solution.py:29
  15.9 1.3 %first.4 = (f32[72,16,128]{2,1,0:T(8,128)S(1)}, f32[16,16,128]{2,1,0:T(8,128)S(1)}) custom-call(s32[1,128]{1,0:T(1,128)S(1)} %bitcast.67, bf16[96,128,128]{2,1,0:T(8,128)(2,1)S(1)} %get-tuple-element.17.refs_4_.high, bf16[96,128,128]{2,1,0:T(8,128)(2,1)S(1)} %get-tuple-element.20.low, f32[32,16,128]{2,1,0:T(8,128)S(1)} %column.1.after.part), custom_call_target="tpu_custom_call" | custom-call | bytes 8388608 | tf_op jit(solution)/shard_map/first/pallas_call | solution.py:45
  17.2 4.6 %collective-permute-start.7 = (f32[16,16,128]{2,1,0:T(8,128)S(1)}, f32[16,16,128]{2,1,0:T(8,128)S(1)}, u32[]{:S(2)}, u32[]{:S(2)}) collective-permute-start(f32[16,16,128]{2,1,0:T(8,128)S(1)} %get-tuple-element.23), channel_id=1, source_target_pairs={{0,16},{1,17},{2,18},{3,19},{4,20},{5,21},{6,22},{7,23},{8,24},{9,... | collective-permute-start | bytes 393224 | tf_op jit(solution)/shard_map/gather_swap/ppermute | solution.py:29
  21.9 0.8 %first.5 = (f32[72,16,128]{2,1,0:T(8,128)S(1)}, f32[16,16,128]{2,1,0:T(8,128)S(1)}) custom-call(s32[1,128]{1,0:T(1,128)S(1)} %bitcast.68, bf16[96,128,128]{2,1,0:T(8,128)(2,1)S(1)} %get-tuple-element.17.refs_4_.high, bf16[96,128,128]{2,1,0:T(8,128)(2,1)S(1)} %get-tuple-element.20.low, ...), custom_call_target="tpu_custom_call", output_to_operand_aliasing={{0}: (4, {})} | custom-call | bytes 8388608 | tf_op jit(solution)/shard_map/first/pallas_call | solution.py:45
  22.7 2.3 %collective-permute-start.8 = (f32[16,16,128]{2,1,0:T(8,128)S(1)}, f32[16,16,128]{2,1,0:T(8,128)S(1)}, u32[]{:S(2)}, u32[]{:S(2)}) collective-permute-start(f32[16,16,128]{2,1,0:T(8,128)S(1)} %get-tuple-element.25), channel_id=1, source_target_pairs={{0,16},{1,17},{2,18},{3,19},{4,20},{5,21},{6,22},{7,23},{8,24},{9,... | collective-permute-start | bytes 393224 | tf_op jit(solution)/shard_map/gather_swap/ppermute | solution.py:29
  25.1 0.8 %first.6 = (f32[72,16,128]{2,1,0:T(8,128)S(1)}, f32[16,16,128]{2,1,0:T(8,128)S(1)}) custom-call(s32[1,128]{1,0:T(1,128)S(1)} %bitcast.69, bf16[96,128,128]{2,1,0:T(8,128)(2,1)S(1)} %get-tuple-element.17.refs_4_.high, bf16[96,128,128]{2,1,0:T(8,128)(2,1)S(1)} %get-tuple-element.20.low, ...), custom_call_target="tpu_custom_call", output_to_operand_aliasing={{0}: (4, {})} | custom-call | bytes 8388608 | tf_op jit(solution)/shard_map/first/pallas_call | solution.py:45
  25.9 2.3 %collective-permute-start.10 = (f32[16,16,128]{2,1,0:T(8,128)S(1)}, f32[16,16,128]{2,1,0:T(8,128)S(1)}, u32[]{:S(2)}, u32[]{:S(2)}) collective-permute-start(f32[16,16,128]{2,1,0:T(8,128)S(1)} %get-tuple-element.27), channel_id=1, source_target_pairs={{0,16},{1,17},{2,18},{3,19},{4,20},{5,21},{6,22},{7,23},{8,24},{9,... | collective-permute-start | bytes 393224 | tf_op jit(solution)/shard_map/gather_swap/ppermute | solution.py:29
  28.3 0.8 %first.7 = (f32[72,16,128]{2,1,0:T(8,128)S(1)}, f32[16,16,128]{2,1,0:T(8,128)S(1)}) custom-call(s32[1,128]{1,0:T(1,128)S(1)} %bitcast.70, bf16[96,128,128]{2,1,0:T(8,128)(2,1)S(1)} %get-tuple-element.17.refs_4_.high, bf16[96,128,128]{2,1,0:T(8,128)(2,1)S(1)} %get-tuple-element.20.low, ...), custom_call_target="tpu_custom_call", output_to_operand_aliasing={{0}: (4, {})} | custom-call | bytes 8388608 | tf_op jit(solution)/shard_map/first/pallas_call | solution.py:45
  29.3 0.5 collective-permute-start.14
  30.8 0.9 %second.4.refs_0_ = f32[32,16,128]{2,1,0:T(8,128)S(1)} custom-call(s32[1,128]{1,0:T(1,128)S(1)} %bitcast.63, bf16[96,128,128]{2,1,0:T(8,128)(2,1)S(1)} %get-tuple-element.17.refs_4_.high, bf16[96,128,128]{2,1,0:T(8,128)(2,1)S(1)} %get-tuple-element.20.low, bf16[64,32,256]{2,1,0:T(8,128)(2,1)S(1)} %split.7, f32[16,16,128]{2,1,0:T(8,128)S(1)} %collective-permute-done.14.got), custom_call_target="tpu_custom_call" | custom-call | bytes 8388608 | tf_op jit(solution)/shard_map/second/pallas_call | solution.py:45
  31.7 4.1 %collective-permute-start.15 = (f32[32,16,128]{2,1,0:T(8,128)S(1)}, f32[32,16,128]{2,1,0:T(8,128)S(1)}, u32[]{:S(2)}, u32[]{:S(2)}) collective-permute-start(f32[32,16,128]{2,1,0:T(8,128)S(1)} %second.4.refs_0_), channel_id=1, source_target_pairs={{0,64},{1,65},{2,66},{3,67},{4,68},{5,69},{6,70},{7,71},{8,72},{9,... | collective-permute-start | bytes 786440 | tf_op jit(solution)/shard_map/sum_side/ppermute | solution.py:29
  35.8 0.9 %second.5.refs_0_ = f32[32,16,128]{2,1,0:T(8,128)S(1)} custom-call(s32[1,128]{1,0:T(1,128)S(1)} %bitcast.64, bf16[96,128,128]{2,1,0:T(8,128)(2,1)S(1)} %get-tuple-element.17.refs_4_.high, bf16[96,128,128]{2,1,0:T(8,128)(2,1)S(1)} %get-tuple-element.20.low, bf16[64,32,256]{2,1,0:T(8,128)(2,1)S(1)} %split.7, f32[16,16,128]{2,1,0:T(8,128)S(1)} %collective-permute-done.13.got, ...), custom_call_target="tpu_custom_call" | custom-call | bytes 8388608 | tf_op jit(solution)/shard_map/second/pallas_call | solution.py:45
  36.7 0.5 collective-permute-start.16
  37.2 1.1 %second.6.refs_0_ = f32[32,16,128]{2,1,0:T(8,128)S(1)} custom-call(s32[1,128]{1,0:T(1,128)S(1)} %bitcast.65, bf16[96,128,128]{2,1,0:T(8,128)(2,1)S(1)} %get-tuple-element.17.refs_4_.high, bf16[96,128,128]{2,1,0:T(8,128)(2,1)S(1)} %get-tuple-element.20.low, bf16[64,32,256]{2,1,0:T(8,128)(2,1)S(1)} %split.7, f32[16,16,128]{2,1,0:T(8,128)S(1)} %collective-permute-done.12.got, ...), custom_call_target="tpu_custom_call" | custom-call | bytes 8388608 | tf_op jit(solution)/shard_map/second/pallas_call | solution.py:45
  38.7 1.3 %collective-permute-start.11 = (f32[16,16,128]{2,1,0:T(8,128)S(1)}, f32[16,16,128]{2,1,0:T(8,128)S(1)}, u32[]{:S(2)}, u32[]{:S(2)}) collective-permute-start(f32[16,16,128]{2,1,0:T(8,128)S(1)} %get-tuple-element.46), channel_id=1, source_target_pairs={{0,16},{1,17},{2,18},{3,19},{4,20},{5,21},{6,22},{7,23},{8,24},{9,... | collective-permute-start | bytes 393224 | tf_op jit(solution)/shard_map/sum_swap/ppermute | solution.py:29
  39.9 1.0 %collective-permute-done.11.got = f32[16,16,128]{2,1,0:T(8,128)S(1)} collective-permute-done((f32[16,16,128]{2,1,0:T(8,128)S(1)}, f32[16,16,128]{2,1,0:T(8,128)S(1)}, u32[]{:S(2)}, u32[]{:S(2)}) %collective-permute-start.11) | collective-permute-done | bytes 131104 | tf_op jit(solution)/shard_map/sum_swap/ppermute | solution.py:29
  40.9 1.5 %second.7.one = f32[32,16,128]{2,1,0:T(8,128)S(1)} custom-call(s32[1,128]{1,0:T(1,128)S(1)} %bitcast.66, bf16[96,128,128]{2,1,0:T(8,128)(2,1)S(1)} %get-tuple-element.17.refs_4_.high, bf16[96,128,128]{2,1,0:T(8,128)(2,1)S(1)} %get-tuple-element.20.low, bf16[64,32,256]{2,1,0:T(8,128)(2,1)S(1)} %split.7, f32[16,16,128]{2,1,0:T(8,128)S(1)} %collective-permute-done.11.got, ...), custom_call_target="tpu_custom_call" | custom-call | bytes 8388608 | tf_op jit(solution)/shard_map/second/pallas_call | solution.py:45
  42.5 2.4 %collective-permute-done.17.two = f32[32,16,128]{2,1,0:T(8,128)S(1)} collective-permute-done((f32[32,16,128]{2,1,0:T(8,128)S(1)}, f32[32,16,128]{2,1,0:T(8,128)S(1)}, u32[]{:S(2)}, u32[]{:S(2)}) %collective-permute-start.17) | collective-permute-done | bytes 262176 | tf_op jit(solution)/shard_map/sum_side/ppermute | solution.py:29
  44.9 1.0 %collective-permute-start.18 = (f32[8,16,128]{2,1,0:T(8,128)S(1)}, f32[8,16,128]{2,1,0:T(8,128)S(1)}, u32[]{:S(2)}, u32[]{:S(2)}) collective-permute-start(f32[8,16,128]{2,1,0:T(8,128)S(1)} %get-tuple-element.47), channel_id=1, source_target_pairs={{0,128},{1,129},{2,130},{3,131},{4,132},{5,133},{6,134},{7,135},{8... | collective-permute-start | bytes 196616 | tf_op jit(solution)/shard_map/sum_z/ppermute | solution.py:29
  45.9 2.3 %collective-permute-start.20 = (f32[8,16,128]{2,1,0:T(8,128)S(1)}, f32[8,16,128]{2,1,0:T(8,128)S(1)}, u32[]{:S(2)}, u32[]{:S(2)}) collective-permute-start(f32[8,16,128]{2,1,0:T(8,128)S(1)} %get-tuple-element.48), channel_id=1, source_target_pairs={{0,32},{1,33},{2,34},{3,35},{4,36},{5,37},{6,38},{7,39},{8,40},{9,... | collective-permute-start | bytes 196616 | tf_op jit(solution)/shard_map/sum_z/ppermute | solution.py:29
  48.2 3.2 %collective-permute-done.20 = f32[8,16,128]{2,1,0:T(8,128)S(1)} collective-permute-done((f32[8,16,128]{2,1,0:T(8,128)S(1)}, f32[8,16,128]{2,1,0:T(8,128)S(1)}, u32[]{:S(2)}, u32[]{:S(2)}) %collective-permute-start.20) | collective-permute-done | bytes 65568 | tf_op jit(solution)/shard_map/sum_z/ppermute | solution.py:29
  51.4 1.9 %collective-permute-done.19 = f32[8,16,128]{2,1,0:T(8,128)S(1)} collective-permute-done((f32[8,16,128]{2,1,0:T(8,128)S(1)}, f32[8,16,128]{2,1,0:T(8,128)S(1)}, u32[]{:S(2)}, u32[]{:S(2)}) %collective-permute-start.19) | collective-permute-done | bytes 65568 | tf_op jit(solution)/shard_map/sum_z/ppermute | solution.py:29
  53.3 1.9 %collective-permute-start.21 = (f32[4,16,128]{2,1,0:T(8,128)S(1)}, f32[4,16,128]{2,1,0:T(8,128)S(1)}, u32[]{:S(2)}, u32[]{:S(2)}) collective-permute-start(f32[4,16,128]{2,1,0:T(8,128)S(1)} %slice.49), channel_id=1, source_target_pairs={{0,16},{1,17},{2,18},{3,19},{4,20},{5,21},{6,22},{7,23},{8,24},{9,... | collective-permute-start | bytes 98312 | tf_op jit(solution)/shard_map/sum_core/ppermute | solution.py:29
  55.2 0.9 %collective-permute-done.21 = f32[4,16,128]{2,1,0:T(8,128)S(1)} collective-permute-done((f32[4,16,128]{2,1,0:T(8,128)S(1)}, f32[4,16,128]{2,1,0:T(8,128)S(1)}, u32[]{:S(2)}, u32[]{:S(2)}) %collective-permute-start.21) | collective-permute-done | bytes 32800 | tf_op jit(solution)/shard_map/sum_core/ppermute | solution.py:29
  56.1 0.6 %fusion.6 = f32[4,1,1,16,128]{4,3,2,1,0:T(8,128)} fusion(f32[4,16,128]{2,1,0:T(8,128)S(1)} %collective-permute-done.21, f32[8,16,128]{2,1,0:T(8,128)S(1)} %fusion.1), kind=kLoop, calls=%fused_computation.15 | loop fusion | flops 8192 | bytes 98304 | tf_op jit(solution)/shard_map/reshape | solution.py:345
  (53 shorter events, 2.6 us)
Async XLA Ops:
  0.0 4.7 %collective-permute-start = (f32[4,16,128]{2,1,0:T(8,128)}, f32[4,16,128]{2,1,0:T(8,128)S(1)}, u32[]{:S(2)}, u32[]{:S(2)}) collective-permute-start(f32[4,16,128]{2,1,0:T(8,128)} %bitcast.61), channel_id=1, source_target_pairs={{0,16},{1,17},{2,18},{3,19},{4,20},{5,21},{6,22},{7,23},{8,24},{9,... | collective-permute-start | bytes 98312 | tf_op jit(solution)/shard_map/gather_core/ppermute | solution.py:29
  3.2 0.8 %copy-start.1 = (f32[4,1,1,16,128]{4,3,2,1,0:T(8,128)S(1)}, f32[4,1,1,16,128]{4,3,2,1,0:T(8,128)}, u32[]{:S(2)}) copy-start(f32[4,1,1,16,128]{4,3,2,1,0:T(8,128)} %param.5) | copy-start | bytes 98308
  4.7 7.4 %collective-permute-start.3 = (f32[8,16,128]{2,1,0:T(8,128)S(1)}, f32[8,16,128]{2,1,0:T(8,128)S(1)}, u32[]{:S(2)}, u32[]{:S(2)}) collective-permute-start(f32[8,16,128]{2,1,0:T(8,128)S(1)} %pair.1.refs_0_), channel_id=1, source_target_pairs={{0,128},{1,129},{2,130},{3,131},{4,132},{5,133},{6,134},{7,135},{8... | collective-permute-start | bytes 196616 | tf_op jit(solution)/shard_map/gather_z/ppermute | solution.py:29
  7.4 4.7 %collective-permute-start.2 = (f32[8,16,128]{2,1,0:T(8,128)S(1)}, f32[8,16,128]{2,1,0:T(8,128)S(1)}, u32[]{:S(2)}, u32[]{:S(2)}) collective-permute-start(f32[8,16,128]{2,1,0:T(8,128)S(1)} %pair.1.refs_0_), channel_id=1, source_target_pairs={{0,32},{1,33},{2,34},{3,35},{4,36},{5,37},{6,38},{7,39},{8,40},{9,... | collective-permute-start | bytes 196616 | tf_op jit(solution)/shard_map/gather_z/ppermute | solution.py:29
  7.4 4.7 %collective-permute-start.1 = (f32[8,16,128]{2,1,0:T(8,128)S(1)}, f32[8,16,128]{2,1,0:T(8,128)S(1)}, u32[]{:S(2)}, u32[]{:S(2)}) collective-permute-start(f32[8,16,128]{2,1,0:T(8,128)S(1)} %pair.1.refs_0_), channel_id=1, source_target_pairs={{0,32},{1,33},{2,34},{3,35},{4,36},{5,37},{6,38},{7,39},{8,40},{9,... | collective-permute-start | bytes 196616 | tf_op jit(solution)/shard_map/gather_z/ppermute | solution.py:29
  8.3 2.8 %copy-start = (f32[1,1,96,128,128]{4,3,2,1,0:T(8,128)S(1)}, f32[1,1,96,128,128]{4,3,2,1,0:T(8,128)}, u32[]{:S(2)}) copy-start(f32[1,1,96,128,128]{4,3,2,1,0:T(8,128)} %param.6) | copy-start | bytes 18874372
  12.0 3.4 %copy-start.2 = (s32[1,1,96]{2,1,0:T(1,128)S(1)}, s32[1,1,96]{2,1,0:T(1,128)}, u32[]{:S(2)}) copy-start(s32[1,1,96]{2,1,0:T(1,128)} %param.7) | copy-start | bytes 1156
  12.0 3.4 %copy-start.3 = (s32[1,1,96]{2,1,0:T(1,128)S(1)}, s32[1,1,96]{2,1,0:T(1,128)}, u32[]{:S(2)}) copy-start(s32[1,1,96]{2,1,0:T(1,128)} %param.8) | copy-start | bytes 1156
  12.1 9.8 %collective-permute-start.6 = (f32[32,16,128]{2,1,0:T(8,128)S(1)}, f32[32,16,128]{2,1,0:T(8,128)S(1)}, u32[]{:S(2)}, u32[]{:S(2)}) collective-permute-start(f32[32,16,128]{2,1,0:T(8,128)S(1)} %column.1.after.part), channel_id=1, source_target_pairs={{0,64},{1,65},{2,66},{3,67},{4,68},{5,69},{6,70},{7,71},{8,72},{9,... | collective-permute-start | bytes 786440 | tf_op jit(solution)/shard_map/gather_side/ppermute | solution.py:29
  14.6 10.5 %collective-permute-start.5 = (f32[32,16,128]{2,1,0:T(8,128)S(1)}, f32[32,16,128]{2,1,0:T(8,128)S(1)}, u32[]{:S(2)}, u32[]{:S(2)}) collective-permute-start(f32[32,16,128]{2,1,0:T(8,128)S(1)} %column.1.after.part), channel_id=1, source_target_pairs={{0,32},{1,33},{2,34},{3,35},{4,36},{5,37},{6,38},{7,39},{8,40},{9,... | collective-permute-start | bytes 786440 | tf_op jit(solution)/shard_map/gather_side/ppermute | solution.py:29
  14.9 13.4 %collective-permute-start.4 = (f32[32,16,128]{2,1,0:T(8,128)S(1)}, f32[32,16,128]{2,1,0:T(8,128)S(1)}, u32[]{:S(2)}, u32[]{:S(2)}) collective-permute-start(f32[32,16,128]{2,1,0:T(8,128)S(1)} %column.1.after.part), channel_id=1, source_target_pairs={{0,96},{1,97},{2,98},{3,99},{4,100},{5,101},{6,102},{7,103},{8,104... | collective-permute-start | bytes 786440 | tf_op jit(solution)/shard_map/gather_side/ppermute | solution.py:29
  17.2 7.8 %collective-permute-start.7 = (f32[16,16,128]{2,1,0:T(8,128)S(1)}, f32[16,16,128]{2,1,0:T(8,128)S(1)}, u32[]{:S(2)}, u32[]{:S(2)}) collective-permute-start(f32[16,16,128]{2,1,0:T(8,128)S(1)} %get-tuple-element.23), channel_id=1, source_target_pairs={{0,16},{1,17},{2,18},{3,19},{4,20},{5,21},{6,22},{7,23},{8,24},{9,... | collective-permute-start | bytes 393224 | tf_op jit(solution)/shard_map/gather_swap/ppermute | solution.py:29
  22.7 5.5 %collective-permute-start.8 = (f32[16,16,128]{2,1,0:T(8,128)S(1)}, f32[16,16,128]{2,1,0:T(8,128)S(1)}, u32[]{:S(2)}, u32[]{:S(2)}) collective-permute-start(f32[16,16,128]{2,1,0:T(8,128)S(1)} %get-tuple-element.25), channel_id=1, source_target_pairs={{0,16},{1,17},{2,18},{3,19},{4,20},{5,21},{6,22},{7,23},{8,24},{9,... | collective-permute-start | bytes 393224 | tf_op jit(solution)/shard_map/gather_swap/ppermute | solution.py:29
  25.9 4.4 %collective-permute-start.10 = (f32[16,16,128]{2,1,0:T(8,128)S(1)}, f32[16,16,128]{2,1,0:T(8,128)S(1)}, u32[]{:S(2)}, u32[]{:S(2)}) collective-permute-start(f32[16,16,128]{2,1,0:T(8,128)S(1)} %get-tuple-element.27), channel_id=1, source_target_pairs={{0,16},{1,17},{2,18},{3,19},{4,20},{5,21},{6,22},{7,23},{8,24},{9,... | collective-permute-start | bytes 393224 | tf_op jit(solution)/shard_map/gather_swap/ppermute | solution.py:29
  29.1 1.4 %collective-permute-start.9 = (f32[16,16,128]{2,1,0:T(8,128)S(1)}, f32[16,16,128]{2,1,0:T(8,128)S(1)}, u32[]{:S(2)}, u32[]{:S(2)}) collective-permute-start(f32[16,16,128]{2,1,0:T(8,128)S(1)} %get-tuple-element.26), channel_id=1, source_target_pairs={{0,16},{1,17},{2,18},{3,19},{4,20},{5,21},{6,22},{7,23},{8,24},{9,... | collective-permute-start | bytes 393224 | tf_op jit(solution)/shard_map/gather_swap/ppermute | solution.py:29
  29.3 1.5 %collective-permute-start.14 = (f32[16,16,128]{2,1,0:T(8,128)S(1)}, f32[16,16,128]{2,1,0:T(8,128)S(1)}, u32[]{:S(2)}, u32[]{:S(2)}) collective-permute-start(f32[16,16,128]{2,1,0:T(8,128)S(1)} %get-tuple-element.43), channel_id=1, source_target_pairs={{0,16},{1,17},{2,18},{3,19},{4,20},{5,21},{6,22},{7,23},{8,24},{9,... | collective-permute-start | bytes 393224 | tf_op jit(solution)/shard_map/sum_swap/ppermute | solution.py:29
  29.8 6.0 %collective-permute-start.13 = (f32[16,16,128]{2,1,0:T(8,128)S(1)}, f32[16,16,128]{2,1,0:T(8,128)S(1)}, u32[]{:S(2)}, u32[]{:S(2)}) collective-permute-start(f32[16,16,128]{2,1,0:T(8,128)S(1)} %get-tuple-element.44), channel_id=1, source_target_pairs={{0,16},{1,17},{2,18},{3,19},{4,20},{5,21},{6,22},{7,23},{8,24},{9,... | collective-permute-start | bytes 393224 | tf_op jit(solution)/shard_map/sum_swap/ppermute | solution.py:29
  29.9 7.3 %collective-permute-start.12 = (f32[16,16,128]{2,1,0:T(8,128)S(1)}, f32[16,16,128]{2,1,0:T(8,128)S(1)}, u32[]{:S(2)}, u32[]{:S(2)}) collective-permute-start(f32[16,16,128]{2,1,0:T(8,128)S(1)} %get-tuple-element.45), channel_id=1, source_target_pairs={{0,16},{1,17},{2,18},{3,19},{4,20},{5,21},{6,22},{7,23},{8,24},{9,... | collective-permute-start | bytes 393224 | tf_op jit(solution)/shard_map/sum_swap/ppermute | solution.py:29
  31.7 10.7 %collective-permute-start.15 = (f32[32,16,128]{2,1,0:T(8,128)S(1)}, f32[32,16,128]{2,1,0:T(8,128)S(1)}, u32[]{:S(2)}, u32[]{:S(2)}) collective-permute-start(f32[32,16,128]{2,1,0:T(8,128)S(1)} %second.4.refs_0_), channel_id=1, source_target_pairs={{0,64},{1,65},{2,66},{3,67},{4,68},{5,69},{6,70},{7,71},{8,72},{9,... | collective-permute-start | bytes 786440 | tf_op jit(solution)/shard_map/sum_side/ppermute | solution.py:29
  36.7 5.7 %collective-permute-start.16 = (f32[32,16,128]{2,1,0:T(8,128)S(1)}, f32[32,16,128]{2,1,0:T(8,128)S(1)}, u32[]{:S(2)}, u32[]{:S(2)}) collective-permute-start(f32[32,16,128]{2,1,0:T(8,128)S(1)} %second.5.refs_0_), channel_id=1, source_target_pairs={{0,32},{1,33},{2,34},{3,35},{4,36},{5,37},{6,38},{7,39},{8,40},{9,... | collective-permute-start | bytes 786440 | tf_op jit(solution)/shard_map/sum_side/ppermute | solution.py:29
  38.3 6.6 %collective-permute-start.17 = (f32[32,16,128]{2,1,0:T(8,128)S(1)}, f32[32,16,128]{2,1,0:T(8,128)S(1)}, u32[]{:S(2)}, u32[]{:S(2)}) collective-permute-start(f32[32,16,128]{2,1,0:T(8,128)S(1)} %second.6.refs_0_), channel_id=1, source_target_pairs={{0,96},{1,97},{2,98},{3,99},{4,100},{5,101},{6,102},{7,103},{8,104... | collective-permute-start | bytes 786440 | tf_op jit(solution)/shard_map/sum_side/ppermute | solution.py:29
  38.7 2.2 %collective-permute-start.11 = (f32[16,16,128]{2,1,0:T(8,128)S(1)}, f32[16,16,128]{2,1,0:T(8,128)S(1)}, u32[]{:S(2)}, u32[]{:S(2)}) collective-permute-start(f32[16,16,128]{2,1,0:T(8,128)S(1)} %get-tuple-element.46), channel_id=1, source_target_pairs={{0,16},{1,17},{2,18},{3,19},{4,20},{5,21},{6,22},{7,23},{8,24},{9,... | collective-permute-start | bytes 393224 | tf_op jit(solution)/shard_map/sum_swap/ppermute | solution.py:29
  44.9 3.3 %collective-permute-start.18 = (f32[8,16,128]{2,1,0:T(8,128)S(1)}, f32[8,16,128]{2,1,0:T(8,128)S(1)}, u32[]{:S(2)}, u32[]{:S(2)}) collective-permute-start(f32[8,16,128]{2,1,0:T(8,128)S(1)} %get-tuple-element.47), channel_id=1, source_target_pairs={{0,128},{1,129},{2,130},{3,131},{4,132},{5,133},{6,134},{7,135},{8... | collective-permute-start | bytes 196616 | tf_op jit(solution)/shard_map/sum_z/ppermute | solution.py:29
  45.9 5.4 %collective-permute-start.20 = (f32[8,16,128]{2,1,0:T(8,128)S(1)}, f32[8,16,128]{2,1,0:T(8,128)S(1)}, u32[]{:S(2)}, u32[]{:S(2)}) collective-permute-start(f32[8,16,128]{2,1,0:T(8,128)S(1)} %get-tuple-element.48), channel_id=1, source_target_pairs={{0,32},{1,33},{2,34},{3,35},{4,36},{5,37},{6,38},{7,39},{8,40},{9,... | collective-permute-start | bytes 196616 | tf_op jit(solution)/shard_map/sum_z/ppermute | solution.py:29
  48.2 5.1 %collective-permute-start.19 = (f32[8,16,128]{2,1,0:T(8,128)S(1)}, f32[8,16,128]{2,1,0:T(8,128)S(1)}, u32[]{:S(2)}, u32[]{:S(2)}) collective-permute-start(f32[8,16,128]{2,1,0:T(8,128)S(1)} %get-tuple-element.49), channel_id=1, source_target_pairs={{0,32},{1,33},{2,34},{3,35},{4,36},{5,37},{6,38},{7,39},{8,40},{9,... | collective-permute-start | bytes 196616 | tf_op jit(solution)/shard_map/sum_z/ppermute | solution.py:29
  53.3 2.8 %collective-permute-start.21 = (f32[4,16,128]{2,1,0:T(8,128)S(1)}, f32[4,16,128]{2,1,0:T(8,128)S(1)}, u32[]{:S(2)}, u32[]{:S(2)}) collective-permute-start(f32[4,16,128]{2,1,0:T(8,128)S(1)} %slice.49), channel_id=1, source_target_pairs={{0,16},{1,17},{2,18},{3,19},{4,20},{5,21},{6,22},{7,23},{8,24},{9,... | collective-permute-start | bytes 98312 | tf_op jit(solution)/shard_map/sum_core/ppermute | solution.py:29

commit v5 on v4

--- a/solution.py
+++ b/solution.py
@@ -8,7 +8,7 @@
 
 AXIS = 16
 GROUP = 4
-CHUNK = 8
+CHUNK = 16
 BF16 = jnp.bfloat16
 F32 = jnp.float32
 AXES = ("row", "col")
@@ -63,14 +63,14 @@
     high_out, low_out = refs[-2:]
 
     def one_chunk(chunk, carry):
-        span = pl.ds(chunk * CHUNK, CHUNK)
+        span = pl.ds(chunk * 8, 8)
         tile = tiles[span]
         high = tile.astype(BF16)
         high_out[span] = high
         low_out[span] = (tile - high.astype(F32)).astype(BF16)
         return carry
 
-    lax.fori_loop(0, tiles.shape[0] // CHUNK, one_chunk, 0)
+    lax.fori_loop(0, tiles.shape[0] // 8, one_chunk, 0)
 
 
 def stage(tiles, after):
@@ -176,12 +176,12 @@
             (((1,), (0 if transposed else 1,)), ((), ())),
             preferred_element_type=F32,
         )
-        target = jnp.where(place < end, code & target_mask, target_mask + 1)
-        total[target] += product[:vecs] + product[vecs:]
+        return jnp.where(place < end, code & target_mask, target_mask + 1), product[:vecs] + product[vecs:]
 
     def one_chunk(chunk, carry):
-        for step in range(CHUNK):
-            one_slot(start + chunk * CHUNK + step)
+        sums = [one_slot(start + chunk * CHUNK + step) for step in range(CHUNK)]
+        for target, value in sums:
+            total[target] += value
         return carry
 
     lax.fori_loop(0, (end - start + CHUNK - 1) // CHUNK, one_chunk, 0)

time: 56.9 us -> 56.1 us (0.986)
  starting transfers between devices: 32 us -> 26.6 us
  Pallas kernels: 9.3 us -> 12.3 us
  waiting for transfers between devices: 9.74 us -> 10.8 us
    ppermute x22, starting transfers between devices: 32 us -> 26.6 us  [send(): return lax.ppermute(value, AXES, pairs)]
    pallas_call x20, Pallas kernels: 9.3 us -> 12.3 us  [call(): pl.pallas_call(kernel, out_shape=out_shape, in_specs=in_specs, out_specs=...]
    ppermute x22, waiting for transfers between devices: 9.74 us -> 10.8 us  [send(): return lax.ppermute(value, AXES, pairs)]
  transfers between devices with their start and end apart: 22 -> 22, of which waited for: 7 -> 9; matrix products, arithmetic and copies ran while one was open for 1% -> 1% of each run, Pallas kernels for 16% -> 22%
where the time goes in v5:
time: 56.1 us; the launch traced here: 55.3 us
  starting transfers between devices  26.6 us (47%)
  Pallas kernels  12.3 us (22%)
  waiting for transfers between devices  10.8 us (19%)
  local copies, waits for them, and re-layouts  3.61 us (6%)
  other arithmetic  1.07 us (2%)
  between operations  0.93 us (2%)
    ppermute x22, starting transfers between devices, send(): return lax.ppermute(value, AXES, pairs)  26.6 us
    pallas_call x20, Pallas kernels, call(): pl.pallas_call(kernel, out_shape=out_shape, in_specs=in_specs, out_specs=...  12.3 us
    ppermute x22, waiting for transfers between devices, send(): return lax.ppermute(value, AXES, pairs)  10.8 us
    unnamed x8, local copies, waits for them, and re-layouts  3.55 us
  transfers between devices with their start and end apart: 22, of which 9 were waited for; matrix products, arithmetic and copies ran while one was open for 1% of the time, Pallas kernels for 22%

profile of v5, /device:TPU:1, one launch (start us, length us, event | category | flops | bytes accessed | tf_op | source)
XLA Modules:
  0.0 55.3 jit_solution(5531026561414775777)
XLA Ops:
  0.0 3.2 %collective-permute-start = (f32[4,16,128]{2,1,0:T(8,128)}, f32[4,16,128]{2,1,0:T(8,128)S(1)}, u32[]{:S(2)}, u32[]{:S(2)}) collective-permute-start(f32[4,16,128]{2,1,0:T(8,128)} %bitcast.61), channel_id=1, source_target_pairs={{0,16},{1,17},{2,18},{3,19},{4,20},{5,21},{6,22},{7,23},{8,24},{9,... | collective-permute-start | bytes 98312 | tf_op jit(solution)/shard_map/gather_core/ppermute | solution.py:29
  3.2 0.8 %copy-done.1 = f32[4,1,1,16,128]{4,3,2,1,0:T(8,128)S(1)} copy-done((f32[4,1,1,16,128]{4,3,2,1,0:T(8,128)S(1)}, f32[4,1,1,16,128]{4,3,2,1,0:T(8,128)}, u32[]{:S(2)}) %copy-start.1) | copy-done | bytes 32792
  4.7 2.7 %collective-permute-start.3 = (f32[8,16,128]{2,1,0:T(8,128)S(1)}, f32[8,16,128]{2,1,0:T(8,128)S(1)}, u32[]{:S(2)}, u32[]{:S(2)}) collective-permute-start(f32[8,16,128]{2,1,0:T(8,128)S(1)} %pair.1.refs_0_), channel_id=1, source_target_pairs={{0,128},{1,129},{2,130},{3,131},{4,132},{5,133},{6,134},{7,135},{8... | collective-permute-start | bytes 196616 | tf_op jit(solution)/shard_map/gather_z/ppermute | solution.py:29
  7.4 0.9 %collective-permute-start.1 = (f32[8,16,128]{2,1,0:T(8,128)S(1)}, f32[8,16,128]{2,1,0:T(8,128)S(1)}, u32[]{:S(2)}, u32[]{:S(2)}) collective-permute-start(f32[8,16,128]{2,1,0:T(8,128)S(1)} %pair.1.refs_0_), channel_id=1, source_target_pairs={{0,32},{1,33},{2,34},{3,35},{4,36},{5,37},{6,38},{7,39},{8,40},{9,... | collective-permute-start | bytes 196616 | tf_op jit(solution)/shard_map/gather_z/ppermute | solution.py:29
  8.3 2.8 %copy-done = f32[1,1,96,128,128]{4,3,2,1,0:T(8,128)S(1)} copy-done((f32[1,1,96,128,128]{4,3,2,1,0:T(8,128)S(1)}, f32[1,1,96,128,128]{4,3,2,1,0:T(8,128)}, u32[]{:S(2)}) %copy-start) | copy-done | bytes 6291480
  11.1 0.9 %stage.1 = (bf16[96,128,128]{2,1,0:T(8,128)(2,1)S(1)}, bf16[96,128,128]{2,1,0:T(8,128)(2,1)S(1)}) custom-call(f32[96,128,128]{2,1,0:T(8,128)S(1)} %bitcast.60, f32[8,16,128]{2,1,0:T(8,128)S(1)} %pair.1.refs_0_), custom_call_target="tpu_custom_call" | custom-call | tf_op jit(solution)/shard_map/stage/pallas_call | solution.py:45
  12.1 2.4 %collective-permute-start.6 = (f32[32,16,128]{2,1,0:T(8,128)S(1)}, f32[32,16,128]{2,1,0:T(8,128)S(1)}, u32[]{:S(2)}, u32[]{:S(2)}) collective-permute-start(f32[32,16,128]{2,1,0:T(8,128)S(1)} %column.1.after.part), channel_id=1, source_target_pairs={{0,64},{1,65},{2,66},{3,67},{4,68},{5,69},{6,70},{7,71},{8,72},{9,... | collective-permute-start | bytes 786440 | tf_op jit(solution)/shard_map/gather_side/ppermute | solution.py:29
  14.9 0.6 %collective-permute-start.4 = (f32[32,16,128]{2,1,0:T(8,128)S(1)}, f32[32,16,128]{2,1,0:T(8,128)S(1)}, u32[]{:S(2)}, u32[]{:S(2)}) collective-permute-start(f32[32,16,128]{2,1,0:T(8,128)S(1)} %column.1.after.part), channel_id=1, source_target_pairs={{0,96},{1,97},{2,98},{3,99},{4,100},{5,101},{6,102},{7,103},{8,104... | collective-permute-start | bytes 786440 | tf_op jit(solution)/shard_map/gather_side/ppermute | solution.py:29
  15.9 1.2 %first.4 = (f32[72,16,128]{2,1,0:T(8,128)S(1)}, f32[16,16,128]{2,1,0:T(8,128)S(1)}) custom-call(s32[1,128]{1,0:T(1,128)S(1)} %bitcast.67, bf16[96,128,128]{2,1,0:T(8,128)(2,1)S(1)} %get-tuple-element.17.refs_4_.high, bf16[96,128,128]{2,1,0:T(8,128)(2,1)S(1)} %get-tuple-element.20.low, f32[32,16,128]{2,1,0:T(8,128)S(1)} %column.1.after.part), custom_call_target="tpu_custom_call" | custom-call | bytes 8388608 | tf_op jit(solution)/shard_map/first/pallas_call | solution.py:45
  17.2 4.9 %collective-permute-start.7 = (f32[16,16,128]{2,1,0:T(8,128)S(1)}, f32[16,16,128]{2,1,0:T(8,128)S(1)}, u32[]{:S(2)}, u32[]{:S(2)}) collective-permute-start(f32[16,16,128]{2,1,0:T(8,128)S(1)} %get-tuple-element.23), channel_id=1, source_target_pairs={{0,16},{1,17},{2,18},{3,19},{4,20},{5,21},{6,22},{7,23},{8,24},{9,... | collective-permute-start | bytes 393224 | tf_op jit(solution)/shard_map/gather_swap/ppermute | solution.py:29
  22.1 1.2 %first.5 = (f32[72,16,128]{2,1,0:T(8,128)S(1)}, f32[16,16,128]{2,1,0:T(8,128)S(1)}) custom-call(s32[1,128]{1,0:T(1,128)S(1)} %bitcast.68, bf16[96,128,128]{2,1,0:T(8,128)(2,1)S(1)} %get-tuple-element.17.refs_4_.high, bf16[96,128,128]{2,1,0:T(8,128)(2,1)S(1)} %get-tuple-element.20.low, ...), custom_call_target="tpu_custom_call", output_to_operand_aliasing={{0}: (4, {})} | custom-call | bytes 8388608 | tf_op jit(solution)/shard_map/first/pallas_call | solution.py:45
  23.3 1.9 %collective-permute-start.8 = (f32[16,16,128]{2,1,0:T(8,128)S(1)}, f32[16,16,128]{2,1,0:T(8,128)S(1)}, u32[]{:S(2)}, u32[]{:S(2)}) collective-permute-start(f32[16,16,128]{2,1,0:T(8,128)S(1)} %get-tuple-element.25), channel_id=1, source_target_pairs={{0,16},{1,17},{2,18},{3,19},{4,20},{5,21},{6,22},{7,23},{8,24},{9,... | collective-permute-start | bytes 393224 | tf_op jit(solution)/shard_map/gather_swap/ppermute | solution.py:29
  25.3 1.2 %first.6 = (f32[72,16,128]{2,1,0:T(8,128)S(1)}, f32[16,16,128]{2,1,0:T(8,128)S(1)}) custom-call(s32[1,128]{1,0:T(1,128)S(1)} %bitcast.69, bf16[96,128,128]{2,1,0:T(8,128)(2,1)S(1)} %get-tuple-element.17.refs_4_.high, bf16[96,128,128]{2,1,0:T(8,128)(2,1)S(1)} %get-tuple-element.20.low, ...), custom_call_target="tpu_custom_call", output_to_operand_aliasing={{0}: (4, {})} | custom-call | bytes 8388608 | tf_op jit(solution)/shard_map/first/pallas_call | solution.py:45
  26.5 1.9 %collective-permute-start.10 = (f32[16,16,128]{2,1,0:T(8,128)S(1)}, f32[16,16,128]{2,1,0:T(8,128)S(1)}, u32[]{:S(2)}, u32[]{:S(2)}) collective-permute-start(f32[16,16,128]{2,1,0:T(8,128)S(1)} %get-tuple-element.27), channel_id=1, source_target_pairs={{0,16},{1,17},{2,18},{3,19},{4,20},{5,21},{6,22},{7,23},{8,24},{9,... | collective-permute-start | bytes 393224 | tf_op jit(solution)/shard_map/gather_swap/ppermute | solution.py:29
  28.4 1.2 %first.7 = (f32[72,16,128]{2,1,0:T(8,128)S(1)}, f32[16,16,128]{2,1,0:T(8,128)S(1)}) custom-call(s32[1,128]{1,0:T(1,128)S(1)} %bitcast.70, bf16[96,128,128]{2,1,0:T(8,128)(2,1)S(1)} %get-tuple-element.17.refs_4_.high, bf16[96,128,128]{2,1,0:T(8,128)(2,1)S(1)} %get-tuple-element.20.low, ...), custom_call_target="tpu_custom_call", output_to_operand_aliasing={{0}: (4, {})} | custom-call | bytes 8388608 | tf_op jit(solution)/shard_map/first/pallas_call | solution.py:45
  29.8 0.6 %collective-permute-start.14 = (f32[16,16,128]{2,1,0:T(8,128)S(1)}, f32[16,16,128]{2,1,0:T(8,128)S(1)}, u32[]{:S(2)}, u32[]{:S(2)}) collective-permute-start(f32[16,16,128]{2,1,0:T(8,128)S(1)} %get-tuple-element.43), channel_id=1, source_target_pairs={{0,16},{1,17},{2,18},{3,19},{4,20},{5,21},{6,22},{7,23},{8,24},{9,... | collective-permute-start | bytes 393224 | tf_op jit(solution)/shard_map/sum_swap/ppermute | solution.py:29
  30.5 0.4 collective-permute-start.12
  31.3 1.5 %second.4.refs_0_ = f32[32,16,128]{2,1,0:T(8,128)S(1)} custom-call(s32[1,128]{1,0:T(1,128)S(1)} %bitcast.63, bf16[96,128,128]{2,1,0:T(8,128)(2,1)S(1)} %get-tuple-element.17.refs_4_.high, bf16[96,128,128]{2,1,0:T(8,128)(2,1)S(1)} %get-tuple-element.20.low, bf16[64,32,256]{2,1,0:T(8,128)(2,1)S(1)} %split.7, f32[16,16,128]{2,1,0:T(8,128)S(1)} %collective-permute-done.14.got), custom_call_target="tpu_custom_call" | custom-call | bytes 8388608 | tf_op jit(solution)/shard_map/second/pallas_call | solution.py:45
  32.9 2.6 %collective-permute-start.15 = (f32[32,16,128]{2,1,0:T(8,128)S(1)}, f32[32,16,128]{2,1,0:T(8,128)S(1)}, u32[]{:S(2)}, u32[]{:S(2)}) collective-permute-start(f32[32,16,128]{2,1,0:T(8,128)S(1)} %second.4.refs_0_), channel_id=1, source_target_pairs={{0,64},{1,65},{2,66},{3,67},{4,68},{5,69},{6,70},{7,71},{8,72},{9,... | collective-permute-start | bytes 786440 | tf_op jit(solution)/shard_map/sum_side/ppermute | solution.py:29
  35.5 1.7 %second.5.refs_0_ = f32[32,16,128]{2,1,0:T(8,128)S(1)} custom-call(s32[1,128]{1,0:T(1,128)S(1)} %bitcast.64, bf16[96,128,128]{2,1,0:T(8,128)(2,1)S(1)} %get-tuple-element.17.refs_4_.high, bf16[96,128,128]{2,1,0:T(8,128)(2,1)S(1)} %get-tuple-element.20.low, bf16[64,32,256]{2,1,0:T(8,128)(2,1)S(1)} %split.7, f32[16,16,128]{2,1,0:T(8,128)S(1)} %collective-permute-done.13.got, ...), custom_call_target="tpu_custom_call" | custom-call | bytes 8388608 | tf_op jit(solution)/shard_map/second/pallas_call | solution.py:45
  37.3 1.5 %second.6.refs_0_ = f32[32,16,128]{2,1,0:T(8,128)S(1)} custom-call(s32[1,128]{1,0:T(1,128)S(1)} %bitcast.65, bf16[96,128,128]{2,1,0:T(8,128)(2,1)S(1)} %get-tuple-element.17.refs_4_.high, bf16[96,128,128]{2,1,0:T(8,128)(2,1)S(1)} %get-tuple-element.20.low, bf16[64,32,256]{2,1,0:T(8,128)(2,1)S(1)} %split.7, f32[16,16,128]{2,1,0:T(8,128)S(1)} %collective-permute-done.12.got, ...), custom_call_target="tpu_custom_call" | custom-call | bytes 8388608 | tf_op jit(solution)/shard_map/second/pallas_call | solution.py:45
  39.3 1.3 %collective-permute-done.11.got = f32[16,16,128]{2,1,0:T(8,128)S(1)} collective-permute-done((f32[16,16,128]{2,1,0:T(8,128)S(1)}, f32[16,16,128]{2,1,0:T(8,128)S(1)}, u32[]{:S(2)}, u32[]{:S(2)}) %collective-permute-start.11) | collective-permute-done | bytes 131104 | tf_op jit(solution)/shard_map/sum_swap/ppermute | solution.py:29
  40.6 1.5 %second.7.one = f32[32,16,128]{2,1,0:T(8,128)S(1)} custom-call(s32[1,128]{1,0:T(1,128)S(1)} %bitcast.66, bf16[96,128,128]{2,1,0:T(8,128)(2,1)S(1)} %get-tuple-element.17.refs_4_.high, bf16[96,128,128]{2,1,0:T(8,128)(2,1)S(1)} %get-tuple-element.20.low, bf16[64,32,256]{2,1,0:T(8,128)(2,1)S(1)} %split.7, f32[16,16,128]{2,1,0:T(8,128)S(1)} %collective-permute-done.11.got, ...), custom_call_target="tpu_custom_call" | custom-call | bytes 8388608 | tf_op jit(solution)/shard_map/second/pallas_call | solution.py:45
  42.1 0.6 %collective-permute-done.16.two = f32[32,16,128]{2,1,0:T(8,128)S(1)} collective-permute-done((f32[32,16,128]{2,1,0:T(8,128)S(1)}, f32[32,16,128]{2,1,0:T(8,128)S(1)}, u32[]{:S(2)}, u32[]{:S(2)}) %collective-permute-start.16) | collective-permute-done | bytes 262176 | tf_op jit(solution)/shard_map/sum_side/ppermute | solution.py:29
  42.8 2.5 %collective-permute-done.17.two = f32[32,16,128]{2,1,0:T(8,128)S(1)} collective-permute-done((f32[32,16,128]{2,1,0:T(8,128)S(1)}, f32[32,16,128]{2,1,0:T(8,128)S(1)}, u32[]{:S(2)}, u32[]{:S(2)}) %collective-permute-start.17) | collective-permute-done | bytes 262176 | tf_op jit(solution)/shard_map/sum_side/ppermute | solution.py:29
  45.6 2.3 %collective-permute-start.20 = (f32[8,16,128]{2,1,0:T(8,128)S(1)}, f32[8,16,128]{2,1,0:T(8,128)S(1)}, u32[]{:S(2)}, u32[]{:S(2)}) collective-permute-start(f32[8,16,128]{2,1,0:T(8,128)S(1)} %get-tuple-element.48), channel_id=1, source_target_pairs={{0,32},{1,33},{2,34},{3,35},{4,36},{5,37},{6,38},{7,39},{8,40},{9,... | collective-permute-start | bytes 196616 | tf_op jit(solution)/shard_map/sum_z/ppermute | solution.py:29
  48.2 0.5 collective-permute-done.18
  48.6 2.0 %collective-permute-done.20 = f32[8,16,128]{2,1,0:T(8,128)S(1)} collective-permute-done((f32[8,16,128]{2,1,0:T(8,128)S(1)}, f32[8,16,128]{2,1,0:T(8,128)S(1)}, u32[]{:S(2)}, u32[]{:S(2)}) %collective-permute-start.20) | collective-permute-done | bytes 65568 | tf_op jit(solution)/shard_map/sum_z/ppermute | solution.py:29
  50.7 2.6 %collective-permute-done.19 = f32[8,16,128]{2,1,0:T(8,128)S(1)} collective-permute-done((f32[8,16,128]{2,1,0:T(8,128)S(1)}, f32[8,16,128]{2,1,0:T(8,128)S(1)}, u32[]{:S(2)}, u32[]{:S(2)}) %collective-permute-start.19) | collective-permute-done | bytes 65568 | tf_op jit(solution)/shard_map/sum_z/ppermute | solution.py:29
  53.3 0.6 %collective-permute-start.21 = (f32[4,16,128]{2,1,0:T(8,128)S(1)}, f32[4,16,128]{2,1,0:T(8,128)S(1)}, u32[]{:S(2)}, u32[]{:S(2)}) collective-permute-start(f32[4,16,128]{2,1,0:T(8,128)S(1)} %slice.49), channel_id=1, source_target_pairs={{0,16},{1,17},{2,18},{3,19},{4,20},{5,21},{6,22},{7,23},{8,24},{9,... | collective-permute-start | bytes 98312 | tf_op jit(solution)/shard_map/sum_core/ppermute | solution.py:29
  53.9 0.9 %collective-permute-done.21 = f32[4,16,128]{2,1,0:T(8,128)S(1)} collective-permute-done((f32[4,16,128]{2,1,0:T(8,128)S(1)}, f32[4,16,128]{2,1,0:T(8,128)S(1)}, u32[]{:S(2)}, u32[]{:S(2)}) %collective-permute-start.21) | collective-permute-done | bytes 32800 | tf_op jit(solution)/shard_map/sum_core/ppermute | solution.py:29
  54.7 0.6 %fusion.6 = f32[4,1,1,16,128]{4,3,2,1,0:T(8,128)} fusion(f32[4,16,128]{2,1,0:T(8,128)S(1)} %collective-permute-done.21, f32[8,16,128]{2,1,0:T(8,128)S(1)} %fusion.1), kind=kLoop, calls=%fused_computation.15 | loop fusion | flops 8192 | bytes 98304 | tf_op jit(solution)/shard_map/reshape | solution.py:345
  (53 shorter events, 2.7 us)
Async XLA Ops:
  0.0 4.7 %collective-permute-start = (f32[4,16,128]{2,1,0:T(8,128)}, f32[4,16,128]{2,1,0:T(8,128)S(1)}, u32[]{:S(2)}, u32[]{:S(2)}) collective-permute-start(f32[4,16,128]{2,1,0:T(8,128)} %bitcast.61), channel_id=1, source_target_pairs={{0,16},{1,17},{2,18},{3,19},{4,20},{5,21},{6,22},{7,23},{8,24},{9,... | collective-permute-start | bytes 98312 | tf_op jit(solution)/shard_map/gather_core/ppermute | solution.py:29
  3.2 0.8 %copy-start.1 = (f32[4,1,1,16,128]{4,3,2,1,0:T(8,128)S(1)}, f32[4,1,1,16,128]{4,3,2,1,0:T(8,128)}, u32[]{:S(2)}) copy-start(f32[4,1,1,16,128]{4,3,2,1,0:T(8,128)} %param.5) | copy-start | bytes 98308
  4.7 7.4 %collective-permute-start.3 = (f32[8,16,128]{2,1,0:T(8,128)S(1)}, f32[8,16,128]{2,1,0:T(8,128)S(1)}, u32[]{:S(2)}, u32[]{:S(2)}) collective-permute-start(f32[8,16,128]{2,1,0:T(8,128)S(1)} %pair.1.refs_0_), channel_id=1, source_target_pairs={{0,128},{1,129},{2,130},{3,131},{4,132},{5,133},{6,134},{7,135},{8... | collective-permute-start | bytes 196616 | tf_op jit(solution)/shard_map/gather_z/ppermute | solution.py:29
  7.4 4.7 %collective-permute-start.2 = (f32[8,16,128]{2,1,0:T(8,128)S(1)}, f32[8,16,128]{2,1,0:T(8,128)S(1)}, u32[]{:S(2)}, u32[]{:S(2)}) collective-permute-start(f32[8,16,128]{2,1,0:T(8,128)S(1)} %pair.1.refs_0_), channel_id=1, source_target_pairs={{0,32},{1,33},{2,34},{3,35},{4,36},{5,37},{6,38},{7,39},{8,40},{9,... | collective-permute-start | bytes 196616 | tf_op jit(solution)/shard_map/gather_z/ppermute | solution.py:29
  7.4 4.7 %collective-permute-start.1 = (f32[8,16,128]{2,1,0:T(8,128)S(1)}, f32[8,16,128]{2,1,0:T(8,128)S(1)}, u32[]{:S(2)}, u32[]{:S(2)}) collective-permute-start(f32[8,16,128]{2,1,0:T(8,128)S(1)} %pair.1.refs_0_), channel_id=1, source_target_pairs={{0,32},{1,33},{2,34},{3,35},{4,36},{5,37},{6,38},{7,39},{8,40},{9,... | collective-permute-start | bytes 196616 | tf_op jit(solution)/shard_map/gather_z/ppermute | solution.py:29
  8.3 2.8 %copy-start = (f32[1,1,96,128,128]{4,3,2,1,0:T(8,128)S(1)}, f32[1,1,96,128,128]{4,3,2,1,0:T(8,128)}, u32[]{:S(2)}) copy-start(f32[1,1,96,128,128]{4,3,2,1,0:T(8,128)} %param.6) | copy-start | bytes 18874372
  12.0 3.4 %copy-start.2 = (s32[1,1,96]{2,1,0:T(1,128)S(1)}, s32[1,1,96]{2,1,0:T(1,128)}, u32[]{:S(2)}) copy-start(s32[1,1,96]{2,1,0:T(1,128)} %param.7) | copy-start | bytes 1156
  12.0 3.4 %copy-start.3 = (s32[1,1,96]{2,1,0:T(1,128)S(1)}, s32[1,1,96]{2,1,0:T(1,128)}, u32[]{:S(2)}) copy-start(s32[1,1,96]{2,1,0:T(1,128)} %param.8) | copy-start | bytes 1156
  12.1 9.9 %collective-permute-start.6 = (f32[32,16,128]{2,1,0:T(8,128)S(1)}, f32[32,16,128]{2,1,0:T(8,128)S(1)}, u32[]{:S(2)}, u32[]{:S(2)}) collective-permute-start(f32[32,16,128]{2,1,0:T(8,128)S(1)} %column.1.after.part), channel_id=1, source_target_pairs={{0,64},{1,65},{2,66},{3,67},{4,68},{5,69},{6,70},{7,71},{8,72},{9,... | collective-permute-start | bytes 786440 | tf_op jit(solution)/shard_map/gather_side/ppermute | solution.py:29
  14.6 10.7 %collective-permute-start.5 = (f32[32,16,128]{2,1,0:T(8,128)S(1)}, f32[32,16,128]{2,1,0:T(8,128)S(1)}, u32[]{:S(2)}, u32[]{:S(2)}) collective-permute-start(f32[32,16,128]{2,1,0:T(8,128)S(1)} %column.1.after.part), channel_id=1, source_target_pairs={{0,32},{1,33},{2,34},{3,35},{4,36},{5,37},{6,38},{7,39},{8,40},{9,... | collective-permute-start | bytes 786440 | tf_op jit(solution)/shard_map/gather_side/ppermute | solution.py:29
  14.9 13.6 %collective-permute-start.4 = (f32[32,16,128]{2,1,0:T(8,128)S(1)}, f32[32,16,128]{2,1,0:T(8,128)S(1)}, u32[]{:S(2)}, u32[]{:S(2)}) collective-permute-start(f32[32,16,128]{2,1,0:T(8,128)S(1)} %column.1.after.part), channel_id=1, source_target_pairs={{0,96},{1,97},{2,98},{3,99},{4,100},{5,101},{6,102},{7,103},{8,104... | collective-permute-start | bytes 786440 | tf_op jit(solution)/shard_map/gather_side/ppermute | solution.py:29
  17.2 8.1 %collective-permute-start.7 = (f32[16,16,128]{2,1,0:T(8,128)S(1)}, f32[16,16,128]{2,1,0:T(8,128)S(1)}, u32[]{:S(2)}, u32[]{:S(2)}) collective-permute-start(f32[16,16,128]{2,1,0:T(8,128)S(1)} %get-tuple-element.23), channel_id=1, source_target_pairs={{0,16},{1,17},{2,18},{3,19},{4,20},{5,21},{6,22},{7,23},{8,24},{9,... | collective-permute-start | bytes 393224 | tf_op jit(solution)/shard_map/gather_swap/ppermute | solution.py:29
  23.3 5.1 %collective-permute-start.8 = (f32[16,16,128]{2,1,0:T(8,128)S(1)}, f32[16,16,128]{2,1,0:T(8,128)S(1)}, u32[]{:S(2)}, u32[]{:S(2)}) collective-permute-start(f32[16,16,128]{2,1,0:T(8,128)S(1)} %get-tuple-element.25), channel_id=1, source_target_pairs={{0,16},{1,17},{2,18},{3,19},{4,20},{5,21},{6,22},{7,23},{8,24},{9,... | collective-permute-start | bytes 393224 | tf_op jit(solution)/shard_map/gather_swap/ppermute | solution.py:29
  26.5 4.4 %collective-permute-start.10 = (f32[16,16,128]{2,1,0:T(8,128)S(1)}, f32[16,16,128]{2,1,0:T(8,128)S(1)}, u32[]{:S(2)}, u32[]{:S(2)}) collective-permute-start(f32[16,16,128]{2,1,0:T(8,128)S(1)} %get-tuple-element.27), channel_id=1, source_target_pairs={{0,16},{1,17},{2,18},{3,19},{4,20},{5,21},{6,22},{7,23},{8,24},{9,... | collective-permute-start | bytes 393224 | tf_op jit(solution)/shard_map/gather_swap/ppermute | solution.py:29
  29.6 1.4 %collective-permute-start.9 = (f32[16,16,128]{2,1,0:T(8,128)S(1)}, f32[16,16,128]{2,1,0:T(8,128)S(1)}, u32[]{:S(2)}, u32[]{:S(2)}) collective-permute-start(f32[16,16,128]{2,1,0:T(8,128)S(1)} %get-tuple-element.26), channel_id=1, source_target_pairs={{0,16},{1,17},{2,18},{3,19},{4,20},{5,21},{6,22},{7,23},{8,24},{9,... | collective-permute-start | bytes 393224 | tf_op jit(solution)/shard_map/gather_swap/ppermute | solution.py:29
  29.8 1.6 %collective-permute-start.14 = (f32[16,16,128]{2,1,0:T(8,128)S(1)}, f32[16,16,128]{2,1,0:T(8,128)S(1)}, u32[]{:S(2)}, u32[]{:S(2)}) collective-permute-start(f32[16,16,128]{2,1,0:T(8,128)S(1)} %get-tuple-element.43), channel_id=1, source_target_pairs={{0,16},{1,17},{2,18},{3,19},{4,20},{5,21},{6,22},{7,23},{8,24},{9,... | collective-permute-start | bytes 393224 | tf_op jit(solution)/shard_map/sum_swap/ppermute | solution.py:29
  30.4 5.1 %collective-permute-start.13 = (f32[16,16,128]{2,1,0:T(8,128)S(1)}, f32[16,16,128]{2,1,0:T(8,128)S(1)}, u32[]{:S(2)}, u32[]{:S(2)}) collective-permute-start(f32[16,16,128]{2,1,0:T(8,128)S(1)} %get-tuple-element.44), channel_id=1, source_target_pairs={{0,16},{1,17},{2,18},{3,19},{4,20},{5,21},{6,22},{7,23},{8,24},{9,... | collective-permute-start | bytes 393224 | tf_op jit(solution)/shard_map/sum_swap/ppermute | solution.py:29
  30.5 6.8 %collective-permute-start.12 = (f32[16,16,128]{2,1,0:T(8,128)S(1)}, f32[16,16,128]{2,1,0:T(8,128)S(1)}, u32[]{:S(2)}, u32[]{:S(2)}) collective-permute-start(f32[16,16,128]{2,1,0:T(8,128)S(1)} %get-tuple-element.45), channel_id=1, source_target_pairs={{0,16},{1,17},{2,18},{3,19},{4,20},{5,21},{6,22},{7,23},{8,24},{9,... | collective-permute-start | bytes 393224 | tf_op jit(solution)/shard_map/sum_swap/ppermute | solution.py:29
  32.9 9.2 %collective-permute-start.15 = (f32[32,16,128]{2,1,0:T(8,128)S(1)}, f32[32,16,128]{2,1,0:T(8,128)S(1)}, u32[]{:S(2)}, u32[]{:S(2)}) collective-permute-start(f32[32,16,128]{2,1,0:T(8,128)S(1)} %second.4.refs_0_), channel_id=1, source_target_pairs={{0,64},{1,65},{2,66},{3,67},{4,68},{5,69},{6,70},{7,71},{8,72},{9,... | collective-permute-start | bytes 786440 | tf_op jit(solution)/shard_map/sum_side/ppermute | solution.py:29
  37.2 5.6 %collective-permute-start.16 = (f32[32,16,128]{2,1,0:T(8,128)S(1)}, f32[32,16,128]{2,1,0:T(8,128)S(1)}, u32[]{:S(2)}, u32[]{:S(2)}) collective-permute-start(f32[32,16,128]{2,1,0:T(8,128)S(1)} %second.5.refs_0_), channel_id=1, source_target_pairs={{0,32},{1,33},{2,34},{3,35},{4,36},{5,37},{6,38},{7,39},{8,40},{9,... | collective-permute-start | bytes 786440 | tf_op jit(solution)/shard_map/sum_side/ppermute | solution.py:29
  38.9 6.5 %collective-permute-start.17 = (f32[32,16,128]{2,1,0:T(8,128)S(1)}, f32[32,16,128]{2,1,0:T(8,128)S(1)}, u32[]{:S(2)}, u32[]{:S(2)}) collective-permute-start(f32[32,16,128]{2,1,0:T(8,128)S(1)} %second.6.refs_0_), channel_id=1, source_target_pairs={{0,96},{1,97},{2,98},{3,99},{4,100},{5,101},{6,102},{7,103},{8,104... | collective-permute-start | bytes 786440 | tf_op jit(solution)/shard_map/sum_side/ppermute | solution.py:29
  39.2 1.3 %collective-permute-start.11 = (f32[16,16,128]{2,1,0:T(8,128)S(1)}, f32[16,16,128]{2,1,0:T(8,128)S(1)}, u32[]{:S(2)}, u32[]{:S(2)}) collective-permute-start(f32[16,16,128]{2,1,0:T(8,128)S(1)} %get-tuple-element.46), channel_id=1, source_target_pairs={{0,16},{1,17},{2,18},{3,19},{4,20},{5,21},{6,22},{7,23},{8,24},{9,... | collective-permute-start | bytes 393224 | tf_op jit(solution)/shard_map/sum_swap/ppermute | solution.py:29
  45.4 3.2 %collective-permute-start.18 = (f32[8,16,128]{2,1,0:T(8,128)S(1)}, f32[8,16,128]{2,1,0:T(8,128)S(1)}, u32[]{:S(2)}, u32[]{:S(2)}) collective-permute-start(f32[8,16,128]{2,1,0:T(8,128)S(1)} %get-tuple-element.47), channel_id=1, source_target_pairs={{0,128},{1,129},{2,130},{3,131},{4,132},{5,133},{6,134},{7,135},{8... | collective-permute-start | bytes 196616 | tf_op jit(solution)/shard_map/sum_z/ppermute | solution.py:29
  45.6 5.1 %collective-permute-start.20 = (f32[8,16,128]{2,1,0:T(8,128)S(1)}, f32[8,16,128]{2,1,0:T(8,128)S(1)}, u32[]{:S(2)}, u32[]{:S(2)}) collective-permute-start(f32[8,16,128]{2,1,0:T(8,128)S(1)} %get-tuple-element.48), channel_id=1, source_target_pairs={{0,32},{1,33},{2,34},{3,35},{4,36},{5,37},{6,38},{7,39},{8,40},{9,... | collective-permute-start | bytes 196616 | tf_op jit(solution)/shard_map/sum_z/ppermute | solution.py:29
  47.9 5.3 %collective-permute-start.19 = (f32[8,16,128]{2,1,0:T(8,128)S(1)}, f32[8,16,128]{2,1,0:T(8,128)S(1)}, u32[]{:S(2)}, u32[]{:S(2)}) collective-permute-start(f32[8,16,128]{2,1,0:T(8,128)S(1)} %get-tuple-element.49), channel_id=1, source_target_pairs={{0,32},{1,33},{2,34},{3,35},{4,36},{5,37},{6,38},{7,39},{8,40},{9,... | collective-permute-start | bytes 196616 | tf_op jit(solution)/shard_map/sum_z/ppermute | solution.py:29
  53.3 1.5 %collective-permute-start.21 = (f32[4,16,128]{2,1,0:T(8,128)S(1)}, f32[4,16,128]{2,1,0:T(8,128)S(1)}, u32[]{:S(2)}, u32[]{:S(2)}) collective-permute-start(f32[4,16,128]{2,1,0:T(8,128)S(1)} %slice.49), channel_id=1, source_target_pairs={{0,16},{1,17},{2,18},{3,19},{4,20},{5,21},{6,22},{7,23},{8,24},{9,... | collective-permute-start | bytes 98312 | tf_op jit(solution)/shard_map/sum_core/ppermute | solution.py:29

commit v6 on v5

--- a/solution.py
+++ b/solution.py
@@ -12,7 +12,7 @@
 BF16 = jnp.bfloat16
 F32 = jnp.float32
 AXES = ("row", "col")
-SIDES = (2, 1, 3)
+SIDES = (2, 3, 1)
 GSIDES = (2, 1, 3)
 VECTOR = pl.BlockSpec(memory_space=pltpu.VMEM)
 SCALAR = pl.BlockSpec(memory_space=pltpu.SMEM)
@@ -299,8 +299,8 @@
         (column,) = call(
             column_kernel,
             [block_of(8)],
-            [VECTOR] * GROUP + [ANYWHERE],
-            (pair, *far, staged[0]),
+            [VECTOR] * GROUP,
+            (pair, *far),
             name="column",
         )
         held = {0: column}

time: 56.1 us -> 56 us (level)
  starting transfers between devices: 26.6 us -> 30.4 us
  Pallas kernels: 12.3 us -> 9.33 us
  waiting for transfers between devices: 10.8 us -> 10.1 us
    ppermute x22, starting transfers between devices: 26.6 us -> 30.4 us  [send(): return lax.ppermute(value, AXES, pairs)]
    pallas_call x20, Pallas kernels: 12.3 us -> 9.33 us  [call(): pl.pallas_call(kernel, out_shape=out_shape, in_specs=in_specs, out_specs=...]
    ppermute x22, waiting for transfers between devices: 10.8 us -> 10.1 us  [send(): return lax.ppermute(value, AXES, pairs)]
  transfers between devices with their start and end apart: 22 -> 22, of which waited for: 9 -> 8; matrix products, arithmetic and copies ran while one was open for 1% -> 1% of each run, Pallas kernels for 22% -> 17%
where the time goes in v6:
time: 56 us; the launch traced here: 55.4 us
  starting transfers between devices  30.4 us (54%)
  waiting for transfers between devices  10.1 us (18%)
  Pallas kernels  9.33 us (17%)
  local copies, waits for them, and re-layouts  3.6 us (6%)
  other arithmetic  1.07 us (2%)
  between operations  0.89 us (2%)
    ppermute x22, starting transfers between devices, send(): return lax.ppermute(value, AXES, pairs)  30.4 us
    ppermute x22, waiting for transfers between devices, send(): return lax.ppermute(value, AXES, pairs)  10.1 us
    pallas_call x20, Pallas kernels, call(): pl.pallas_call(kernel, out_shape=out_shape, in_specs=in_specs, out_specs=...  9.33 us
    unnamed x8, local copies, waits for them, and re-layouts  3.55 us
  transfers between devices with their start and end apart: 22, of which 8 were waited for; matrix products, arithmetic and copies ran while one was open for 1% of the time, Pallas kernels for 17%

profile of v6, /device:TPU:1, one launch (start us, length us, event | category | flops | bytes accessed | tf_op | source)
XLA Modules:
  0.0 55.4 jit_solution(11218018426841080498)
XLA Ops:
  0.0 3.2 %collective-permute-start = (f32[4,16,128]{2,1,0:T(8,128)}, f32[4,16,128]{2,1,0:T(8,128)S(1)}, u32[]{:S(2)}, u32[]{:S(2)}) collective-permute-start(f32[4,16,128]{2,1,0:T(8,128)} %bitcast.61), channel_id=1, source_target_pairs={{0,16},{1,17},{2,18},{3,19},{4,20},{5,21},{6,22},{7,23},{8,24},{9,... | collective-permute-start | bytes 98312 | tf_op jit(solution)/shard_map/gather_core/ppermute | solution.py:29
  3.2 0.8 %copy-done.1 = f32[4,1,1,16,128]{4,3,2,1,0:T(8,128)S(1)} copy-done((f32[4,1,1,16,128]{4,3,2,1,0:T(8,128)S(1)}, f32[4,1,1,16,128]{4,3,2,1,0:T(8,128)}, u32[]{:S(2)}) %copy-start.1) | copy-done | bytes 32792
  4.7 2.7 %collective-permute-start.3 = (f32[8,16,128]{2,1,0:T(8,128)S(1)}, f32[8,16,128]{2,1,0:T(8,128)S(1)}, u32[]{:S(2)}, u32[]{:S(2)}) collective-permute-start(f32[8,16,128]{2,1,0:T(8,128)S(1)} %pair.1.refs_0_), channel_id=1, source_target_pairs={{0,128},{1,129},{2,130},{3,131},{4,132},{5,133},{6,134},{7,135},{8... | collective-permute-start | bytes 196616 | tf_op jit(solution)/shard_map/gather_z/ppermute | solution.py:29
  7.4 0.9 %collective-permute-start.1 = (f32[8,16,128]{2,1,0:T(8,128)S(1)}, f32[8,16,128]{2,1,0:T(8,128)S(1)}, u32[]{:S(2)}, u32[]{:S(2)}) collective-permute-start(f32[8,16,128]{2,1,0:T(8,128)S(1)} %pair.1.refs_0_), channel_id=1, source_target_pairs={{0,32},{1,33},{2,34},{3,35},{4,36},{5,37},{6,38},{7,39},{8,40},{9,... | collective-permute-start | bytes 196616 | tf_op jit(solution)/shard_map/gather_z/ppermute | solution.py:29
  8.3 2.8 %copy-done = f32[1,1,96,128,128]{4,3,2,1,0:T(8,128)S(1)} copy-done((f32[1,1,96,128,128]{4,3,2,1,0:T(8,128)S(1)}, f32[1,1,96,128,128]{4,3,2,1,0:T(8,128)}, u32[]{:S(2)}) %copy-start) | copy-done | bytes 6291480
  11.1 0.9 %stage.1 = (bf16[96,128,128]{2,1,0:T(8,128)(2,1)S(1)}, bf16[96,128,128]{2,1,0:T(8,128)(2,1)S(1)}) custom-call(f32[96,128,128]{2,1,0:T(8,128)S(1)} %bitcast.60, f32[8,16,128]{2,1,0:T(8,128)S(1)} %pair.1.refs_0_), custom_call_target="tpu_custom_call" | custom-call | tf_op jit(solution)/shard_map/stage/pallas_call | solution.py:45
  12.1 2.4 %collective-permute-start.6 = (f32[32,16,128]{2,1,0:T(8,128)S(1)}, f32[32,16,128]{2,1,0:T(8,128)S(1)}, u32[]{:S(2)}, u32[]{:S(2)}) collective-permute-start(f32[32,16,128]{2,1,0:T(8,128)S(1)} %column.1.after.part), channel_id=1, source_target_pairs={{0,64},{1,65},{2,66},{3,67},{4,68},{5,69},{6,70},{7,71},{8,72},{9,... | collective-permute-start | bytes 786440 | tf_op jit(solution)/shard_map/gather_side/ppermute | solution.py:29
  14.9 0.6 %collective-permute-start.4 = (f32[32,16,128]{2,1,0:T(8,128)S(1)}, f32[32,16,128]{2,1,0:T(8,128)S(1)}, u32[]{:S(2)}, u32[]{:S(2)}) collective-permute-start(f32[32,16,128]{2,1,0:T(8,128)S(1)} %column.1.after.part), channel_id=1, source_target_pairs={{0,96},{1,97},{2,98},{3,99},{4,100},{5,101},{6,102},{7,103},{8,104... | collective-permute-start | bytes 786440 | tf_op jit(solution)/shard_map/gather_side/ppermute | solution.py:29
  15.9 0.9 %first.4 = (f32[72,16,128]{2,1,0:T(8,128)S(1)}, f32[16,16,128]{2,1,0:T(8,128)S(1)}) custom-call(s32[1,128]{1,0:T(1,128)S(1)} %bitcast.67, bf16[96,128,128]{2,1,0:T(8,128)(2,1)S(1)} %get-tuple-element.19.high, bf16[96,128,128]{2,1,0:T(8,128)(2,1)S(1)} %get-tuple-element.20.low, f32[32,16,128]{2,1,0:T(8,128)S(1)} %column.1.after.part), custom_call_target="tpu_custom_call" | custom-call | bytes 8388608 | tf_op jit(solution)/shard_map/first/pallas_call | solution.py:45
  16.9 5.2 %collective-permute-start.7 = (f32[16,16,128]{2,1,0:T(8,128)S(1)}, f32[16,16,128]{2,1,0:T(8,128)S(1)}, u32[]{:S(2)}, u32[]{:S(2)}) collective-permute-start(f32[16,16,128]{2,1,0:T(8,128)S(1)} %get-tuple-element.23), channel_id=1, source_target_pairs={{0,16},{1,17},{2,18},{3,19},{4,20},{5,21},{6,22},{7,23},{8,24},{9,... | collective-permute-start | bytes 393224 | tf_op jit(solution)/shard_map/gather_swap/ppermute | solution.py:29
  22.1 0.9 %first.5 = (f32[72,16,128]{2,1,0:T(8,128)S(1)}, f32[16,16,128]{2,1,0:T(8,128)S(1)}) custom-call(s32[1,128]{1,0:T(1,128)S(1)} %bitcast.68, bf16[96,128,128]{2,1,0:T(8,128)(2,1)S(1)} %get-tuple-element.19.high, bf16[96,128,128]{2,1,0:T(8,128)(2,1)S(1)} %get-tuple-element.20.low, ...), custom_call_target="tpu_custom_call", output_to_operand_aliasing={{0}: (4, {})} | custom-call | bytes 8388608 | tf_op jit(solution)/shard_map/first/pallas_call | solution.py:45
  23.0 2.3 %collective-permute-start.8 = (f32[16,16,128]{2,1,0:T(8,128)S(1)}, f32[16,16,128]{2,1,0:T(8,128)S(1)}, u32[]{:S(2)}, u32[]{:S(2)}) collective-permute-start(f32[16,16,128]{2,1,0:T(8,128)S(1)} %get-tuple-element.25), channel_id=1, source_target_pairs={{0,16},{1,17},{2,18},{3,19},{4,20},{5,21},{6,22},{7,23},{8,24},{9,... | collective-permute-start | bytes 393224 | tf_op jit(solution)/shard_map/gather_swap/ppermute | solution.py:29
  25.3 0.9 %first.6 = (f32[72,16,128]{2,1,0:T(8,128)S(1)}, f32[16,16,128]{2,1,0:T(8,128)S(1)}) custom-call(s32[1,128]{1,0:T(1,128)S(1)} %bitcast.69, bf16[96,128,128]{2,1,0:T(8,128)(2,1)S(1)} %get-tuple-element.19.high, bf16[96,128,128]{2,1,0:T(8,128)(2,1)S(1)} %get-tuple-element.20.low, ...), custom_call_target="tpu_custom_call", output_to_operand_aliasing={{0}: (4, {})} | custom-call | bytes 8388608 | tf_op jit(solution)/shard_map/first/pallas_call | solution.py:45
  26.2 2.2 %collective-permute-start.10 = (f32[16,16,128]{2,1,0:T(8,128)S(1)}, f32[16,16,128]{2,1,0:T(8,128)S(1)}, u32[]{:S(2)}, u32[]{:S(2)}) collective-permute-start(f32[16,16,128]{2,1,0:T(8,128)S(1)} %get-tuple-element.27), channel_id=1, source_target_pairs={{0,16},{1,17},{2,18},{3,19},{4,20},{5,21},{6,22},{7,23},{8,24},{9,... | collective-permute-start | bytes 393224 | tf_op jit(solution)/shard_map/gather_swap/ppermute | solution.py:29
  28.4 0.9 %first.7 = (f32[72,16,128]{2,1,0:T(8,128)S(1)}, f32[16,16,128]{2,1,0:T(8,128)S(1)}) custom-call(s32[1,128]{1,0:T(1,128)S(1)} %bitcast.70, bf16[96,128,128]{2,1,0:T(8,128)(2,1)S(1)} %get-tuple-element.19.high, bf16[96,128,128]{2,1,0:T(8,128)(2,1)S(1)} %get-tuple-element.20.low, ...), custom_call_target="tpu_custom_call", output_to_operand_aliasing={{0}: (4, {})} | custom-call | bytes 8388608 | tf_op jit(solution)/shard_map/first/pallas_call | solution.py:45
  31.1 1.1 %second.4.refs_0_ = f32[32,16,128]{2,1,0:T(8,128)S(1)} custom-call(s32[1,128]{1,0:T(1,128)S(1)} %bitcast.63, bf16[96,128,128]{2,1,0:T(8,128)(2,1)S(1)} %get-tuple-element.19.high, bf16[96,128,128]{2,1,0:T(8,128)(2,1)S(1)} %get-tuple-element.20.low, bf16[64,32,256]{2,1,0:T(8,128)(2,1)S(1)} %split.7, f32[16,16,128]{2,1,0:T(8,128)S(1)} %collective-permute-done.14.got), custom_call_target="tpu_custom_call" | custom-call | bytes 8388608 | tf_op jit(solution)/shard_map/second/pallas_call | solution.py:45
  32.1 3.3 %collective-permute-start.15 = (f32[32,16,128]{2,1,0:T(8,128)S(1)}, f32[32,16,128]{2,1,0:T(8,128)S(1)}, u32[]{:S(2)}, u32[]{:S(2)}) collective-permute-start(f32[32,16,128]{2,1,0:T(8,128)S(1)} %second.4.refs_0_), channel_id=1, source_target_pairs={{0,64},{1,65},{2,66},{3,67},{4,68},{5,69},{6,70},{7,71},{8,72},{9,... | collective-permute-start | bytes 786440 | tf_op jit(solution)/shard_map/sum_side/ppermute | solution.py:29
  35.4 1.3 %second.5.refs_0_ = f32[32,16,128]{2,1,0:T(8,128)S(1)} custom-call(s32[1,128]{1,0:T(1,128)S(1)} %bitcast.64, bf16[96,128,128]{2,1,0:T(8,128)(2,1)S(1)} %get-tuple-element.19.high, bf16[96,128,128]{2,1,0:T(8,128)(2,1)S(1)} %get-tuple-element.20.low, bf16[64,32,256]{2,1,0:T(8,128)(2,1)S(1)} %split.7, f32[16,16,128]{2,1,0:T(8,128)S(1)} %collective-permute-done.13.got, ...), custom_call_target="tpu_custom_call" | custom-call | bytes 8388608 | tf_op jit(solution)/shard_map/second/pallas_call | solution.py:45
  36.7 0.5 collective-permute-start.16
  37.2 1.1 %second.6.refs_0_ = f32[32,16,128]{2,1,0:T(8,128)S(1)} custom-call(s32[1,128]{1,0:T(1,128)S(1)} %bitcast.65, bf16[96,128,128]{2,1,0:T(8,128)(2,1)S(1)} %get-tuple-element.19.high, bf16[96,128,128]{2,1,0:T(8,128)(2,1)S(1)} %get-tuple-element.20.low, bf16[64,32,256]{2,1,0:T(8,128)(2,1)S(1)} %split.7, f32[16,16,128]{2,1,0:T(8,128)S(1)} %collective-permute-done.12.got, ...), custom_call_target="tpu_custom_call" | custom-call | bytes 8388608 | tf_op jit(solution)/shard_map/second/pallas_call | solution.py:45
  38.4 0.6 %collective-permute-start.11 = (f32[16,16,128]{2,1,0:T(8,128)S(1)}, f32[16,16,128]{2,1,0:T(8,128)S(1)}, u32[]{:S(2)}, u32[]{:S(2)}) collective-permute-start(f32[16,16,128]{2,1,0:T(8,128)S(1)} %get-tuple-element.46), channel_id=1, source_target_pairs={{0,16},{1,17},{2,18},{3,19},{4,20},{5,21},{6,22},{7,23},{8,24},{9,... | collective-permute-start | bytes 393224 | tf_op jit(solution)/shard_map/sum_swap/ppermute | solution.py:29
  39.0 1.0 %collective-permute-done.11.got = f32[16,16,128]{2,1,0:T(8,128)S(1)} collective-permute-done((f32[16,16,128]{2,1,0:T(8,128)S(1)}, f32[16,16,128]{2,1,0:T(8,128)S(1)}, u32[]{:S(2)}, u32[]{:S(2)}) %collective-permute-start.11) | collective-permute-done | bytes 131104 | tf_op jit(solution)/shard_map/sum_swap/ppermute | solution.py:29
  39.9 1.1 %second.7.one = f32[32,16,128]{2,1,0:T(8,128)S(1)} custom-call(s32[1,128]{1,0:T(1,128)S(1)} %bitcast.66, bf16[96,128,128]{2,1,0:T(8,128)(2,1)S(1)} %get-tuple-element.19.high, bf16[96,128,128]{2,1,0:T(8,128)(2,1)S(1)} %get-tuple-element.20.low, bf16[64,32,256]{2,1,0:T(8,128)(2,1)S(1)} %split.7, f32[16,16,128]{2,1,0:T(8,128)S(1)} %collective-permute-done.11.got, ...), custom_call_target="tpu_custom_call" | custom-call | bytes 8388608 | tf_op jit(solution)/shard_map/second/pallas_call | solution.py:45
  41.1 2.2 %collective-permute-done.16.two = f32[32,16,128]{2,1,0:T(8,128)S(1)} collective-permute-done((f32[32,16,128]{2,1,0:T(8,128)S(1)}, f32[32,16,128]{2,1,0:T(8,128)S(1)}, u32[]{:S(2)}, u32[]{:S(2)}) %collective-permute-start.16) | collective-permute-done | bytes 262176 | tf_op jit(solution)/shard_map/sum_side/ppermute | solution.py:29
  43.3 0.6 %collective-permute-done.17.two = f32[32,16,128]{2,1,0:T(8,128)S(1)} collective-permute-done((f32[32,16,128]{2,1,0:T(8,128)S(1)}, f32[32,16,128]{2,1,0:T(8,128)S(1)}, u32[]{:S(2)}, u32[]{:S(2)}) %collective-permute-start.17) | collective-permute-done | bytes 262176 | tf_op jit(solution)/shard_map/sum_side/ppermute | solution.py:29
  43.9 1.8 %collective-permute-start.18 = (f32[8,16,128]{2,1,0:T(8,128)S(1)}, f32[8,16,128]{2,1,0:T(8,128)S(1)}, u32[]{:S(2)}, u32[]{:S(2)}) collective-permute-start(f32[8,16,128]{2,1,0:T(8,128)S(1)} %get-tuple-element.47), channel_id=1, source_target_pairs={{0,128},{1,129},{2,130},{3,131},{4,132},{5,133},{6,134},{7,135},{8... | collective-permute-start | bytes 196616 | tf_op jit(solution)/shard_map/sum_z/ppermute | solution.py:29
  45.7 2.3 %collective-permute-start.20 = (f32[8,16,128]{2,1,0:T(8,128)S(1)}, f32[8,16,128]{2,1,0:T(8,128)S(1)}, u32[]{:S(2)}, u32[]{:S(2)}) collective-permute-start(f32[8,16,128]{2,1,0:T(8,128)S(1)} %get-tuple-element.48), channel_id=1, source_target_pairs={{0,32},{1,33},{2,34},{3,35},{4,36},{5,37},{6,38},{7,39},{8,40},{9,... | collective-permute-start | bytes 196616 | tf_op jit(solution)/shard_map/sum_z/ppermute | solution.py:29
  48.0 2.8 %collective-permute-done.20 = f32[8,16,128]{2,1,0:T(8,128)S(1)} collective-permute-done((f32[8,16,128]{2,1,0:T(8,128)S(1)}, f32[8,16,128]{2,1,0:T(8,128)S(1)}, u32[]{:S(2)}, u32[]{:S(2)}) %collective-permute-start.20) | collective-permute-done | bytes 65568 | tf_op jit(solution)/shard_map/sum_z/ppermute | solution.py:29
  50.7 2.3 %collective-permute-done.19 = f32[8,16,128]{2,1,0:T(8,128)S(1)} collective-permute-done((f32[8,16,128]{2,1,0:T(8,128)S(1)}, f32[8,16,128]{2,1,0:T(8,128)S(1)}, u32[]{:S(2)}, u32[]{:S(2)}) %collective-permute-start.19) | collective-permute-done | bytes 65568 | tf_op jit(solution)/shard_map/sum_z/ppermute | solution.py:29
  53.1 0.8 %collective-permute-start.21 = (f32[4,16,128]{2,1,0:T(8,128)S(1)}, f32[4,16,128]{2,1,0:T(8,128)S(1)}, u32[]{:S(2)}, u32[]{:S(2)}) collective-permute-start(f32[4,16,128]{2,1,0:T(8,128)S(1)} %slice.49), channel_id=1, source_target_pairs={{0,16},{1,17},{2,18},{3,19},{4,20},{5,21},{6,22},{7,23},{8,24},{9,... | collective-permute-start | bytes 98312 | tf_op jit(solution)/shard_map/sum_core/ppermute | solution.py:29
  53.9 0.9 %collective-permute-done.21 = f32[4,16,128]{2,1,0:T(8,128)S(1)} collective-permute-done((f32[4,16,128]{2,1,0:T(8,128)S(1)}, f32[4,16,128]{2,1,0:T(8,128)S(1)}, u32[]{:S(2)}, u32[]{:S(2)}) %collective-permute-start.21) | collective-permute-done | bytes 32800 | tf_op jit(solution)/shard_map/sum_core/ppermute | solution.py:29
  54.7 0.6 %fusion.6 = f32[4,1,1,16,128]{4,3,2,1,0:T(8,128)} fusion(f32[4,16,128]{2,1,0:T(8,128)S(1)} %collective-permute-done.21, f32[8,16,128]{2,1,0:T(8,128)S(1)} %fusion.1), kind=kLoop, calls=%fused_computation.15 | loop fusion | flops 8192 | bytes 98304 | tf_op jit(solution)/shard_map/reshape | solution.py:345
  (53 shorter events, 2.9 us)
Async XLA Ops:
  0.0 4.7 %collective-permute-start = (f32[4,16,128]{2,1,0:T(8,128)}, f32[4,16,128]{2,1,0:T(8,128)S(1)}, u32[]{:S(2)}, u32[]{:S(2)}) collective-permute-start(f32[4,16,128]{2,1,0:T(8,128)} %bitcast.61), channel_id=1, source_target_pairs={{0,16},{1,17},{2,18},{3,19},{4,20},{5,21},{6,22},{7,23},{8,24},{9,... | collective-permute-start | bytes 98312 | tf_op jit(solution)/shard_map/gather_core/ppermute | solution.py:29
  3.2 0.8 %copy-start.1 = (f32[4,1,1,16,128]{4,3,2,1,0:T(8,128)S(1)}, f32[4,1,1,16,128]{4,3,2,1,0:T(8,128)}, u32[]{:S(2)}) copy-start(f32[4,1,1,16,128]{4,3,2,1,0:T(8,128)} %param.5) | copy-start | bytes 98308
  4.7 7.4 %collective-permute-start.3 = (f32[8,16,128]{2,1,0:T(8,128)S(1)}, f32[8,16,128]{2,1,0:T(8,128)S(1)}, u32[]{:S(2)}, u32[]{:S(2)}) collective-permute-start(f32[8,16,128]{2,1,0:T(8,128)S(1)} %pair.1.refs_0_), channel_id=1, source_target_pairs={{0,128},{1,129},{2,130},{3,131},{4,132},{5,133},{6,134},{7,135},{8... | collective-permute-start | bytes 196616 | tf_op jit(solution)/shard_map/gather_z/ppermute | solution.py:29
  7.4 4.7 %collective-permute-start.2 = (f32[8,16,128]{2,1,0:T(8,128)S(1)}, f32[8,16,128]{2,1,0:T(8,128)S(1)}, u32[]{:S(2)}, u32[]{:S(2)}) collective-permute-start(f32[8,16,128]{2,1,0:T(8,128)S(1)} %pair.1.refs_0_), channel_id=1, source_target_pairs={{0,32},{1,33},{2,34},{3,35},{4,36},{5,37},{6,38},{7,39},{8,40},{9,... | collective-permute-start | bytes 196616 | tf_op jit(solution)/shard_map/gather_z/ppermute | solution.py:29
  7.4 4.7 %collective-permute-start.1 = (f32[8,16,128]{2,1,0:T(8,128)S(1)}, f32[8,16,128]{2,1,0:T(8,128)S(1)}, u32[]{:S(2)}, u32[]{:S(2)}) collective-permute-start(f32[8,16,128]{2,1,0:T(8,128)S(1)} %pair.1.refs_0_), channel_id=1, source_target_pairs={{0,32},{1,33},{2,34},{3,35},{4,36},{5,37},{6,38},{7,39},{8,40},{9,... | collective-permute-start | bytes 196616 | tf_op jit(solution)/shard_map/gather_z/ppermute | solution.py:29
  8.3 2.8 %copy-start = (f32[1,1,96,128,128]{4,3,2,1,0:T(8,128)S(1)}, f32[1,1,96,128,128]{4,3,2,1,0:T(8,128)}, u32[]{:S(2)}) copy-start(f32[1,1,96,128,128]{4,3,2,1,0:T(8,128)} %param.6) | copy-start | bytes 18874372
  11.1 4.4 %copy-start.2 = (s32[1,1,96]{2,1,0:T(1,128)S(1)}, s32[1,1,96]{2,1,0:T(1,128)}, u32[]{:S(2)}) copy-start(s32[1,1,96]{2,1,0:T(1,128)} %param.7) | copy-start | bytes 1156
  11.1 4.4 %copy-start.3 = (s32[1,1,96]{2,1,0:T(1,128)S(1)}, s32[1,1,96]{2,1,0:T(1,128)}, u32[]{:S(2)}) copy-start(s32[1,1,96]{2,1,0:T(1,128)} %param.8) | copy-start | bytes 1156
  12.1 9.9 %collective-permute-start.6 = (f32[32,16,128]{2,1,0:T(8,128)S(1)}, f32[32,16,128]{2,1,0:T(8,128)S(1)}, u32[]{:S(2)}, u32[]{:S(2)}) collective-permute-start(f32[32,16,128]{2,1,0:T(8,128)S(1)} %column.1.after.part), channel_id=1, source_target_pairs={{0,64},{1,65},{2,66},{3,67},{4,68},{5,69},{6,70},{7,71},{8,72},{9,... | collective-permute-start | bytes 786440 | tf_op jit(solution)/shard_map/gather_side/ppermute | solution.py:29
  14.6 10.7 %collective-permute-start.5 = (f32[32,16,128]{2,1,0:T(8,128)S(1)}, f32[32,16,128]{2,1,0:T(8,128)S(1)}, u32[]{:S(2)}, u32[]{:S(2)}) collective-permute-start(f32[32,16,128]{2,1,0:T(8,128)S(1)} %column.1.after.part), channel_id=1, source_target_pairs={{0,32},{1,33},{2,34},{3,35},{4,36},{5,37},{6,38},{7,39},{8,40},{9,... | collective-permute-start | bytes 786440 | tf_op jit(solution)/shard_map/gather_side/ppermute | solution.py:29
  14.9 13.5 %collective-permute-start.4 = (f32[32,16,128]{2,1,0:T(8,128)S(1)}, f32[32,16,128]{2,1,0:T(8,128)S(1)}, u32[]{:S(2)}, u32[]{:S(2)}) collective-permute-start(f32[32,16,128]{2,1,0:T(8,128)S(1)} %column.1.after.part), channel_id=1, source_target_pairs={{0,96},{1,97},{2,98},{3,99},{4,100},{5,101},{6,102},{7,103},{8,104... | collective-permute-start | bytes 786440 | tf_op jit(solution)/shard_map/gather_side/ppermute | solution.py:29
  16.9 8.4 %collective-permute-start.7 = (f32[16,16,128]{2,1,0:T(8,128)S(1)}, f32[16,16,128]{2,1,0:T(8,128)S(1)}, u32[]{:S(2)}, u32[]{:S(2)}) collective-permute-start(f32[16,16,128]{2,1,0:T(8,128)S(1)} %get-tuple-element.23), channel_id=1, source_target_pairs={{0,16},{1,17},{2,18},{3,19},{4,20},{5,21},{6,22},{7,23},{8,24},{9,... | collective-permute-start | bytes 393224 | tf_op jit(solution)/shard_map/gather_swap/ppermute | solution.py:29
  23.0 5.4 %collective-permute-start.8 = (f32[16,16,128]{2,1,0:T(8,128)S(1)}, f32[16,16,128]{2,1,0:T(8,128)S(1)}, u32[]{:S(2)}, u32[]{:S(2)}) collective-permute-start(f32[16,16,128]{2,1,0:T(8,128)S(1)} %get-tuple-element.25), channel_id=1, source_target_pairs={{0,16},{1,17},{2,18},{3,19},{4,20},{5,21},{6,22},{7,23},{8,24},{9,... | collective-permute-start | bytes 393224 | tf_op jit(solution)/shard_map/gather_swap/ppermute | solution.py:29
  26.2 4.4 %collective-permute-start.10 = (f32[16,16,128]{2,1,0:T(8,128)S(1)}, f32[16,16,128]{2,1,0:T(8,128)S(1)}, u32[]{:S(2)}, u32[]{:S(2)}) collective-permute-start(f32[16,16,128]{2,1,0:T(8,128)S(1)} %get-tuple-element.27), channel_id=1, source_target_pairs={{0,16},{1,17},{2,18},{3,19},{4,20},{5,21},{6,22},{7,23},{8,24},{9,... | collective-permute-start | bytes 393224 | tf_op jit(solution)/shard_map/gather_swap/ppermute | solution.py:29
  29.3 1.4 %collective-permute-start.9 = (f32[16,16,128]{2,1,0:T(8,128)S(1)}, f32[16,16,128]{2,1,0:T(8,128)S(1)}, u32[]{:S(2)}, u32[]{:S(2)}) collective-permute-start(f32[16,16,128]{2,1,0:T(8,128)S(1)} %get-tuple-element.26), channel_id=1, source_target_pairs={{0,16},{1,17},{2,18},{3,19},{4,20},{5,21},{6,22},{7,23},{8,24},{9,... | collective-permute-start | bytes 393224 | tf_op jit(solution)/shard_map/gather_swap/ppermute | solution.py:29
  29.6 1.4 %collective-permute-start.14 = (f32[16,16,128]{2,1,0:T(8,128)S(1)}, f32[16,16,128]{2,1,0:T(8,128)S(1)}, u32[]{:S(2)}, u32[]{:S(2)}) collective-permute-start(f32[16,16,128]{2,1,0:T(8,128)S(1)} %get-tuple-element.43), channel_id=1, source_target_pairs={{0,16},{1,17},{2,18},{3,19},{4,20},{5,21},{6,22},{7,23},{8,24},{9,... | collective-permute-start | bytes 393224 | tf_op jit(solution)/shard_map/sum_swap/ppermute | solution.py:29
  30.1 5.4 %collective-permute-start.13 = (f32[16,16,128]{2,1,0:T(8,128)S(1)}, f32[16,16,128]{2,1,0:T(8,128)S(1)}, u32[]{:S(2)}, u32[]{:S(2)}) collective-permute-start(f32[16,16,128]{2,1,0:T(8,128)S(1)} %get-tuple-element.44), channel_id=1, source_target_pairs={{0,16},{1,17},{2,18},{3,19},{4,20},{5,21},{6,22},{7,23},{8,24},{9,... | collective-permute-start | bytes 393224 | tf_op jit(solution)/shard_map/sum_swap/ppermute | solution.py:29
  30.2 6.9 %collective-permute-start.12 = (f32[16,16,128]{2,1,0:T(8,128)S(1)}, f32[16,16,128]{2,1,0:T(8,128)S(1)}, u32[]{:S(2)}, u32[]{:S(2)}) collective-permute-start(f32[16,16,128]{2,1,0:T(8,128)S(1)} %get-tuple-element.45), channel_id=1, source_target_pairs={{0,16},{1,17},{2,18},{3,19},{4,20},{5,21},{6,22},{7,23},{8,24},{9,... | collective-permute-start | bytes 393224 | tf_op jit(solution)/shard_map/sum_swap/ppermute | solution.py:29
  32.1 8.9 %collective-permute-start.15 = (f32[32,16,128]{2,1,0:T(8,128)S(1)}, f32[32,16,128]{2,1,0:T(8,128)S(1)}, u32[]{:S(2)}, u32[]{:S(2)}) collective-permute-start(f32[32,16,128]{2,1,0:T(8,128)S(1)} %second.4.refs_0_), channel_id=1, source_target_pairs={{0,64},{1,65},{2,66},{3,67},{4,68},{5,69},{6,70},{7,71},{8,72},{9,... | collective-permute-start | bytes 786440 | tf_op jit(solution)/shard_map/sum_side/ppermute | solution.py:29
  36.7 6.5 %collective-permute-start.16 = (f32[32,16,128]{2,1,0:T(8,128)S(1)}, f32[32,16,128]{2,1,0:T(8,128)S(1)}, u32[]{:S(2)}, u32[]{:S(2)}) collective-permute-start(f32[32,16,128]{2,1,0:T(8,128)S(1)} %second.5.refs_0_), channel_id=1, source_target_pairs={{0,96},{1,97},{2,98},{3,99},{4,100},{5,101},{6,102},{7,103},{8,104... | collective-permute-start | bytes 786440 | tf_op jit(solution)/shard_map/sum_side/ppermute | solution.py:29
  38.3 5.6 %collective-permute-start.17 = (f32[32,16,128]{2,1,0:T(8,128)S(1)}, f32[32,16,128]{2,1,0:T(8,128)S(1)}, u32[]{:S(2)}, u32[]{:S(2)}) collective-permute-start(f32[32,16,128]{2,1,0:T(8,128)S(1)} %second.6.refs_0_), channel_id=1, source_target_pairs={{0,32},{1,33},{2,34},{3,35},{4,36},{5,37},{6,38},{7,39},{8,40},{9,... | collective-permute-start | bytes 786440 | tf_op jit(solution)/shard_map/sum_side/ppermute | solution.py:29
  38.4 1.6 %collective-permute-start.11 = (f32[16,16,128]{2,1,0:T(8,128)S(1)}, f32[16,16,128]{2,1,0:T(8,128)S(1)}, u32[]{:S(2)}, u32[]{:S(2)}) collective-permute-start(f32[16,16,128]{2,1,0:T(8,128)S(1)} %get-tuple-element.46), channel_id=1, source_target_pairs={{0,16},{1,17},{2,18},{3,19},{4,20},{5,21},{6,22},{7,23},{8,24},{9,... | collective-permute-start | bytes 393224 | tf_op jit(solution)/shard_map/sum_swap/ppermute | solution.py:29
  43.9 4.1 %collective-permute-start.18 = (f32[8,16,128]{2,1,0:T(8,128)S(1)}, f32[8,16,128]{2,1,0:T(8,128)S(1)}, u32[]{:S(2)}, u32[]{:S(2)}) collective-permute-start(f32[8,16,128]{2,1,0:T(8,128)S(1)} %get-tuple-element.47), channel_id=1, source_target_pairs={{0,128},{1,129},{2,130},{3,131},{4,132},{5,133},{6,134},{7,135},{8... | collective-permute-start | bytes 196616 | tf_op jit(solution)/shard_map/sum_z/ppermute | solution.py:29
  45.7 5.0 %collective-permute-start.20 = (f32[8,16,128]{2,1,0:T(8,128)S(1)}, f32[8,16,128]{2,1,0:T(8,128)S(1)}, u32[]{:S(2)}, u32[]{:S(2)}) collective-permute-start(f32[8,16,128]{2,1,0:T(8,128)S(1)} %get-tuple-element.48), channel_id=1, source_target_pairs={{0,32},{1,33},{2,34},{3,35},{4,36},{5,37},{6,38},{7,39},{8,40},{9,... | collective-permute-start | bytes 196616 | tf_op jit(solution)/shard_map/sum_z/ppermute | solution.py:29
  48.0 5.1 %collective-permute-start.19 = (f32[8,16,128]{2,1,0:T(8,128)S(1)}, f32[8,16,128]{2,1,0:T(8,128)S(1)}, u32[]{:S(2)}, u32[]{:S(2)}) collective-permute-start(f32[8,16,128]{2,1,0:T(8,128)S(1)} %get-tuple-element.49), channel_id=1, source_target_pairs={{0,32},{1,33},{2,34},{3,35},{4,36},{5,37},{6,38},{7,39},{8,40},{9,... | collective-permute-start | bytes 196616 | tf_op jit(solution)/shard_map/sum_z/ppermute | solution.py:29
  53.1 1.7 %collective-permute-start.21 = (f32[4,16,128]{2,1,0:T(8,128)S(1)}, f32[4,16,128]{2,1,0:T(8,128)S(1)}, u32[]{:S(2)}, u32[]{:S(2)}) collective-permute-start(f32[4,16,128]{2,1,0:T(8,128)S(1)} %slice.49), channel_id=1, source_target_pairs={{0,16},{1,17},{2,18},{3,19},{4,20},{5,21},{6,22},{7,23},{8,24},{9,... | collective-permute-start | bytes 98312 | tf_op jit(solution)/shard_map/sum_core/ppermute | solution.py:29
